TPU v7x, 32 devices: a whole 2x2x4 slice. The times are simulated.
32 devices in a mesh: gx: 4 (over x, core), gy: 4 (over z), gz: 2 (over y).
Axes of the slice: x: 2, y: 2, z: 4, core: 2. Of those that a mesh axis runs over, the one named last changes fastest.
Arguments:
- sketch: float32 [8, 8, 4, 64, 384], P('gx', 'gy', 'gz'), may hold values from -1200 to 1200
- test_matrix: bfloat16 [8, 8, 4, 64, 384], P('gx', 'gy', 'gz'), may hold values from -0.1796875 to 0.1796875
- offsets: bfloat16 [8, 8, 4, 3, 128], P('gx', 'gy', 'gz'), may hold values from 0 to 1
- near: int32 [8, 8, 4, 27], P('gx', 'gy', 'gz'), may hold values 0 or 1
Outputs:
- leaf_basis: float32 [8, 8, 4, 64, 384], P('gx', 'gy', 'gz')
- level1_transfer: float32 [4, 4, 2, 64, 512], P('gx', 'gy', 'gz')
- level2_basis: float32 [8, 8, 4, 64, 384], P('gx', 'gy', 'gz')
All inputs are finite; a program needn't handle non-finite values. No bound on the sum of `near` on one device may be relied on, other than what follows from the above.
Results may differ from a plain program's by a relative error of at most 0.0029.
Values may be sent and summed in bfloat16 or wider, within the bound.
No kernel may reach another device: no remote copies, remote signals or barrier semaphores. Data moves between devices by JAX's collectives and lax.ppermute only.
A program may use at most 64 MiB of HBM per device.

v0:
```python
import functools
import math

import jax
import jax.numpy as jnp
from jax import lax
from jax.experimental import pallas as pl
from jax.experimental.pallas import tpu as pltpu
from jax.sharding import PartitionSpec as P

EPSILON = 0.1
GROUP = 8
SIDE = 2
HIGHEST = lax.Precision.HIGHEST


def from_partner(x, axis, distance):
    return lax.ppermute(x, axis, [(i, i ^ 1 << distance) for i in range(lax.axis_size(axis))])


SMALL = 0.2


def matmul(a, b, precision=HIGHEST):
    return lax.dot_general(
        a, b, (((1,), (0,)), ((), ())), precision=precision, preferred_element_type=jnp.float32
    )


def matmul_t(a, b, precision=HIGHEST):
    return lax.dot_general(
        a, b, (((1,), (1,)), ((), ())), precision=precision, preferred_element_type=jnp.float32
    )


def halves(x):
    high = x.astype(jnp.bfloat16)
    return high, (x - high.astype(jnp.float32)).astype(jnp.bfloat16)


def positions(shape):
    return (
        lax.broadcasted_iota(jnp.int32, shape, 0),
        lax.broadcasted_iota(jnp.int32, shape, 1),
    )


def unit(rank):
    row, column = positions((rank, rank))
    return jnp.where(row == column, 1.0, 0.0).astype(jnp.float32)


def upper(x):
    row, column = positions(x.shape)
    return jnp.where(row <= column, x, 0.0)


def half_lower(x):
    row, column = positions(x.shape)
    return jnp.where(row > column, x, jnp.where(row == column, 0.5 * x, 0.0))


def excess_of(x):
    rank = x.shape[0]
    stacked = jnp.concatenate(halves(x), axis=0)
    products = matmul_t(stacked, stacked, None)
    crossed = products[:rank, rank:] + products[rank:, :rank]
    return products[:rank, :rank] + crossed


def near_unit_factor(excess):
    x = half_lower(excess)
    for _ in range(2):
        x = half_lower(excess - matmul_t(x, x, None))
    square = matmul(x, x, None)
    return x, x - square + matmul(square, x, None)


def batch_steps(work, rank, batch, width):
    shape = (batch, 2 * rank)

    def lane(values, index):
        return jnp.broadcast_to(values[:, rank + index : rank + index + 1], shape)

    for start in range(0, rank, width):
        rows = [work[(start + i) * batch : (start + i + 1) * batch, :] for i in range(width)]
        scalars = [
            [lane(rows[i], start + j) if j >= i else None for j in range(width)]
            for i in range(width)
        ]
        for j in range(width):
            root = lax.rsqrt(scalars[j][j])
            rows[j] = rows[j] * root
            factor = [None if i <= j else scalars[j][i] * root for i in range(width)]
            for i in range(j + 1, width):
                rows[i] = rows[i] - factor[i] * rows[j]
                for k in range(i, width):
                    scalars[i][k] = scalars[i][k] - factor[i] * factor[k]
            work[(start + j) * batch : (start + j + 1) * batch, :] = rows[j]
        for lower in range(start + width, rank):
            total = work[lower * batch : (lower + 1) * batch, :]
            for j in range(width):
                total = total - lane(rows[j], lower) * rows[j]
            work[lower * batch : (lower + 1) * batch, :] = total
        yield


def single_steps(work, rank):
    shape = (8, 2 * rank)
    row, _ = positions(shape)
    for start in range(0, rank, 8):
        z = work[start : start + 8, :]
        columns = [
            jnp.broadcast_to(z[:, rank + start + j : rank + start + j + 1], shape)
            for j in range(8)
        ]
        done = z
        for j in range(8):
            root = lax.rsqrt(columns[j][j : j + 1, :])
            scaled = z[j : j + 1, :] * root
            done = jnp.where(row == j, scaled, done)
            if j < 7:
                factor = columns[j] * root
                z = z - factor * scaled
                for i in range(j + 1, 8):
                    columns[i] = columns[i] - factor * (columns[i][j : j + 1, :] * root)
        work[start : start + 8, :] = done
        turned = done.T
        for lower in range(start + 8, rank, 8):
            total = work[lower : lower + 8, :]
            factors = turned[rank + lower : rank + lower + 8, :]
            for j in range(8):
                total = total - jnp.broadcast_to(factors[:, j : j + 1], shape) * done[j : j + 1, :]
            work[lower : lower + 8, :] = total
        yield


def run_together(*steps):
    for _ in zip(*steps):
        pass


def shifted(x, axis, step):
    size = lax.axis_size(axis)
    return lax.ppermute(x, axis, [(i, i + step) for i in range(size) if 0 <= i + step < size])


def leaf_index(x, y, z):
    return (x * SIDE + y) * SIDE + z


def planes_of(gz_size):
    return {0: 0, 1: 1, -1: 2, 2: 2 if gz_size == 2 else 3}


def pair_tables(gz_size):
    planes = planes_of(gz_size)
    depth = max(planes.values()) + 1
    stages = ([], [], [])
    for a in range(SIDE**3):
        place = (a // 4, a // 2 % 2, a % 2)
        for k in range(27):
            x, y, z = (p + d for p, d in zip(place, (k // 9 - 1, k // 3 % 3 - 1, k % 3 - 1)))
            sides = tuple((axis, t) for axis, t in enumerate((x, y, z)) if t in (-1, 2))
            if x in (-1, 2):
                first = 0 if x == -1 else 4 * depth
                stages[2].append((a, k, first + (y + 1) * depth + planes[z], sides))
            elif y in (-1, 2):
                first = 4 * (depth - 2) + (0 if y == -1 else 2 * depth)
                stages[1].append((a, k, first + x * depth + planes[z], sides))
            elif z in (-1, 2):
                first = 4 * (planes[z] - 2)
                stages[1].append((a, k, first + x * 2 + y, sides))
            else:
                stages[0].append((a, k, leaf_index(x, y, z), sides))
    return stages


def side_flags():
    flags = {}
    for axis, name in enumerate(("gx", "gy", "gz")):
        place = lax.axis_index(name)
        flags[axis, -1] = (place > 0).astype(jnp.int32)
        flags[axis, 2] = (place < lax.axis_size(name) - 1).astype(jnp.int32)
    return flags


def list_pairs(pairs, near, listed, blank):
    flags = side_flags()
    joint = {(): None}
    count = jnp.int32(0)
    for a, k, source, sides in pairs:
        if sides not in joint:
            product = flags[sides[0]]
            for side in sides[1:]:
                product = product * flags[side]
            joint[sides] = product
        listed[count] = jnp.int32((source * 8 + a) * 27 + k)
        taken = near[a * 27 + k]
        if sides:
            taken = taken * joint[sides]
        count = count + taken
    for i in range(GROUP):
        listed[count + i] = jnp.int32(blank * 8 * 27 + 13)
    return lax.div(count + (GROUP - 1), jnp.int32(GROUP))


def spread_offsets(blocks, count, turned, spread):
    rank3 = blocks.shape[1] - 16
    turned[...] = jnp.zeros_like(turned)
    for s in range(count):
        turned[4 * s : 4 * s + 4, :] = blocks[s, rank3:, :].astype(jnp.float32)[:4]
    columns = turned[...].T.astype(jnp.bfloat16)
    row, lane = positions((128, 384))
    for s in range(count):
        chosen = jnp.where(row == 4 * s + lane // 128, 1.0, 0.0).astype(jnp.bfloat16)
        values = matmul(columns, chosen, None)
        for p in range(3):
            spread[s, p] = values[:, 128 * p : 128 * (p + 1)]


def tile_rows(own, spread, rows):
    r = [own[p] - spread[p, rows, :] for p in range(3)]
    squares = [v * v for v in r]
    softened = squares[0] + squares[1] + squares[2] + EPSILON * EPSILON
    lifted = softened + EPSILON * EPSILON
    root = lax.rsqrt(softened)
    h = root * root * root
    ry, rz = r[1] * h, r[2] * h
    tiles = {(p, p): (squares[p] + lifted) * h for p in range(3)}
    tiles[0, 1], tiles[0, 2], tiles[1, 2] = r[0] * ry, r[0] * rz, r[1] * rz
    return {pq: tile.astype(jnp.bfloat16) for pq, tile in tiles.items()}


def add_pairs(groups, listed, blocks, own, spread, total):
    chunk = 16

    @pl.loop(0, groups)
    def _(group):
        for u in range(GROUP):
            code = listed[group * GROUP + u]
            pair = lax.div(code, jnp.int32(27))
            k = code - pair * 27
            source = lax.shift_right_logical(pair, jnp.int32(3))
            a = lax.bitwise_and(pair, jnp.int32(7))
            dx = lax.div(k, jnp.int32(9))
            dy = lax.div(k, jnp.int32(3)) - dx * 3
            dz = k - dx * 9 - dy * 3
            own_rows = own[a]
            placed = [
                jnp.broadcast_to(
                    own_rows[p : p + 1] + (1 - step).astype(jnp.float32), (chunk, 128)
                )
                for p, step in enumerate((dx, dy, dz))
            ]
            parts = [
                tile_rows(placed, spread.at[source], pl.ds(j, chunk))
                for j in range(0, 128, chunk)
            ]
            tiles = {
                pq: jnp.concatenate([part[pq] for part in parts], axis=0) for pq in parts[0]
            }
            matrix = jnp.concatenate(
                [
                    jnp.concatenate([tiles[min(p, q), max(p, q)] for p in range(3)], axis=1)
                    for q in range(3)
                ],
                axis=0,
            )
            rank = total.shape[1]
            sampled = jnp.concatenate(
                [blocks[source, q * rank : (q + 1) * rank, :] for q in range(3)], axis=1
            )
            total[a] += matmul(sampled, matrix, None)


def fetch(parts, blocks, semaphore):
    copies = []
    first = 0
    for i, part in enumerate(parts):
        copies.append(
            pltpu.make_async_copy(
                part, blocks.at[pl.ds(first, part.shape[0])], semaphore.at[i]
            )
        )
        copies[-1].start()
        first += part.shape[0]
    return copies, first


def near_stage(pairs, near, own, parts, total, listed, blocks, turned, spread, semaphore):
    copies, count = fetch(parts, blocks, semaphore)
    groups = list_pairs(pairs, near, listed, count)
    blocks[count] = jnp.zeros_like(blocks[count])
    for copy in copies:
        copy.wait()
    spread_offsets(blocks, count, turned, spread)
    spread[count] = jnp.zeros_like(spread[count])
    add_pairs(groups, listed, blocks, own, spread, total)


def first_kernel(pairs, near, own, own_blocks, total, *scratch):
    total[...] = jnp.zeros_like(total)
    near_stage(pairs, near, own, [own_blocks], total, *scratch)


def second_kernel(pairs, near, own, before, *rest):
    *parts, total, listed, blocks, turned, spread, semaphore = rest
    total[...] = before[...]
    near_stage(pairs, near, own, parts, total, listed, blocks, turned, spread, semaphore)


def third_kernel(pairs, near, own, before, sketch, low, high, *rest):
    outs, scratch = rest[:4], rest[4:]
    total, near_scratch, leaf_scratch = scratch[0], scratch[1:6], scratch[6:]
    total[...] = before[...]
    near_stage(pairs, near, own, [low, high], total, *near_scratch)
    total[...] = sketch[...] - total[...]
    leaf_kernel(total, *outs, *leaf_scratch)


def pack_kernel(samples, offsets, packed, own, *faces):
    count, rank, leaf_rows = samples.shape
    filler = jnp.zeros((13, 128), jnp.float32)
    for a in range(count):
        for q in range(3):
            packed[a, q * rank : (q + 1) * rank, :] = samples[a, :, q * 128 : (q + 1) * 128]
        rows = jnp.concatenate([offsets[a].astype(jnp.float32), filler], axis=0)
        packed[a, 3 * rank :, :] = rows.astype(jnp.bfloat16)
        own[a] = rows[:8]
    if len(faces) == 1:
        planes = [1 - lax.axis_index("gz")]
    else:
        planes = [1, 0]
    for face, plane in zip(faces, planes):
        for column in range(SIDE * SIDE):
            face[column] = packed[column * SIDE + plane]


VMEM_LIMIT = 48 * 1024 * 1024


def near_scratch(pairs, count, block):
    return [
        pltpu.SMEM((len(pairs) + GROUP + 1,), jnp.int32),
        pltpu.VMEM((count + 1,) + block, jnp.bfloat16),
        pltpu.VMEM((128, 128), jnp.float32),
        pltpu.VMEM((count + 1, 3, 128, 128), jnp.float32),
        pltpu.SemaphoreType.DMA((4,)),
    ]


def near_cost(pairs, rank):
    return pl.CostEstimate(
        flops=len(pairs) * 2 * rank * 384 * 384 * 8, bytes_accessed=4 * 1024 * 1024, transcendentals=0
    )


IN_SMEM = pl.BlockSpec(memory_space=pltpu.SMEM)
IN_VMEM = pl.BlockSpec(memory_space=pltpu.VMEM)
ANYWHERE = pl.BlockSpec(memory_space=pl.ANY)


def leaf_kernel(far, leaf_out, level_out, scaled_out, factor_out, work, single, es, xs, zs):
    count, rank, leaf_rows = far.shape
    eye = unit(rank)
    zeros = jnp.zeros((rank, leaf_rows), jnp.float32)
    left_unit = jnp.concatenate([eye, jnp.zeros_like(eye)], axis=1)
    total = left_unit
    for a in range(count):
        rows = far[a]
        gram = matmul_t(rows, jnp.concatenate([zeros, rows], axis=0))
        work[pl.ds(a, rank, stride=count), :] = left_unit + gram
        total = total + gram
    single[...] = total
    run_together(batch_steps(work, rank, count, 8), single_steps(single, rank))
    box_inverse = single[:, :rank]
    box_upper = upper(single[:, rank:])
    box_excess = -eye
    largest = jnp.zeros((1, 1), jnp.float32)
    for a in range(count):
        inverse = work[pl.ds(a, rank, stride=count), :][:, :rank]
        both = matmul(jnp.concatenate([inverse, box_inverse], axis=0), far[a])
        leaf_out[a] = both[:rank]
        scaled_out[a] = both[rank:]
        excess = excess_of(both[:rank]) - eye
        box_excess = box_excess + excess_of(both[rank:])
        xs[a], zs[a] = near_unit_factor(excess)
        es[a] = excess
        largest = jnp.maximum(largest, jnp.sum(excess * excess, keepdims=True))
    xs[count], zs[count] = near_unit_factor(box_excess)
    largest = jnp.maximum(largest, jnp.sum(box_excess * box_excess, keepdims=True))
    es[count] = box_excess
    uppers = [upper(work[pl.ds(a, rank, stride=count), :][:, rank:]) for a in range(count)]

    @pl.when(jnp.logical_not(largest[0, 0] <= SMALL * SMALL))
    def _():
        for a in range(count):
            work[pl.ds(a, rank, stride=count), :] = jnp.concatenate([eye, eye + es[a]], axis=1)
        single[...] = jnp.concatenate([eye, eye + es[count]], axis=1)
        run_together(batch_steps(work, rank, count, 8), single_steps(single, rank))
        for a in range(count + 1):
            rows = single[...] if a == count else work[pl.ds(a, rank, stride=count), :]
            xs[a] = upper(rows[:, rank:]).T - eye
            zs[a] = eye - rows[:, :rank]

    box_x, box_z = xs[count], zs[count]
    lower_box = box_upper.T
    factor_out[...] = lower_box + matmul(lower_box, box_x)
    for a in range(count):
        basis = leaf_out[a]
        leaf_out[a] = (basis - matmul(zs[a], basis)) * math.sqrt(leaf_rows)
        scaled = scaled_out[a]
        scaled_out[a] = scaled - matmul(box_z, scaled)
        block = matmul_t(box_inverse, uppers[a])
        block = block + matmul(block, xs[a])
        block = block - matmul(box_z, block)
        level_out[:, a * rank : (a + 1) * rank] = block * math.sqrt(count * rank)


def group_kernel(factors, scaled, nested_out, single, z_out):
    count, rank, _ = factors.shape
    eye = unit(rank)
    gram = jnp.zeros((rank, rank), jnp.float32)
    for b in range(count):
        gram = gram + matmul_t(factors[b], factors[b])
    single[...] = jnp.concatenate([eye, gram], axis=1)
    run_together(single_steps(single, rank))
    inverse = single[:, :rank]
    excess = -eye
    for b in range(count):
        block = matmul(inverse, factors[b])
        if b == 0:
            own = block
        excess = excess + excess_of(block)
    _, z_out[...] = near_unit_factor(excess)
    largest = jnp.sum(excess * excess, keepdims=True)

    @pl.when(jnp.logical_not(largest[0, 0] <= SMALL * SMALL))
    def _():
        single[...] = jnp.concatenate([eye, eye + excess], axis=1)
        run_together(single_steps(single, rank))
        z_out[...] = eye - single[:, :rank]

    z = z_out[...]
    mixing = (own - matmul(z, own)) * (8.0 * math.sqrt(scaled.shape[2]))
    for a in range(scaled.shape[0]):
        nested_out[a] = matmul(mixing, scaled[a])


def leaf_scratch(count, rank):
    square = pltpu.VMEM((count + 1, rank, rank), jnp.float32)
    return [
        pltpu.VMEM((rank * count, 2 * rank), jnp.float32),
        pltpu.VMEM((rank, 2 * rank), jnp.float32),
        square,
        square,
        square,
    ]


def join(parts, axis):
    return jnp.concatenate(parts, axis=axis)


def group_level(factors, scaled):
    rank = factors.shape[1]
    return pl.pallas_call(
        group_kernel,
        out_shape=jax.ShapeDtypeStruct(scaled.shape, jnp.float32),
        scratch_shapes=[
            pltpu.VMEM((rank, 2 * rank), jnp.float32),
            pltpu.VMEM((rank, rank), jnp.float32),
        ],
        compiler_params=pltpu.CompilerParams(vmem_limit_bytes=32 * 1024 * 1024),
        name="group_level",
    )(factors, scaled)


def body(sketch, test_matrix, offsets, near):
    rank, leaf_rows = sketch.shape[3:]
    count = SIDE**3
    gz_size = lax.axis_size("gz")
    like = jax.ShapeDtypeStruct
    block = (3 * rank + 16, 128)
    params = pltpu.CompilerParams(vmem_limit_bytes=VMEM_LIMIT)
    flat_near = near.reshape(count * 27)
    flat_sketch = sketch.reshape(count, rank, leaf_rows)
    stages = pair_tables(gz_size)
    faces = 1 if gz_size == 2 else 2
    packed, own, *sent = pl.pallas_call(
        pack_kernel,
        out_shape=(
            like((count,) + block, jnp.bfloat16),
            like((count, 8, 128), jnp.float32),
        )
        + (like((SIDE * SIDE,) + block, jnp.bfloat16),) * faces,
        compiler_params=params,
        name="pack",
    )(test_matrix.reshape(count, rank, leaf_rows), offsets.reshape(count, 3, 128))
    if faces == 1:
        z_halos = [from_partner(sent[0], "gz", 0)]
    else:
        z_halos = [shifted(sent[0], "gz", 1), shifted(sent[1], "gz", -1)]
    inner = packed.reshape((SIDE, SIDE, SIDE) + block)
    columns = [h.reshape((SIDE, SIDE, 1) + block) for h in z_halos]
    extended = join([inner] + columns, 2)
    depth = extended.shape[2]
    y_low = shifted(extended[:, 1], "gy", 1)
    y_high = shifted(extended[:, 0], "gy", -1)
    wide = join([y_low[:, None], extended, y_high[:, None]], 1)
    x_low = shifted(wide[1], "gx", 1)
    x_high = shifted(wide[0], "gx", -1)

    total = pl.pallas_call(
        functools.partial(first_kernel, stages[0]),
        out_shape=like((count, rank, leaf_rows), jnp.float32),
        in_specs=[IN_SMEM, IN_VMEM, ANYWHERE],
        scratch_shapes=near_scratch(stages[0], count, block),
        cost_estimate=near_cost(stages[0], rank),
        compiler_params=params,
        name="near_inner",
    )(flat_near, own, packed)
    flat = lambda x: x.reshape((-1,) + block)
    parts = [flat(h) for h in z_halos] + [flat(y_low), flat(y_high)]
    total = pl.pallas_call(
        functools.partial(second_kernel, stages[1]),
        out_shape=like((count, rank, leaf_rows), jnp.float32),
        in_specs=[IN_SMEM, IN_VMEM, IN_VMEM] + [ANYWHERE] * len(parts),
        scratch_shapes=near_scratch(stages[1], 4 * faces + 4 * depth, block),
        cost_estimate=near_cost(stages[1], rank),
        compiler_params=params,
        name="near_columns",
    )(flat_near, own, total, *parts)
    leaf_t, level_t, scaled, factor = pl.pallas_call(
        functools.partial(third_kernel, stages[2]),
        out_shape=(
            like((count, rank, leaf_rows), jnp.float32),
            like((rank, count * rank), jnp.float32),
            like((count, rank, leaf_rows), jnp.float32),
            like((rank, rank), jnp.float32),
        ),
        in_specs=[IN_SMEM, IN_VMEM, IN_VMEM, IN_VMEM] + [ANYWHERE] * 2,
        scratch_shapes=[pltpu.VMEM((count, rank, leaf_rows), jnp.float32)]
        + near_scratch(stages[2], 8 * depth, block)
        + leaf_scratch(count, rank),
        compiler_params=params,
        name="near_sides_and_leaf_level",
    )(flat_near, own, total, flat_sketch, flat(x_low), flat(x_high))
    grouped = factor[None]
    for axis in ("gz", "gy", "gx"):
        grouped = jnp.concatenate([grouped, from_partner(grouped, axis, 0)], axis=0)
    nested = group_level(grouped, scaled)
    return (leaf_t.reshape(sketch.shape), level_t[None, None, None], nested.reshape(sketch.shape))


def solution(mesh):
    placed = (
        P("gx", "gy", "gz", None, None),
        P("gx", "gy", "gz", None, None),
        P("gx", "gy", "gz", None, None),
        P("gx", "gy", "gz", None),
    )
    return jax.shard_map(
        body,
        mesh=mesh,
        in_specs=placed,
        out_specs=(
            P("gx", "gy", "gz", None, None),
            P("gx", "gy", "gz", None, None),
            P("gx", "gy", "gz", None, None),
        ),
        check_vma=False,
    )
```

profile of v0, /device:TPU:0, one launch (start us, length us, event | category | flops | bytes accessed | tf_op | source)
XLA Modules:
  0.0 81.5 jit_solution(2659991657718509292)
XLA Ops:
  0.6 0.7 copy.7
  1.3 0.0 copy-start.1
  1.3 1.0 %copy-done.1 = bf16[2,2,2,64,384]{4,3,2,1,0:T(8,128)(2,1)S(1)} copy-done((bf16[2,2,2,64,384]{4,3,2,1,0:T(8,128)(2,1)S(1)}, bf16[2,2,2,64,384]{4,3,2,1,0:T(8,128)(2,1)}, u32[]{:S(2)}) %copy-start.1) | copy-done | bytes 393240
  2.3 0.1 pack.1
  2.4 3.0 %collective-permute-start = (bf16[4,208,128]{2,1,0:T(8,128)(2,1)S(1)}, bf16[4,208,128]{2,1,0:T(8,128)(2,1)S(1)}, u32[]{:S(2)}, u32[]{:S(2)}) collective-permute-start(bf16[4,208,128]{2,1,0:T(8,128)(2,1)S(1)} %get-tuple-element.12), channel_id=1, source_target_pairs={{0,1},{1,0},{2,3},{3,2},{4,5},{5,4},{6,7},{7,6},{8,9},{9,8},{10,11... | collective-permute-start | bytes 638984 | tf_op jit(solution)/shard_map/ppermute | solution.py:18
  5.5 0.8 reshape.42.near
  6.3 4.4 %collective-permute-done.rest_0_ = bf16[4,208,128]{2,1,0:T(8,128)(2,1)S(1)} collective-permute-done((bf16[4,208,128]{2,1,0:T(8,128)(2,1)S(1)}, bf16[4,208,128]{2,1,0:T(8,128)(2,1)S(1)}, u32[]{:S(2)}, u32[]{:S(2)}) %collective-permute-start) | collective-permute-done | bytes 213024 | tf_op jit(solution)/shard_map/ppermute | solution.py:18
  10.8 3.7 %collective-permute-start.1 = (bf16[2,3,208,128]{3,2,1,0:T(8,128)(2,1)S(1)}, bf16[2,3,208,128]{3,2,1,0:T(8,128)(2,1)S(1)}, u32[]{:S(2)}, u32[]{:S(2)}) collective-permute-start(bf16[2,3,208,128]{3,2,1,0:T(8,128)(2,1)S(1)} %get-tuple-element.20), channel_id=1, source_target_pairs={{0,2},{2,4},{4,6},{1,3},{3,5},{5,7},{8,10},{10,12},{12,14},{9,11},... | collective-permute-start | bytes 958472 | tf_op jit(solution)/shard_map/ppermute | solution.py:145
  14.5 1.3 %collective-permute-start.2 = (bf16[2,3,208,128]{3,2,1,0:T(8,128)(2,1)S(1)}, bf16[2,3,208,128]{3,2,1,0:T(8,128)(2,1)S(1)}, u32[]{:S(2)}, u32[]{:S(2)}) collective-permute-start(bf16[2,3,208,128]{3,2,1,0:T(8,128)(2,1)S(1)} %get-tuple-element.19), channel_id=1, source_target_pairs={{2,0},{4,2},{6,4},{3,1},{5,3},{7,5},{10,8},{12,10},{14,12},{11,9},... | collective-permute-start | bytes 958472 | tf_op jit(solution)/shard_map/ppermute | solution.py:145
  15.8 7.1 %near_inner.1.before = f32[8,64,384]{2,1,0:T(8,128)S(1)} custom-call(s32[216]{0:T(256)S(1)} %reshape.42.near, f32[8,8,128]{2,1,0:T(8,128)S(1)} %get-tuple-element.10.own, bf16[8,208,128]{2,1,0:T(8,128)(2,1)S(1)} %get-tuple-element.11.own_blocks), custom_call_target="tpu_custom_call" | custom-call | flops 9663676416 | bytes 4194304 | tf_op jit(solution)/shard_map/near_inner/pallas_call | solution.py:515
  22.9 0.0 collective-permute-done.1
  23.0 1.6 %collective-permute-done.2 = bf16[2,3,208,128]{3,2,1,0:T(8,128)(2,1)S(1)} collective-permute-done((bf16[2,3,208,128]{3,2,1,0:T(8,128)(2,1)S(1)}, bf16[2,3,208,128]{3,2,1,0:T(8,128)(2,1)S(1)}, u32[]{:S(2)}, u32[]{:S(2)}) %collective-permute-start.2) | collective-permute-done | bytes 319520 | tf_op jit(solution)/shard_map/ppermute | solution.py:145
  24.5 0.1 pad_maximum_fusion
  24.6 0.1 slice_bitcast_fusion
  24.7 1.3 %collective-permute-start.3 = (bf16[4,3,208,128]{3,2,1,0:T(8,128)(2,1)S(1)}, bf16[4,3,208,128]{3,2,1,0:T(8,128)(2,1)S(1)}, u32[]{:S(2)}, u32[]{:S(2)}) collective-permute-start(bf16[4,3,208,128]{3,2,1,0:T(8,128)(2,1)S(1)} %get-tuple-element.18), channel_id=1, source_target_pairs={{0,8},{8,16},{16,24},{1,9},{9,17},{17,25},{2,10},{10,18},{18,26},{... | collective-permute-start | bytes 1916936 | tf_op jit(solution)/shard_map/ppermute | solution.py:145
  26.1 1.3 %collective-permute-start.4 = (bf16[4,3,208,128]{3,2,1,0:T(8,128)(2,1)S(1)}, bf16[4,3,208,128]{3,2,1,0:T(8,128)(2,1)S(1)}, u32[]{:S(2)}, u32[]{:S(2)}) collective-permute-start(bf16[4,3,208,128]{3,2,1,0:T(8,128)(2,1)S(1)} %get-tuple-element.17), channel_id=1, source_target_pairs={{8,0},{16,8},{24,16},{9,1},{17,9},{25,17},{10,2},{18,10},{26,18},{... | collective-permute-start | bytes 1916936 | tf_op jit(solution)/shard_map/ppermute | solution.py:145
  27.4 0.0 copy-start
  27.4 5.2 %near_columns.1.before = f32[8,64,384]{2,1,0:T(8,128)S(1)} custom-call(s32[216]{0:T(256)S(1)} %reshape.42.near, f32[8,8,128]{2,1,0:T(8,128)S(1)} %get-tuple-element.10.own, f32[8,64,384]{2,1,0:T(8,128)S(1)} %near_inner.1.before, bf16[4,208,128]{2,1,0:T(8,128)(2,1)S(1)} %collective-permute-done.rest_0_, bf16[6,208,128]{2,1,0:T(8,128)(2,1)S(1)} %bitcast.31, ...), custom_call_target="tpu_custom_call" | custom-call | flops 12079595520 | bytes 4194304 | tf_op jit(solution)/shard_map/near_columns/pallas_call | solution.py:526
  32.6 0.0 collective-permute-done.3
  32.6 0.0 collective-permute-done.4
  32.6 0.0 copy-done
  32.6 23.7 %near_sides_and_leaf_level.1 = (f32[8,64,384]{2,1,0:T(8,128)}, f32[64,512]{1,0:T(8,128)}, f32[8,64,384]{2,1,0:T(8,128)S(1)}, f32[64,64]{1,0:T(8,128)S(1)}) custom-call(s32[216]{0:T(256)S(1)} %reshape.42.near, f32[8,8,128]{2,1,0:T(8,128)S(1)} %get-tuple-element.10.own, f32[8,64,384]{2,1,0:T(8,128)S(1)} %near_columns.1.before, f32[8,64,384]{2,1,0:T(8,128)S(1)} %bitcast.25, ...), custom_call_target="tpu_custom_call" | custom-call | tf_op jit(solution)/shard_map/near_sides_and_leaf_level/pallas_call | solution.py:535
  56.3 1.6 %collective-permute-start.5 = (f32[1,64,64]{2,1,0:T(8,128)S(1)}, f32[1,64,64]{2,1,0:T(8,128)S(1)}, u32[]{:S(2)}, u32[]{:S(2)}) collective-permute-start(f32[1,64,64]{2,1,0:T(8,128)S(1)} %bitcast.34), channel_id=1, source_target_pairs={{0,1},{1,0},{2,3},{3,2},{4,5},{5,4},{6,7},{7,6},{8,9},{9,8},{10,11... | collective-permute-start | bytes 49160 | tf_op jit(solution)/shard_map/ppermute | solution.py:18
  57.9 2.4 %collective-permute-done.5 = f32[1,64,64]{2,1,0:T(8,128)S(1)} collective-permute-done((f32[1,64,64]{2,1,0:T(8,128)S(1)}, f32[1,64,64]{2,1,0:T(8,128)S(1)}, u32[]{:S(2)}, u32[]{:S(2)}) %collective-permute-start.5) | collective-permute-done | bytes 16416 | tf_op jit(solution)/shard_map/ppermute | solution.py:18
  60.3 3.3 %collective-permute-start.6 = (f32[2,64,64]{2,1,0:T(8,128)S(1)}, f32[2,64,64]{2,1,0:T(8,128)S(1)}, u32[]{:S(2)}, u32[]{:S(2)}) collective-permute-start(f32[2,64,64]{2,1,0:T(8,128)S(1)} %pad_maximum_fusion.3), channel_id=1, source_target_pairs={{0,2},{2,0},{4,6},{6,4},{1,3},{3,1},{5,7},{7,5},{8,10},{10,8},{12,... | collective-permute-start | bytes 98312 | tf_op jit(solution)/shard_map/ppermute | solution.py:18
  63.5 2.2 %collective-permute-done.6 = f32[2,64,64]{2,1,0:T(8,128)S(1)} collective-permute-done((f32[2,64,64]{2,1,0:T(8,128)S(1)}, f32[2,64,64]{2,1,0:T(8,128)S(1)}, u32[]{:S(2)}, u32[]{:S(2)}) %collective-permute-start.6) | collective-permute-done | bytes 32800 | tf_op jit(solution)/shard_map/ppermute | solution.py:18
  65.8 7.0 %collective-permute-start.7 = (f32[4,64,64]{2,1,0:T(8,128)S(1)}, f32[4,64,64]{2,1,0:T(8,128)S(1)}, u32[]{:S(2)}, u32[]{:S(2)}) collective-permute-start(f32[4,64,64]{2,1,0:T(8,128)S(1)} %pad_maximum_fusion.2), channel_id=1, source_target_pairs={{0,8},{8,0},{16,24},{24,16},{1,9},{9,1},{17,25},{25,17},{2,10},{10... | collective-permute-start | bytes 196616 | tf_op jit(solution)/shard_map/ppermute | solution.py:18
  72.8 1.0 %collective-permute-done.7 = f32[4,64,64]{2,1,0:T(8,128)S(1)} collective-permute-done((f32[4,64,64]{2,1,0:T(8,128)S(1)}, f32[4,64,64]{2,1,0:T(8,128)S(1)}, u32[]{:S(2)}, u32[]{:S(2)}) %collective-permute-start.7) | collective-permute-done | bytes 65568 | tf_op jit(solution)/shard_map/ppermute | solution.py:18
  73.8 7.7 %group_level.1 = f32[8,64,384]{2,1,0:T(8,128)} custom-call(f32[8,64,64]{2,1,0:T(8,128)S(1)} %pad_maximum_fusion.1.factors, f32[8,64,384]{2,1,0:T(8,128)S(1)} %get-tuple-element.16.scaled), custom_call_target="tpu_custom_call" | custom-call | tf_op jit(solution)/shard_map/group_level/pallas_call | solution.py:468
  (6 shorter events, 0.1 us)
Async XLA Ops:
  1.3 1.0 %copy-start.1 = (bf16[2,2,2,64,384]{4,3,2,1,0:T(8,128)(2,1)S(1)}, bf16[2,2,2,64,384]{4,3,2,1,0:T(8,128)(2,1)}, u32[]{:S(2)}) copy-start(bf16[2,2,2,64,384]{4,3,2,1,0:T(8,128)(2,1)} %param.5) | copy-start | bytes 1179652
  2.4 8.3 %collective-permute-start = (bf16[4,208,128]{2,1,0:T(8,128)(2,1)S(1)}, bf16[4,208,128]{2,1,0:T(8,128)(2,1)S(1)}, u32[]{:S(2)}, u32[]{:S(2)}) collective-permute-start(bf16[4,208,128]{2,1,0:T(8,128)(2,1)S(1)} %get-tuple-element.12), channel_id=1, source_target_pairs={{0,1},{1,0},{2,3},{3,2},{4,5},{5,4},{6,7},{7,6},{8,9},{9,8},{10,11... | collective-permute-start | bytes 638984 | tf_op jit(solution)/shard_map/ppermute | solution.py:18
  10.8 12.2 %collective-permute-start.1 = (bf16[2,3,208,128]{3,2,1,0:T(8,128)(2,1)S(1)}, bf16[2,3,208,128]{3,2,1,0:T(8,128)(2,1)S(1)}, u32[]{:S(2)}, u32[]{:S(2)}) collective-permute-start(bf16[2,3,208,128]{3,2,1,0:T(8,128)(2,1)S(1)} %get-tuple-element.20), channel_id=1, source_target_pairs={{0,2},{2,4},{4,6},{1,3},{3,5},{5,7},{8,10},{10,12},{12,14},{9,11},... | collective-permute-start | bytes 958472 | tf_op jit(solution)/shard_map/ppermute | solution.py:145
  14.5 10.0 %collective-permute-start.2 = (bf16[2,3,208,128]{3,2,1,0:T(8,128)(2,1)S(1)}, bf16[2,3,208,128]{3,2,1,0:T(8,128)(2,1)S(1)}, u32[]{:S(2)}, u32[]{:S(2)}) collective-permute-start(bf16[2,3,208,128]{3,2,1,0:T(8,128)(2,1)S(1)} %get-tuple-element.19), channel_id=1, source_target_pairs={{2,0},{4,2},{6,4},{3,1},{5,3},{7,5},{10,8},{12,10},{14,12},{11,9},... | collective-permute-start | bytes 958472 | tf_op jit(solution)/shard_map/ppermute | solution.py:145
  24.7 7.8 %collective-permute-start.3 = (bf16[4,3,208,128]{3,2,1,0:T(8,128)(2,1)S(1)}, bf16[4,3,208,128]{3,2,1,0:T(8,128)(2,1)S(1)}, u32[]{:S(2)}, u32[]{:S(2)}) collective-permute-start(bf16[4,3,208,128]{3,2,1,0:T(8,128)(2,1)S(1)} %get-tuple-element.18), channel_id=1, source_target_pairs={{0,8},{8,16},{16,24},{1,9},{9,17},{17,25},{2,10},{10,18},{18,26},{... | collective-permute-start | bytes 1916936 | tf_op jit(solution)/shard_map/ppermute | solution.py:145
  26.1 6.5 %collective-permute-start.4 = (bf16[4,3,208,128]{3,2,1,0:T(8,128)(2,1)S(1)}, bf16[4,3,208,128]{3,2,1,0:T(8,128)(2,1)S(1)}, u32[]{:S(2)}, u32[]{:S(2)}) collective-permute-start(bf16[4,3,208,128]{3,2,1,0:T(8,128)(2,1)S(1)} %get-tuple-element.17), channel_id=1, source_target_pairs={{8,0},{16,8},{24,16},{9,1},{17,9},{25,17},{10,2},{18,10},{26,18},{... | collective-permute-start | bytes 1916936 | tf_op jit(solution)/shard_map/ppermute | solution.py:145
  27.4 5.2 %copy-start = (f32[2,2,2,64,384]{4,3,2,1,0:T(8,128)S(1)}, f32[2,2,2,64,384]{4,3,2,1,0:T(8,128)}, u32[]{:S(2)}) copy-start(f32[2,2,2,64,384]{4,3,2,1,0:T(8,128)} %param.4) | copy-start | bytes 2359300
  56.3 4.0 %collective-permute-start.5 = (f32[1,64,64]{2,1,0:T(8,128)S(1)}, f32[1,64,64]{2,1,0:T(8,128)S(1)}, u32[]{:S(2)}, u32[]{:S(2)}) collective-permute-start(f32[1,64,64]{2,1,0:T(8,128)S(1)} %bitcast.34), channel_id=1, source_target_pairs={{0,1},{1,0},{2,3},{3,2},{4,5},{5,4},{6,7},{7,6},{8,9},{9,8},{10,11... | collective-permute-start | bytes 49160 | tf_op jit(solution)/shard_map/ppermute | solution.py:18
  60.3 5.5 %collective-permute-start.6 = (f32[2,64,64]{2,1,0:T(8,128)S(1)}, f32[2,64,64]{2,1,0:T(8,128)S(1)}, u32[]{:S(2)}, u32[]{:S(2)}) collective-permute-start(f32[2,64,64]{2,1,0:T(8,128)S(1)} %pad_maximum_fusion.3), channel_id=1, source_target_pairs={{0,2},{2,0},{4,6},{6,4},{1,3},{3,1},{5,7},{7,5},{8,10},{10,8},{12,... | collective-permute-start | bytes 98312 | tf_op jit(solution)/shard_map/ppermute | solution.py:18
  65.8 8.0 %collective-permute-start.7 = (f32[4,64,64]{2,1,0:T(8,128)S(1)}, f32[4,64,64]{2,1,0:T(8,128)S(1)}, u32[]{:S(2)}, u32[]{:S(2)}) collective-permute-start(f32[4,64,64]{2,1,0:T(8,128)S(1)} %pad_maximum_fusion.2), channel_id=1, source_target_pairs={{0,8},{8,0},{16,24},{24,16},{1,9},{9,1},{17,25},{25,17},{2,10},{10... | collective-permute-start | bytes 196616 | tf_op jit(solution)/shard_map/ppermute | solution.py:18
where the time goes:
time: 81.8 us; the launch traced here: 81.5 us
  Pallas kernels  43.8 us (54%)
  starting transfers between devices  22.5 us (28%)
  waiting for transfers between devices  11.7 us (14%)
  local copies, waits for them, and re-layouts  2.66 us (3%)
    pallas_call x1, Pallas kernels, body(): pl.pallas_call(functools.partial(third_kernel, stages[2]), out_shape=(lik...  23.7 us
    ppermute x4, starting transfers between devices, from_partner(): lax.ppermute(x, axis, [(i, i ^ 1 << distance) for i in range(lax.axis_siz...  14.9 us
    ppermute x4, waiting for transfers between devices, from_partner(): lax.ppermute(x, axis, [(i, i ^ 1 << distance) for i in range(lax.axis_siz...  10.1 us
    pallas_call x1, Pallas kernels, group_level(): pl.pallas_call(group_kernel, out_shape=jax.ShapeDtypeStruct(scaled.shape,...  7.66 us
    ppermute x4, starting transfers between devices, shifted(): lax.ppermute(x, axis, [(i, i + step) for i in range(size) if 0 <= i + ste...  7.63 us
    pallas_call x1, Pallas kernels, body(): pl.pallas_call(functools.partial(first_kernel, stages[0]), out_shape=like...  7.12 us
    pallas_call x1, Pallas kernels, body(): pl.pallas_call(functools.partial(second_kernel, stages[1]), out_shape=lik...  5.18 us
    unnamed x6, local copies, waits for them, and re-layouts  1.73 us
  transfers between devices with their start and end apart: 8, of which 5 were waited for; matrix products, arithmetic and copies ran while one was open for 1% of the time, Pallas kernels for 15%

commit v1 on v0

v1 whole, which is shorter than its diff:
```python
import functools
import math

import jax
import jax.numpy as jnp
from jax import lax
from jax.experimental import pallas as pl
from jax.experimental.pallas import tpu as pltpu
from jax.sharding import PartitionSpec as P

EPSILON = 0.1
GROUP = 8
SIDE = 2
HIGHEST = lax.Precision.HIGHEST


def from_partner(x, axis, distance):
    return lax.ppermute(x, axis, [(i, i ^ 1 << distance) for i in range(lax.axis_size(axis))])


SMALL = 0.06


def matmul(a, b, precision=HIGHEST):
    return lax.dot_general(
        a, b, (((1,), (0,)), ((), ())), precision=precision, preferred_element_type=jnp.float32
    )


def matmul_t(a, b, precision=HIGHEST):
    return lax.dot_general(
        a, b, (((1,), (1,)), ((), ())), precision=precision, preferred_element_type=jnp.float32
    )


def join(parts, axis):
    return jnp.concatenate(parts, axis=axis)


def halves(x):
    high = x.astype(jnp.bfloat16)
    return high, (x - high.astype(jnp.float32)).astype(jnp.bfloat16)


def thirds(x):
    high = x.astype(jnp.bfloat16)
    rest = x - high.astype(jnp.float32)
    return (high,) + halves(rest)


def positions(shape):
    return (
        lax.broadcasted_iota(jnp.int32, shape, 0),
        lax.broadcasted_iota(jnp.int32, shape, 1),
    )


def unit(rank):
    row, column = positions((rank, rank))
    return jnp.where(row == column, 1.0, 0.0).astype(jnp.float32)


def upper(x):
    row, column = positions(x.shape)
    return jnp.where(row <= column, x, 0.0)


def half_lower(x):
    row, column = positions(x.shape)
    return jnp.where(row > column, x, jnp.where(row == column, 0.5 * x, 0.0))


def gram_of(parts):
    f, g, h = parts
    return matmul_t(join([f, f, g, g, f, h], 1), join([f, g, f, g, h, f], 1), None)


def right_side(parts):
    f, g, h = parts
    return join([f, f, g, g, h, f], 0)


def left_side(x):
    f, g, h = thirds(x)
    first = join([f, g], 1)
    return join([first, first, join([f, h], 1)], 1)


def near_gram(x, y):
    f, g = halves(x)
    u, v = halves(y)
    return matmul_t(join([f, f, g], 1), join([u, v, u], 1), None)


def near_unit_factor(excess):
    x = half_lower(excess)
    square = matmul(x, x, None)
    x = half_lower(excess - matmul_t(x, x, None))
    return x, x - square


def not_small(norm):
    return jnp.logical_not(norm[0, 0] <= SMALL * SMALL)


def batch_rows(work, rank, batch, low, high, width=8):
    shape = (batch, 2 * rank)

    def lane(values, index):
        return jnp.broadcast_to(values[:, rank + index : rank + index + 1], shape)

    for start in range(low, high, width):
        rows = [work[(start + i) * batch : (start + i + 1) * batch, :] for i in range(width)]
        scalars = [
            [lane(rows[i], start + j) if j >= i else None for j in range(width)]
            for i in range(width)
        ]
        for j in range(width):
            root = lax.rsqrt(scalars[j][j])
            rows[j] = rows[j] * root
            factor = [None if i <= j else scalars[j][i] * root for i in range(width)]
            for i in range(j + 1, width):
                rows[i] = rows[i] - factor[i] * rows[j]
                for k in range(i, width):
                    scalars[i][k] = scalars[i][k] - factor[i] * factor[k]
            work[(start + j) * batch : (start + j + 1) * batch, :] = rows[j]
        for lower in range(start + width, high):
            total = work[lower * batch : (lower + 1) * batch, :]
            for j in range(width):
                total = total - lane(rows[j], lower) * rows[j]
            work[lower * batch : (lower + 1) * batch, :] = total


def batch_update(work, rank, batch, low, high):
    size = high - low
    each = 128 // size
    row, column = positions((128, 128))
    for first in range(0, batch, each):
        done = join(
            [work[pl.ds(low * batch + first + i, size, stride=batch), :] for i in range(each)], 0
        )
        turned = done.T
        right = right_side(thirds(done))
        for top in range(high, rank, size):
            factor = join([turned[rank + top : rank + top + size, :]] * each, 0)
            f, g, h = thirds(jnp.where(row // size == column // size, factor, 0.0))
            change = matmul(join([f, g, f, g, f, h], 1), right, None)
            for i in range(each):
                place = pl.ds(top * batch + first + i, size, stride=batch)
                work[place, :] = work[place, :] - change[i * size : (i + 1) * size]


def eliminate_batch(work, rank, batch):
    half = rank // 2
    batch_rows(work, rank, batch, 0, half)
    batch_update(work, rank, batch, 0, half)
    batch_rows(work, rank, batch, half, rank)


def eliminate_single(work, rank):
    shape = (8, 2 * rank)
    row, _ = positions(shape)
    for start in range(0, rank, 8):
        blocks = {m: work[m : m + 8, :] for m in range(start, rank, 8)}
        columns = {
            m: [
                jnp.broadcast_to(blocks[m][:, rank + start + j : rank + start + j + 1], shape)
                for j in range(8)
            ]
            for m in blocks
        }
        done = blocks[start]
        for j in range(8):
            root = lax.rsqrt(columns[start][j][j : j + 1, :])
            line = [columns[start][i][j : j + 1, :] * root for i in range(8)]
            scaled = blocks[start][j : j + 1, :] * root
            done = jnp.where(row == j, scaled, done)
            for m in blocks:
                factor = columns[m][j] * root
                blocks[m] = blocks[m] - factor * scaled
                for i in range(j + 1, 8):
                    columns[m][i] = columns[m][i] - factor * line[i]
        work[start : start + 8, :] = done
        for m in blocks:
            if m > start:
                work[m : m + 8, :] = blocks[m]


def parity(axis):
    return lax.axis_index(axis) % 2


def to_neighbours(low, high, axis):
    size = lax.axis_size(axis)
    even = parity(axis) == 0
    pairs = [(i, i ^ 1) for i in range(size)]
    received = [lax.ppermute(jnp.where(even, high, low), axis, pairs)]
    if size > 2:
        across = [(i, i + 1) for i in range(1, size - 1, 2)]
        across = across + [(j, i) for i, j in across]
        received.insert(0, lax.ppermute(jnp.where(even, low, high), axis, across))
    return received[::-1]


def halo_count(axis):
    return 1 if lax.axis_size(axis) == 2 else 2


def leaf_index(x, y, z):
    return (x * SIDE + y) * SIDE + z


def pair_tables(halos):
    depth = SIDE + halos[2]
    stages = ([], [], [])
    for a in range(SIDE**3):
        place = (a // 4, a // 2 % 2, a % 2)
        for k in range(27):
            at = [p + d for p, d in zip(place, (k // 9 - 1, k // 3 % 3 - 1, k % 3 - 1))]
            sides = tuple((axis, t) for axis, t in enumerate(at) if t in (-1, 2))
            x, y, z = (2 if t == -1 else t for t in at)
            if x == 2:
                stages[2].append((a, k, y * depth + z, sides))
            elif y == 2:
                stages[1].append((a, k, 4 * halos[2] + x * depth + z, sides))
            elif z == 2:
                stages[1].append((a, k, x * SIDE + y, sides))
            else:
                stages[0].append((a, k, leaf_index(x, y, z), sides))
    return stages


def far_sides(halos):
    found = {}
    for axis, name in enumerate(("gx", "gy", "gz")):
        place = lax.axis_index(name)
        odd = place % 2
        other = halos[axis] - 1
        found[axis, -1] = ((place > 0).astype(jnp.int32), (1 - odd) * other)
        found[axis, 2] = ((place < lax.axis_size(name) - 1).astype(jnp.int32), odd * other)
    return found


def list_pairs(pairs, halos, near, listed, blank):
    found = far_sides(halos)
    depth = SIDE + halos[2]
    wide = SIDE + halos[1]
    joint = {}
    count = jnp.int32(0)
    for a, k, source, sides in pairs:
        if sides not in joint:
            inside, moved = jnp.int32(1), jnp.int32(0)
            first = min((axis for axis, _ in sides), default=None)
            steps = {
                0: {0: wide * depth, 1: depth, 2: 1},
                1: {1: SIDE * depth, 2: 1},
                2: {2: SIDE * SIDE},
            }
            for side in sides:
                inside = inside * found[side][0]
                moved = moved + found[side][1] * steps[first][side[0]]
            joint[sides] = (inside, moved * (8 * 27))
        code = jnp.int32((source * 8 + a) * 27 + k)
        taken = near[a * 27 + k]
        if sides:
            code = code + joint[sides][1]
            taken = taken * joint[sides][0]
        listed[count] = code
        count = count + taken
    for i in range(GROUP):
        listed[count + i] = jnp.int32(blank * 8 * 27 + 13)
    return lax.div(count + (GROUP - 1), jnp.int32(GROUP))


def spread_offsets(blocks, count, turned, spread):
    rank3 = blocks.shape[1] - 16
    turned[...] = jnp.zeros_like(turned)
    for s in range(count):
        turned[4 * s : 4 * s + 4, :] = blocks[s, rank3:, :].astype(jnp.float32)[:4]
    columns = turned[...].T.astype(jnp.bfloat16)
    row, lane = positions((128, 384))
    for s in range(count):
        chosen = jnp.where(row == 4 * s + lane // 128, 1.0, 0.0).astype(jnp.bfloat16)
        values = matmul(columns, chosen, None)
        for p in range(3):
            spread[s, p] = values[:, 128 * p : 128 * (p + 1)]


def tile_rows(own, spread, rows):
    r = [own[p] - spread[p, rows, :] for p in range(3)]
    squares = [v * v for v in r]
    softened = squares[0] + squares[1] + squares[2] + EPSILON * EPSILON
    lifted = softened + EPSILON * EPSILON
    root = lax.rsqrt(softened)
    h = root * root * root
    ry, rz = r[1] * h, r[2] * h
    tiles = {(p, p): (squares[p] + lifted) * h for p in range(3)}
    tiles[0, 1], tiles[0, 2], tiles[1, 2] = r[0] * ry, r[0] * rz, r[1] * rz
    return {pq: tile.astype(jnp.bfloat16) for pq, tile in tiles.items()}


def add_pairs(groups, listed, blocks, own, spread, total):
    chunk = 16

    @pl.loop(0, groups)
    def _(group):
        for u in range(GROUP):
            code = listed[group * GROUP + u]
            pair = lax.div(code, jnp.int32(27))
            k = code - pair * 27
            source = lax.shift_right_logical(pair, jnp.int32(3))
            a = lax.bitwise_and(pair, jnp.int32(7))
            dx = lax.div(k, jnp.int32(9))
            dy = lax.div(k, jnp.int32(3)) - dx * 3
            dz = k - dx * 9 - dy * 3
            own_rows = own[a]
            placed = [
                jnp.broadcast_to(
                    own_rows[p : p + 1] + (1 - step).astype(jnp.float32), (chunk, 128)
                )
                for p, step in enumerate((dx, dy, dz))
            ]
            parts = [
                tile_rows(placed, spread.at[source], pl.ds(j, chunk))
                for j in range(0, 128, chunk)
            ]
            tiles = {
                pq: jnp.concatenate([part[pq] for part in parts], axis=0) for pq in parts[0]
            }
            matrix = jnp.concatenate(
                [
                    jnp.concatenate([tiles[min(p, q), max(p, q)] for p in range(3)], axis=1)
                    for q in range(3)
                ],
                axis=0,
            )
            rank = total.shape[1]
            sampled = jnp.concatenate(
                [blocks[source, q * rank : (q + 1) * rank, :] for q in range(3)], axis=1
            )
            total[a] += matmul(sampled, matrix, None)


def fetch(parts, blocks, semaphore):
    copies = []
    first = 0
    for i, part in enumerate(parts):
        copies.append(
            pltpu.make_async_copy(
                part, blocks.at[pl.ds(first, part.shape[0])], semaphore.at[i]
            )
        )
        copies[-1].start()
        first += part.shape[0]
    return copies, first


def near_stage(pairs, halos, near, own, parts, total, listed, blocks, turned, spread, semaphore):
    copies, count = fetch(parts, blocks, semaphore)
    groups = list_pairs(pairs, halos, near, listed, count)
    blocks[count] = jnp.zeros_like(blocks[count])
    for copy in copies:
        copy.wait()
    spread_offsets(blocks, count, turned, spread)
    spread[count] = jnp.zeros_like(spread[count])
    add_pairs(groups, listed, blocks, own, spread, total)


def first_kernel(pairs, halos, near, own, own_blocks, total, *scratch):
    total[...] = jnp.zeros_like(total)
    near_stage(pairs, halos, near, own, [own_blocks], total, *scratch)


def second_kernel(pairs, halos, near, own, before, *rest):
    *parts, total, listed, blocks, turned, spread, semaphore = rest
    total[...] = before[...]
    near_stage(
        pairs, halos, near, own, parts, total, listed, blocks, turned, spread, semaphore
    )


def third_kernel(pairs, halos, near, own, before, sketch, *rest):
    parts, rest = rest[: halos[0]], rest[halos[0] :]
    far, *outs = rest[:5]
    listed, blocks, turned, spread, semaphore, single = rest[5:]
    far[...] = before[...]
    near_stage(
        pairs, halos, near, own, parts, far, listed, blocks, turned, spread, semaphore
    )
    far[...] = sketch[...] - far[...]
    box_level(far, *outs, single)


def pack_kernel(samples, offsets, packed, own, *faces):
    count, rank, leaf_rows = samples.shape
    filler = jnp.zeros((13, 128), jnp.float32)
    for a in range(count):
        for q in range(3):
            packed[a, q * rank : (q + 1) * rank, :] = samples[a, :, q * 128 : (q + 1) * 128]
        rows = jnp.concatenate([offsets[a].astype(jnp.float32), filler], axis=0)
        packed[a, 3 * rank :, :] = rows.astype(jnp.bfloat16)
        own[a] = rows[:8]
    planes = [1 - parity("gz"), parity("gz")]
    for face, plane in zip(faces, planes):
        for column in range(SIDE * SIDE):
            face[column] = packed[column * SIDE + plane]


VMEM_LIMIT = 48 * 1024 * 1024


def near_scratch(pairs, count, block):
    return [
        pltpu.SMEM((len(pairs) + GROUP + 1,), jnp.int32),
        pltpu.VMEM((count + 1,) + block, jnp.bfloat16),
        pltpu.VMEM((128, 128), jnp.float32),
        pltpu.VMEM((count + 1, 3, 128, 128), jnp.float32),
        pltpu.SemaphoreType.DMA((4,)),
    ]


def near_cost(pairs, rank):
    return pl.CostEstimate(
        flops=len(pairs) * 2 * rank * 384 * 384 * 8, bytes_accessed=4 * 1024 * 1024, transcendentals=0
    )


IN_SMEM = pl.BlockSpec(memory_space=pltpu.SMEM)
IN_VMEM = pl.BlockSpec(memory_space=pltpu.VMEM)
ANYWHERE = pl.BlockSpec(memory_space=pl.ANY)


def box_level(far, grams_out, factor_out, samples_out, z_out, single):
    count, rank, _ = far.shape
    eye = unit(rank)
    total = jnp.zeros_like(eye)
    for a in range(count):
        gram = gram_of(thirds(far[a]))
        grams_out[a] = gram
        total = total + gram
    single[...] = join([eye, 0.5 * (total + total.T)], 1)
    eliminate_single(single, rank)
    left = left_side(single[:, :rank])
    lower = upper(single[:, rank:]).T
    excess = -eye
    for a in range(count):
        samples = matmul(left, right_side(thirds(far[a])), None)
        samples_out[a] = samples
        excess = excess + near_gram(samples, samples)
    x, z_out[...] = near_unit_factor(excess)
    factor_out[...] = lower + matmul(lower, x)

    @pl.when(not_small(jnp.sum(excess * excess, keepdims=True)))
    def _():
        single[...] = join([eye, eye + excess], 1)
        eliminate_single(single, rank)
        factor_out[...] = matmul(lower, upper(single[:, rank:]).T)
        for a in range(count):
            samples_out[a] = matmul(single[:, :rank], samples_out[a])
        z_out[...] = jnp.zeros_like(eye)


def leaf_kernel(far, grams, samples, box_z, leaf_out, level_out, work, blocks, es, zs):
    count, rank, leaf_rows = far.shape
    eye = unit(rank)
    for a in range(count):
        work[pl.ds(a, rank, stride=count), :] = join([eye, grams[a]], 1)
    eliminate_batch(work, rank, count)
    largest = jnp.zeros((1, 1), jnp.float32)
    for a in range(count):
        inverse = work[pl.ds(a, rank, stride=count), :][:, :rank]
        basis = matmul(left_side(inverse), right_side(thirds(far[a])), None)
        leaf_out[a] = basis
        products = near_gram(join([basis, samples[a]], 0), basis)
        blocks[a] = products[rank:]
        excess = products[:rank] - eye
        es[a] = excess
        largest = jnp.maximum(largest, jnp.sum(excess * excess, keepdims=True))
    for a in range(count):
        zs[a] = near_unit_factor(es[a])[1]

    @pl.when(not_small(largest))
    def _():
        for a in range(count):
            work[pl.ds(a, rank, stride=count), :] = join([eye, eye + es[a]], 1)
        eliminate_batch(work, rank, count)
        for a in range(count):
            inverse = work[pl.ds(a, rank, stride=count), :][:, :rank]
            leaf_out[a] = matmul(inverse, leaf_out[a])
            blocks[a] = matmul_t(blocks[a], inverse)
            zs[a] = jnp.zeros_like(eye)

    for a in range(count):
        basis = leaf_out[a]
        leaf_out[a] = (basis - matmul(zs[a], basis, None)) * math.sqrt(leaf_rows)
        block = blocks[a]
        blocks[a] = (block - matmul_t(block, zs[a], None)) * math.sqrt(count * rank)
    block = join([blocks[a] for a in range(count)], 1)
    level_out[...] = block - matmul(box_z[...], block, None)


def group_kernel(factors, samples, box_z, nested_out, single, stack):
    count, rank, _ = factors.shape
    eye = unit(rank)
    for b in range(count):
        stack[:, b * rank : (b + 1) * rank] = factors[b]
    parts = thirds(stack[...])
    gram = gram_of(parts)
    single[...] = join([eye, 0.5 * (gram + gram.T)], 1)
    eliminate_single(single, rank)
    block = matmul(left_side(single[:, :rank]), right_side(parts), None)
    excess = near_gram(block, block) - eye
    own = block[:, :rank] * (8.0 * math.sqrt(samples.shape[2]))
    mixing = own - matmul(near_unit_factor(excess)[1], own, None)
    mix_samples(mixing, samples, box_z, nested_out)

    @pl.when(not_small(jnp.sum(excess * excess, keepdims=True)))
    def _():
        single[...] = join([eye, eye + excess], 1)
        eliminate_single(single, rank)
        mix_samples(matmul(single[:, :rank], own), samples, box_z, nested_out)


def mix_samples(mixing, samples, box_z, nested_out):
    mixing = mixing - matmul(mixing, box_z[...], None)
    left = join(halves(mixing) * 2, 1)
    for a in range(samples.shape[0]):
        f, g = halves(samples[a])
        nested_out[a] = matmul(left, join([f, f, g, g], 0), None)


def body(sketch, test_matrix, offsets, near):
    rank, leaf_rows = sketch.shape[3:]
    count = SIDE**3
    halos = [halo_count(axis) for axis in ("gx", "gy", "gz")]
    like = jax.ShapeDtypeStruct
    block = (3 * rank + 16, 128)
    params = pltpu.CompilerParams(vmem_limit_bytes=VMEM_LIMIT)
    flat_near = near.reshape(count * 27)
    flat_sketch = sketch.reshape(count, rank, leaf_rows)
    stages = pair_tables(halos)
    faces = halos[2]
    packed, own, *sent = pl.pallas_call(
        pack_kernel,
        out_shape=(
            like((count,) + block, jnp.bfloat16),
            like((count, 8, 128), jnp.float32),
        )
        + (like((SIDE * SIDE,) + block, jnp.bfloat16),) * faces,
        compiler_params=params,
        name="pack",
    )(test_matrix.reshape(count, rank, leaf_rows), offsets.reshape(count, 3, 128))
    z_halos = [from_partner(sent[0], "gz", 0)]
    if faces == 2:
        size = lax.axis_size("gz")
        across = [(i, i + 1) for i in range(1, size - 1, 2)]
        across = across + [(j, i) for i, j in across]
        z_halos.append(lax.ppermute(sent[1], "gz", across))
    inner = packed.reshape((SIDE, SIDE, SIDE) + block)
    columns = [h.reshape((SIDE, SIDE, 1) + block) for h in z_halos]
    extended = join([inner] + columns, 2)
    depth = extended.shape[2]
    y_halos = to_neighbours(extended[:, 0], extended[:, 1], "gy")
    wide = join([extended] + [h[:, None] for h in y_halos], 1)
    x_halos = to_neighbours(wide[0], wide[1], "gx")

    total = pl.pallas_call(
        functools.partial(first_kernel, stages[0], halos),
        out_shape=like((count, rank, leaf_rows), jnp.float32),
        in_specs=[IN_SMEM, IN_VMEM, ANYWHERE],
        scratch_shapes=near_scratch(stages[0], count, block),
        cost_estimate=near_cost(stages[0], rank),
        compiler_params=params,
        name="near_inner",
    )(flat_near, own, packed)
    flat = lambda x: x.reshape((-1,) + block)
    parts = [flat(h) for h in z_halos + y_halos]
    total = pl.pallas_call(
        functools.partial(second_kernel, stages[1], halos),
        out_shape=like((count, rank, leaf_rows), jnp.float32),
        in_specs=[IN_SMEM, IN_VMEM, IN_VMEM] + [ANYWHERE] * len(parts),
        scratch_shapes=near_scratch(stages[1], 4 * faces + SIDE * depth * halos[1], block),
        cost_estimate=near_cost(stages[1], rank),
        compiler_params=params,
        name="near_columns",
    )(flat_near, own, total, *parts)
    whole = like((count, rank, leaf_rows), jnp.float32)
    squares = like((count, rank, rank), jnp.float32)
    square = like((rank, rank), jnp.float32)
    single_scratch = pltpu.VMEM((rank, 2 * rank), jnp.float32)
    far, grams, factor, samples, box_z = pl.pallas_call(
        functools.partial(third_kernel, stages[2], halos),
        out_shape=(whole, squares, square, whole, square),
        in_specs=[IN_SMEM, IN_VMEM, IN_VMEM, IN_VMEM] + [ANYWHERE] * halos[0],
        scratch_shapes=near_scratch(stages[2], halos[0] * (SIDE + halos[1]) * depth, block)
        + [single_scratch],
        compiler_params=params,
        name="near_sides_and_box_level",
    )(flat_near, own, total, flat_sketch, *[flat(h) for h in x_halos])
    grouped = factor[None]
    for axis in ("gz", "gy", "gx"):
        grouped = jnp.concatenate([grouped, from_partner(grouped, axis, 0)], axis=0)
    leaf_t, level_t = pl.pallas_call(
        leaf_kernel,
        out_shape=(whole, like((rank, count * rank), jnp.float32)),
        scratch_shapes=[pltpu.VMEM((rank * count, 2 * rank), jnp.float32)]
        + [pltpu.VMEM((count, rank, rank), jnp.float32)] * 3,
        cost_estimate=pl.CostEstimate(
            flops=8 * 1000 * 1000 * 1000, bytes_accessed=4 * 1024 * 1024, transcendentals=0
        ),
        compiler_params=params,
        name="leaf_level",
    )(far, grams, samples, box_z)
    nested = pl.pallas_call(
        group_kernel,
        out_shape=whole,
        scratch_shapes=[
            single_scratch,
            pltpu.VMEM((rank, count * rank), jnp.float32),
        ],
        compiler_params=params,
        name="group_level",
    )(grouped, samples, box_z)
    return (leaf_t.reshape(sketch.shape), level_t[None, None, None], nested.reshape(sketch.shape))


def solution(mesh):
    placed = (
        P("gx", "gy", "gz", None, None),
        P("gx", "gy", "gz", None, None),
        P("gx", "gy", "gz", None, None),
        P("gx", "gy", "gz", None),
    )
    return jax.shard_map(
        body,
        mesh=mesh,
        in_specs=placed,
        out_specs=(
            P("gx", "gy", "gz", None, None),
            P("gx", "gy", "gz", None, None),
            P("gx", "gy", "gz", None, None),
        ),
        check_vma=False,
    )
```

time: 81.8 us -> 64.7 us (0.79)
  the two profiles are of different devices: /device:TPU:0 before, /device:TPU:15 now
where the time goes in v1:
time: 64.7 us; the launch traced here: 64.8 us
  Pallas kernels  33.3 us (51%)
  starting transfers between devices  17.9 us (28%)
  waiting for transfers between devices  10 us (15%)
  local copies, waits for them, and re-layouts  2.53 us (4%)
  between operations  0.78 us (1%)
    ppermute x4, waiting for transfers between devices, from_partner(): lax.ppermute(x, axis, [(i, i ^ 1 << distance) for i in range(lax.axis_siz...  9.95 us
    ppermute x4, starting transfers between devices, from_partner(): lax.ppermute(x, axis, [(i, i ^ 1 << distance) for i in range(lax.axis_siz...  9.92 us
    pallas_call x1, Pallas kernels, body(): pl.pallas_call(functools.partial(third_kernel, stages[2], halos), out_sha...  9.09 us
    pallas_call x1, Pallas kernels, body(): pl.pallas_call(functools.partial(first_kernel, stages[0], halos), out_sha...  7.12 us
    pallas_call x1, Pallas kernels, body(): pl.pallas_call(functools.partial(second_kernel, stages[1], halos), out_sh...  6.8 us
    pallas_call x1, Pallas kernels, body(): pl.pallas_call(leaf_kernel, out_shape=(whole, like((rank, count * rank),...  6.12 us
    ppermute x2, starting transfers between devices, to_neighbours(): received = [lax.ppermute(jnp.where(even, high, low), axis, pairs)]  4.1 us
    pallas_call x1, Pallas kernels, body(): pl.pallas_call(group_kernel, out_shape=whole, scratch_shapes=[single_scra...  4.1 us
  transfers between devices with their start and end apart: 8, of which 3 were waited for; matrix products, arithmetic and copies ran while one was open for 1% of the time, Pallas kernels for 31%

profile of v1, /device:TPU:15, one launch (start us, length us, event | category | flops | bytes accessed | tf_op | source)
XLA Modules:
  0.0 64.8 jit_solution(10161595512728478283)
XLA Ops:
  0.6 0.7 %copy.7 = bf16[2,2,2,3,128]{4,3,2,1,0:T(4,128)(2,1)S(1)} copy(bf16[2,2,2,3,128]{4,2,3,1,0:T(2,128)(2,1)} %param.6) | data formatting | bytes 12288 | tf_op args[2]
  1.3 0.0 copy-start.1
  1.3 1.0 %copy-done.1 = bf16[2,2,2,64,384]{4,3,2,1,0:T(8,128)(2,1)S(1)} copy-done((bf16[2,2,2,64,384]{4,3,2,1,0:T(8,128)(2,1)S(1)}, bf16[2,2,2,64,384]{4,3,2,1,0:T(8,128)(2,1)}, u32[]{:S(2)}) %copy-start.1) | copy-done | bytes 393240
  2.3 0.1 pack.1
  2.4 0.3 collective-permute-start
  2.7 0.8 %reshape.50.near = s32[216]{0:T(256)S(1)} reshape(s32[2,2,2,27]{3,2,1,0:T(2,128)} %param.7) | data formatting | bytes 1728 | tf_op jit(solution)/shard_map/reshape | solution.py:539
  3.5 5.1 %collective-permute-done.rest_0_ = bf16[4,208,128]{2,1,0:T(8,128)(2,1)S(1)} collective-permute-done((bf16[4,208,128]{2,1,0:T(8,128)(2,1)S(1)}, bf16[4,208,128]{2,1,0:T(8,128)(2,1)S(1)}, u32[]{:S(2)}, u32[]{:S(2)}) %collective-permute-start) | collective-permute-done | bytes 213024 | tf_op jit(solution)/shard_map/ppermute | solution.py:18
  8.7 3.2 %collective-permute-start.2 = (bf16[2,3,208,128]{3,2,1,0:T(8,128)(2,1)S(1)}, bf16[2,3,208,128]{3,2,1,0:T(8,128)(2,1)S(1)}, u32[]{:S(2)}, u32[]{:S(2)}) collective-permute-start(bf16[2,3,208,128]{3,2,1,0:T(8,128)(2,1)S(1)} %get-tuple-element.25), channel_id=1, source_target_pairs={{2,4},{4,2},{3,5},{5,3},{10,12},{12,10},{11,13},{13,11},{18,20},{2... | collective-permute-start | bytes 958472 | tf_op jit(solution)/shard_map/ppermute | solution.py:201
  11.9 0.1 collective-permute-start.1
  12.0 7.1 %near_inner.1.before = f32[8,64,384]{2,1,0:T(8,128)S(1)} custom-call(s32[216]{0:T(256)S(1)} %reshape.50.near, f32[8,8,128]{2,1,0:T(8,128)S(1)} %get-tuple-element.13.own, bf16[8,208,128]{2,1,0:T(8,128)(2,1)S(1)} %get-tuple-element.14.own_blocks), custom_call_target="tpu_custom_call" | custom-call | flops 9663676416 | bytes 4194304 | tf_op jit(solution)/shard_map/near_inner/pallas_call | solution.py:567
  19.1 0.0 collective-permute-done.2
  19.1 0.0 collective-permute-done.1
  19.2 0.1 pad_maximum_fusion
  19.3 0.1 select_bitcast_fusion
  19.4 0.7 %collective-permute-start.4 = (bf16[4,3,208,128]{3,2,1,0:T(8,128)(2,1)S(1)}, bf16[4,3,208,128]{3,2,1,0:T(8,128)(2,1)S(1)}, u32[]{:S(2)}, u32[]{:S(2)}) collective-permute-start(bf16[4,3,208,128]{3,2,1,0:T(8,128)(2,1)S(1)} %get-tuple-element.23), channel_id=1, source_target_pairs={{8,16},{16,8},{9,17},{17,9},{10,18},{18,10},{11,19},{19,11},{12,20... | collective-permute-start | bytes 1916936 | tf_op jit(solution)/shard_map/ppermute | solution.py:201
  20.1 4.0 %collective-permute-start.3 = (bf16[4,3,208,128]{3,2,1,0:T(8,128)(2,1)S(1)}, bf16[4,3,208,128]{3,2,1,0:T(8,128)(2,1)S(1)}, u32[]{:S(2)}, u32[]{:S(2)}) collective-permute-start(bf16[4,3,208,128]{3,2,1,0:T(8,128)(2,1)S(1)} %get-tuple-element.24), channel_id=1, source_target_pairs={{0,8},{8,0},{16,24},{24,16},{1,9},{9,1},{17,25},{25,17},{2,10},{10... | collective-permute-start | bytes 1916936 | tf_op jit(solution)/shard_map/ppermute | solution.py:197
  24.1 0.0 copy-start
  24.1 6.8 %near_columns.1.before = f32[8,64,384]{2,1,0:T(8,128)S(1)} custom-call(s32[216]{0:T(256)S(1)} %reshape.50.near, f32[8,8,128]{2,1,0:T(8,128)S(1)} %get-tuple-element.13.own, f32[8,64,384]{2,1,0:T(8,128)S(1)} %near_inner.1.before, bf16[4,208,128]{2,1,0:T(8,128)(2,1)S(1)} %collective-permute-done.rest_0_, bf16[6,208,128]{2,1,0:T(8,128)(2,1)S(1)} %bitcast.33, ...), custom_call_target="tpu_custom_call" | custom-call | flops 12079595520 | bytes 4194304 | tf_op jit(solution)/shard_map/near_columns/pallas_call | solution.py:578
  30.9 0.0 collective-permute-done.4
  30.9 0.0 collective-permute-done.3
  30.9 0.0 copy-done
  30.9 9.1 %near_sides_and_box_level.1 = (f32[8,64,384]{2,1,0:T(8,128)S(1)}, f32[8,64,64]{2,1,0:T(8,128)S(1)}, f32[64,64]{1,0:T(8,128)S(1)}, f32[8,64,384]{2,1,0:T(8,128)S(1)}, f32[64,64]{1,0:T(8,128)S(1)}) custom-call(s32[216]{0:T(256)S(1)} %reshape.50.near, f32[8,8,128]{2,1,0:T(8,128)S(1)} %get-tuple-element.13.own, f32[8,64,384]{2,1,0:T(8,128)S(1)} %near_columns.1.before, ...), custom_call_target="tpu_custom_call" | custom-call | tf_op jit(solution)/shard_map/near_sides_and_box_level/pallas_call | solution.py:591
  40.0 1.1 %collective-permute-start.5 = (f32[1,64,64]{2,1,0:T(8,128)S(1)}, f32[1,64,64]{2,1,0:T(8,128)S(1)}, u32[]{:S(2)}, u32[]{:S(2)}) collective-permute-start(f32[1,64,64]{2,1,0:T(8,128)S(1)} %bitcast.34), channel_id=1, source_target_pairs={{0,1},{1,0},{2,3},{3,2},{4,5},{5,4},{6,7},{7,6},{8,9},{9,8},{10,11... | collective-permute-start | bytes 49160 | tf_op jit(solution)/shard_map/ppermute | solution.py:18
  41.1 1.8 %collective-permute-done.5 = f32[1,64,64]{2,1,0:T(8,128)S(1)} collective-permute-done((f32[1,64,64]{2,1,0:T(8,128)S(1)}, f32[1,64,64]{2,1,0:T(8,128)S(1)}, u32[]{:S(2)}, u32[]{:S(2)}) %collective-permute-start.5) | collective-permute-done | bytes 16416 | tf_op jit(solution)/shard_map/ppermute | solution.py:18
  42.9 0.1 collective-permute-start.6
  43.0 3.1 %collective-permute-done.6 = f32[2,64,64]{2,1,0:T(8,128)S(1)} collective-permute-done((f32[2,64,64]{2,1,0:T(8,128)S(1)}, f32[2,64,64]{2,1,0:T(8,128)S(1)}, u32[]{:S(2)}, u32[]{:S(2)}) %collective-permute-start.6) | collective-permute-done | bytes 32800 | tf_op jit(solution)/shard_map/ppermute | solution.py:18
  46.1 8.5 %collective-permute-start.7 = (f32[4,64,64]{2,1,0:T(8,128)S(1)}, f32[4,64,64]{2,1,0:T(8,128)S(1)}, u32[]{:S(2)}, u32[]{:S(2)}) collective-permute-start(f32[4,64,64]{2,1,0:T(8,128)S(1)} %pad_maximum_fusion.2), channel_id=1, source_target_pairs={{0,8},{8,0},{16,24},{24,16},{1,9},{9,1},{17,25},{25,17},{2,10},{10... | collective-permute-start | bytes 196616 | tf_op jit(solution)/shard_map/ppermute | solution.py:18
  54.6 6.1 %leaf_level.1 = (f32[8,64,384]{2,1,0:T(8,128)}, f32[64,512]{1,0:T(8,128)}) custom-call(f32[8,64,384]{2,1,0:T(8,128)S(1)} %get-tuple-element.16.far, f32[8,64,64]{2,1,0:T(8,128)S(1)} %get-tuple-element.17.grams, f32[8,64,384]{2,1,0:T(8,128)S(1)} %get-tuple-element.18.samples, f32[64,64]{1,0:T(8,128)S(1)} %get-tuple-element.19.box_z), custom_call_target="tpu_custom_call" | custom-call | flops 8000000000 | bytes 4194304 | tf_op jit(solution)/shard_map/leaf_level/pallas_call | solution.py:603
  60.7 0.0 collective-permute-done.7
  60.7 4.1 %group_level.1 = f32[8,64,384]{2,1,0:T(8,128)} custom-call(f32[8,64,64]{2,1,0:T(8,128)S(1)} %pad_maximum_fusion.1.factors, f32[8,64,384]{2,1,0:T(8,128)S(1)} %get-tuple-element.18.samples, f32[64,64]{1,0:T(8,128)S(1)} %get-tuple-element.19.box_z), custom_call_target="tpu_custom_call" | custom-call | tf_op jit(solution)/shard_map/group_level/pallas_call | solution.py:614
  (6 shorter events, 0.2 us)
Async XLA Ops:
  1.3 1.0 %copy-start.1 = (bf16[2,2,2,64,384]{4,3,2,1,0:T(8,128)(2,1)S(1)}, bf16[2,2,2,64,384]{4,3,2,1,0:T(8,128)(2,1)}, u32[]{:S(2)}) copy-start(bf16[2,2,2,64,384]{4,3,2,1,0:T(8,128)(2,1)} %param.5) | copy-start | bytes 1179652
  2.4 6.2 %collective-permute-start = (bf16[4,208,128]{2,1,0:T(8,128)(2,1)S(1)}, bf16[4,208,128]{2,1,0:T(8,128)(2,1)S(1)}, u32[]{:S(2)}, u32[]{:S(2)}) collective-permute-start(bf16[4,208,128]{2,1,0:T(8,128)(2,1)S(1)} %get-tuple-element.15), channel_id=1, source_target_pairs={{0,1},{1,0},{2,3},{3,2},{4,5},{5,4},{6,7},{7,6},{8,9},{9,8},{10,11... | collective-permute-start | bytes 638984 | tf_op jit(solution)/shard_map/ppermute | solution.py:18
  8.7 10.4 %collective-permute-start.2 = (bf16[2,3,208,128]{3,2,1,0:T(8,128)(2,1)S(1)}, bf16[2,3,208,128]{3,2,1,0:T(8,128)(2,1)S(1)}, u32[]{:S(2)}, u32[]{:S(2)}) collective-permute-start(bf16[2,3,208,128]{3,2,1,0:T(8,128)(2,1)S(1)} %get-tuple-element.25), channel_id=1, source_target_pairs={{2,4},{4,2},{3,5},{5,3},{10,12},{12,10},{11,13},{13,11},{18,20},{2... | collective-permute-start | bytes 958472 | tf_op jit(solution)/shard_map/ppermute | solution.py:201
  11.9 7.3 %collective-permute-start.1 = (bf16[2,3,208,128]{3,2,1,0:T(8,128)(2,1)S(1)}, bf16[2,3,208,128]{3,2,1,0:T(8,128)(2,1)S(1)}, u32[]{:S(2)}, u32[]{:S(2)}) collective-permute-start(bf16[2,3,208,128]{3,2,1,0:T(8,128)(2,1)S(1)} %get-tuple-element.26), channel_id=1, source_target_pairs={{0,2},{2,0},{4,6},{6,4},{1,3},{3,1},{5,7},{7,5},{8,10},{10,8},{12,... | collective-permute-start | bytes 958472 | tf_op jit(solution)/shard_map/ppermute | solution.py:197
  19.4 11.6 %collective-permute-start.4 = (bf16[4,3,208,128]{3,2,1,0:T(8,128)(2,1)S(1)}, bf16[4,3,208,128]{3,2,1,0:T(8,128)(2,1)S(1)}, u32[]{:S(2)}, u32[]{:S(2)}) collective-permute-start(bf16[4,3,208,128]{3,2,1,0:T(8,128)(2,1)S(1)} %get-tuple-element.23), channel_id=1, source_target_pairs={{8,16},{16,8},{9,17},{17,9},{10,18},{18,10},{11,19},{19,11},{12,20... | collective-permute-start | bytes 1916936 | tf_op jit(solution)/shard_map/ppermute | solution.py:201
  20.1 10.9 %collective-permute-start.3 = (bf16[4,3,208,128]{3,2,1,0:T(8,128)(2,1)S(1)}, bf16[4,3,208,128]{3,2,1,0:T(8,128)(2,1)S(1)}, u32[]{:S(2)}, u32[]{:S(2)}) collective-permute-start(bf16[4,3,208,128]{3,2,1,0:T(8,128)(2,1)S(1)} %get-tuple-element.24), channel_id=1, source_target_pairs={{0,8},{8,0},{16,24},{24,16},{1,9},{9,1},{17,25},{25,17},{2,10},{10... | collective-permute-start | bytes 1916936 | tf_op jit(solution)/shard_map/ppermute | solution.py:197
  24.1 6.8 %copy-start = (f32[2,2,2,64,384]{4,3,2,1,0:T(8,128)S(1)}, f32[2,2,2,64,384]{4,3,2,1,0:T(8,128)}, u32[]{:S(2)}) copy-start(f32[2,2,2,64,384]{4,3,2,1,0:T(8,128)} %param.4) | copy-start | bytes 2359300
  40.0 2.8 %collective-permute-start.5 = (f32[1,64,64]{2,1,0:T(8,128)S(1)}, f32[1,64,64]{2,1,0:T(8,128)S(1)}, u32[]{:S(2)}, u32[]{:S(2)}) collective-permute-start(f32[1,64,64]{2,1,0:T(8,128)S(1)} %bitcast.34), channel_id=1, source_target_pairs={{0,1},{1,0},{2,3},{3,2},{4,5},{5,4},{6,7},{7,6},{8,9},{9,8},{10,11... | collective-permute-start | bytes 49160 | tf_op jit(solution)/shard_map/ppermute | solution.py:18
  42.9 3.2 %collective-permute-start.6 = (f32[2,64,64]{2,1,0:T(8,128)S(1)}, f32[2,64,64]{2,1,0:T(8,128)S(1)}, u32[]{:S(2)}, u32[]{:S(2)}) collective-permute-start(f32[2,64,64]{2,1,0:T(8,128)S(1)} %pad_maximum_fusion.3), channel_id=1, source_target_pairs={{0,2},{2,0},{4,6},{6,4},{1,3},{3,1},{5,7},{7,5},{8,10},{10,8},{12,... | collective-permute-start | bytes 98312 | tf_op jit(solution)/shard_map/ppermute | solution.py:18
  46.1 14.6 %collective-permute-start.7 = (f32[4,64,64]{2,1,0:T(8,128)S(1)}, f32[4,64,64]{2,1,0:T(8,128)S(1)}, u32[]{:S(2)}, u32[]{:S(2)}) collective-permute-start(f32[4,64,64]{2,1,0:T(8,128)S(1)} %pad_maximum_fusion.2), channel_id=1, source_target_pairs={{0,8},{8,0},{16,24},{24,16},{1,9},{9,1},{17,25},{25,17},{2,10},{10... | collective-permute-start | bytes 196616 | tf_op jit(solution)/shard_map/ppermute | solution.py:18

commit v2 on v1

--- a/solution.py
+++ b/solution.py
@@ -212,21 +212,23 @@
 
 def pair_tables(halos):
     depth = SIDE + halos[2]
-    stages = ([], [], [])
+    stages = ([], [], [], [])
     for a in range(SIDE**3):
         place = (a // 4, a // 2 % 2, a % 2)
         for k in range(27):
             at = [p + d for p, d in zip(place, (k // 9 - 1, k // 3 % 3 - 1, k % 3 - 1))]
             sides = tuple((axis, t) for axis, t in enumerate(at) if t in (-1, 2))
             x, y, z = (2 if t == -1 else t for t in at)
-            if x == 2:
-                stages[2].append((a, k, y * depth + z, sides))
+            if at[0] == -1:
+                stages[3].append((a, k, y * depth + z, sides[1:], True))
+            elif at[0] == 2:
+                continue
             elif y == 2:
-                stages[1].append((a, k, 4 * halos[2] + x * depth + z, sides))
+                stages[2].append((a, k, x * depth + z, sides, False))
             elif z == 2:
-                stages[1].append((a, k, x * SIDE + y, sides))
+                stages[1].append((a, k, SIDE**3 + x * SIDE + y, sides, False))
             else:
-                stages[0].append((a, k, leaf_index(x, y, z), sides))
+                stages[a * 2 // SIDE**3].append((a, k, leaf_index(x, y, z), sides, False))
     return stages
 
 
@@ -241,32 +243,39 @@
     return found
 
 
-def list_pairs(pairs, halos, near, listed, blank):
+def list_pairs(pairs, halos, near, listed, count, x_side):
     found = far_sides(halos)
     depth = SIDE + halos[2]
-    wide = SIDE + halos[1]
     joint = {}
-    count = jnp.int32(0)
-    for a, k, source, sides in pairs:
-        if sides not in joint:
-            inside, moved = jnp.int32(1), jnp.int32(0)
-            first = min((axis for axis, _ in sides), default=None)
-            steps = {
-                0: {0: wide * depth, 1: depth, 2: 1},
-                1: {1: SIDE * depth, 2: 1},
-                2: {2: SIDE * SIDE},
-            }
+    for a, k, source, sides, across in pairs:
+        key = (sides, across)
+        if key not in joint:
+            inside, moved, entry = jnp.int32(1), jnp.int32(0), jnp.int32(0)
+            if across:
+                steps = {1: depth, 2: 1}
+                inside = x_side[1]
+                entry = x_side[0] * (4 * 27 + 18)
+            elif any(axis == 1 for axis, _ in sides):
+                steps = {1: SIDE * depth, 2: 1}
+            else:
+                steps = {2: SIDE * SIDE}
             for side in sides:
                 inside = inside * found[side][0]
-                moved = moved + found[side][1] * steps[first][side[0]]
-            joint[sides] = (inside, moved * (8 * 27))
+                moved = moved + found[side][1] * steps[side[0]]
+            joint[key] = (inside, moved * (8 * 27) + entry, entry)
+        inside, moved, entry = joint[key]
         code = jnp.int32((source * 8 + a) * 27 + k)
-        taken = near[a * 27 + k]
-        if sides:
-            code = code + joint[sides][1]
-            taken = taken * joint[sides][0]
+        if sides or across:
+            taken = near[a * 27 + k + entry] * inside
+            code = code + moved
+        else:
+            taken = near[a * 27 + k]
         listed[count] = code
         count = count + taken
+    return count
+
+
+def close_list(listed, count, blank):
     for i in range(GROUP):
         listed[count + i] = jnp.int32(blank * 8 * 27 + 13)
     return lax.div(count + (GROUP - 1), jnp.int32(GROUP))
@@ -355,9 +364,23 @@
     return copies, first
 
 
-def near_stage(pairs, halos, near, own, parts, total, listed, blocks, turned, spread, semaphore):
+def near_stage(stage, near, own, parts, total, listed, blocks, turned, spread, semaphore):
+    halos, lists = stage
     copies, count = fetch(parts, blocks, semaphore)
-    groups = list_pairs(pairs, halos, near, listed, count)
+    odd = lax.axis_index("gx") % 2
+    size = lax.axis_size("gx")
+    start = jnp.int32(0)
+    for pairs, first, within in lists:
+        pairs = [(a, k, source + first, sides, across) for a, k, source, sides, across in pairs]
+        x_side = None
+        if within is True:
+            x_side = (1 - odd, jnp.int32(1))
+        elif within is False:
+            place = lax.axis_index("gx")
+            inside = jnp.logical_and(place > 0, place < size - 1).astype(jnp.int32)
+            x_side = (odd, inside)
+        start = list_pairs(pairs, halos, near, listed, start, x_side)
+    groups = close_list(listed, start, count)
     blocks[count] = jnp.zeros_like(blocks[count])
     for copy in copies:
         copy.wait()
@@ -366,29 +389,24 @@
     add_pairs(groups, listed, blocks, own, spread, total)
 
 
-def first_kernel(pairs, halos, near, own, own_blocks, total, *scratch):
+def first_kernel(stage, near, own, own_blocks, total, *scratch):
     total[...] = jnp.zeros_like(total)
-    near_stage(pairs, halos, near, own, [own_blocks], total, *scratch)
-
-
-def second_kernel(pairs, halos, near, own, before, *rest):
+    near_stage(stage, near, own, [own_blocks], total, *scratch)
+
+
+def next_kernel(stage, near, own, before, *rest):
     *parts, total, listed, blocks, turned, spread, semaphore = rest
     total[...] = before[...]
-    near_stage(
-        pairs, halos, near, own, parts, total, listed, blocks, turned, spread, semaphore
-    )
-
-
-def third_kernel(pairs, halos, near, own, before, sketch, *rest):
-    parts, rest = rest[: halos[0]], rest[halos[0] :]
-    far, *outs = rest[:5]
-    listed, blocks, turned, spread, semaphore, single = rest[5:]
+    near_stage(stage, near, own, parts, total, listed, blocks, turned, spread, semaphore)
+
+
+def last_kernel(stage, near, own, before, sketch, *rest):
+    *parts, far, grams, factor, samples, z_out = rest[:-6]
+    listed, blocks, turned, spread, semaphore, single = rest[-6:]
     far[...] = before[...]
-    near_stage(
-        pairs, halos, near, own, parts, far, listed, blocks, turned, spread, semaphore
-    )
+    near_stage(stage, near, own, parts, far, listed, blocks, turned, spread, semaphore)
     far[...] = sketch[...] - far[...]
-    box_level(far, *outs, single)
+    box_level(far, grams, factor, samples, z_out, single)
 
 
 def pack_kernel(samples, offsets, packed, own, *faces):
@@ -409,9 +427,10 @@
 VMEM_LIMIT = 48 * 1024 * 1024
 
 
-def near_scratch(pairs, count, block):
+def near_scratch(stage, count, block):
+    length = sum(len(pairs) for pairs, _, _ in stage[1])
     return [
-        pltpu.SMEM((len(pairs) + GROUP + 1,), jnp.int32),
+        pltpu.SMEM((length + GROUP + 1,), jnp.int32),
         pltpu.VMEM((count + 1,) + block, jnp.bfloat16),
         pltpu.VMEM((128, 128), jnp.float32),
         pltpu.VMEM((count + 1, 3, 128, 128), jnp.float32),
@@ -419,9 +438,9 @@
     ]
 
 
-def near_cost(pairs, rank):
+def cost(microseconds):
     return pl.CostEstimate(
-        flops=len(pairs) * 2 * rank * 384 * 384 * 8, bytes_accessed=4 * 1024 * 1024, transcendentals=0
+        flops=microseconds * 1000 * 1000 * 1000, bytes_accessed=4 * 1024 * 1024, transcendentals=0
     )
 
 
@@ -460,15 +479,20 @@
         z_out[...] = jnp.zeros_like(eye)
 
 
-def leaf_kernel(far, grams, samples, box_z, leaf_out, level_out, work, blocks, es, zs):
-    count, rank, leaf_rows = far.shape
+def leaf_factors(grams, work):
+    count, rank, _ = grams.shape
     eye = unit(rank)
     for a in range(count):
         work[pl.ds(a, rank, stride=count), :] = join([eye, grams[a]], 1)
     eliminate_batch(work, rank, count)
+
+
+def leaf_kernel(far, factors, samples, box_z, leaf_out, level_out, work, blocks, es, zs):
+    count, rank, leaf_rows = far.shape
+    eye = unit(rank)
     largest = jnp.zeros((1, 1), jnp.float32)
     for a in range(count):
-        inverse = work[pl.ds(a, rank, stride=count), :][:, :rank]
+        inverse = factors[pl.ds(a, rank, stride=count), :][:, :rank]
         basis = matmul(left_side(inverse), right_side(thirds(far[a])), None)
         leaf_out[a] = basis
         products = near_gram(join([basis, samples[a]], 0), basis)
@@ -560,57 +584,78 @@
     columns = [h.reshape((SIDE, SIDE, 1) + block) for h in z_halos]
     extended = join([inner] + columns, 2)
     depth = extended.shape[2]
-    y_halos = to_neighbours(extended[:, 0], extended[:, 1], "gy")
-    wide = join([extended] + [h[:, None] for h in y_halos], 1)
-    x_halos = to_neighbours(wide[0], wide[1], "gx")
-
-    total = pl.pallas_call(
-        functools.partial(first_kernel, stages[0], halos),
-        out_shape=like((count, rank, leaf_rows), jnp.float32),
-        in_specs=[IN_SMEM, IN_VMEM, ANYWHERE],
-        scratch_shapes=near_scratch(stages[0], count, block),
-        cost_estimate=near_cost(stages[0], rank),
-        compiler_params=params,
-        name="near_inner",
-    )(flat_near, own, packed)
-    flat = lambda x: x.reshape((-1,) + block)
-    parts = [flat(h) for h in z_halos + y_halos]
-    total = pl.pallas_call(
-        functools.partial(second_kernel, stages[1], halos),
-        out_shape=like((count, rank, leaf_rows), jnp.float32),
-        in_specs=[IN_SMEM, IN_VMEM, IN_VMEM] + [ANYWHERE] * len(parts),
-        scratch_shapes=near_scratch(stages[1], 4 * faces + SIDE * depth * halos[1], block),
-        cost_estimate=near_cost(stages[1], rank),
-        compiler_params=params,
-        name="near_columns",
-    )(flat_near, own, total, *parts)
+    flat = lambda parts: [x.reshape((-1,) + block) for x in parts]
+    column = (SIDE + halos[1]) * depth
+    y_blocks = SIDE * depth * halos[1]
     whole = like((count, rank, leaf_rows), jnp.float32)
     squares = like((count, rank, rank), jnp.float32)
     square = like((rank, rank), jnp.float32)
     single_scratch = pltpu.VMEM((rank, 2 * rank), jnp.float32)
+
+    stage = (halos, [(stages[0], 0, None)])
+    total = pl.pallas_call(
+        functools.partial(first_kernel, stage),
+        out_shape=whole,
+        in_specs=[IN_SMEM, IN_VMEM, ANYWHERE],
+        scratch_shapes=near_scratch(stage, count, block),
+        cost_estimate=cost(4),
+        compiler_params=params,
+        name="near_inner",
+    )(flat_near, own, packed)
+
+    extended, total = lax.optimization_barrier((extended, total))
+    y_halos = to_neighbours(extended[:, 0], extended[:, 1], "gy")
+
+    def add_stage(stage, total, parts, name, time):
+        return pl.pallas_call(
+            functools.partial(next_kernel, stage),
+            out_shape=whole,
+            in_specs=[IN_SMEM, IN_VMEM, IN_VMEM] + [ANYWHERE] * len(parts),
+            scratch_shapes=near_scratch(stage, sum(part.shape[0] for part in parts), block),
+            cost_estimate=cost(time),
+            compiler_params=params,
+            name=name,
+        )(flat_near, own, total, *parts)
+
+    stage = (halos, [(stages[1], 0, None)])
+    total = add_stage(stage, total, [packed] + flat(z_halos), "near_inner_and_z", 5)
+    wide = join([extended] + [h[:, None] for h in y_halos], 1)
+    wide, total = lax.optimization_barrier((wide, total))
+    x_halos = to_neighbours(wide[0], wide[1], "gx")
+    stage = (halos, [(stages[2], 0, None), (stages[3], y_blocks, True)])
+    total = add_stage(stage, total, flat(y_halos) + flat(x_halos[:1]), "near_y_and_x", 7)
+    stage = (halos, [(stages[3], 0, False)] if halos[0] == 2 else [])
+    parts = flat(x_halos[1:])
     far, grams, factor, samples, box_z = pl.pallas_call(
-        functools.partial(third_kernel, stages[2], halos),
+        functools.partial(last_kernel, stage),
         out_shape=(whole, squares, square, whole, square),
-        in_specs=[IN_SMEM, IN_VMEM, IN_VMEM, IN_VMEM] + [ANYWHERE] * halos[0],
-        scratch_shapes=near_scratch(stages[2], halos[0] * (SIDE + halos[1]) * depth, block)
-        + [single_scratch],
+        in_specs=[IN_SMEM, IN_VMEM, IN_VMEM, IN_VMEM] + [ANYWHERE] * len(parts),
+        scratch_shapes=near_scratch(stage, column * len(parts), block) + [single_scratch],
         compiler_params=params,
-        name="near_sides_and_box_level",
-    )(flat_near, own, total, flat_sketch, *[flat(h) for h in x_halos])
+        name="near_x_and_box_level",
+    )(flat_near, own, total, flat_sketch, *parts)
     grouped = factor[None]
-    for axis in ("gz", "gy", "gx"):
-        grouped = jnp.concatenate([grouped, from_partner(grouped, axis, 0)], axis=0)
+    grouped = join([grouped, from_partner(grouped, "gz", 0)], 0)
+    factors = pl.pallas_call(
+        leaf_factors,
+        out_shape=like((rank * count, 2 * rank), jnp.float32),
+        cost_estimate=cost(3),
+        compiler_params=params,
+        name="leaf_factors",
+    )(grams)
+    grouped, factors = lax.optimization_barrier((grouped, factors))
+    grouped = join([grouped, from_partner(grouped, "gy", 0)], 0)
     leaf_t, level_t = pl.pallas_call(
         leaf_kernel,
         out_shape=(whole, like((rank, count * rank), jnp.float32)),
         scratch_shapes=[pltpu.VMEM((rank * count, 2 * rank), jnp.float32)]
         + [pltpu.VMEM((count, rank, rank), jnp.float32)] * 3,
-        cost_estimate=pl.CostEstimate(
-            flops=8 * 1000 * 1000 * 1000, bytes_accessed=4 * 1024 * 1024, transcendentals=0
-        ),
+        cost_estimate=cost(4),
         compiler_params=params,
         name="leaf_level",
-    )(far, grams, samples, box_z)
+    )(far, factors, samples, box_z)
+    grouped, leaf_t, level_t = lax.optimization_barrier((grouped, leaf_t, level_t))
+    grouped = join([grouped, from_partner(grouped, "gx", 0)], 0)
     nested = pl.pallas_call(
         group_kernel,
         out_shape=whole,

time: 64.7 us -> 58.7 us (0.907)
  the two profiles are of different devices: /device:TPU:15 before, /device:TPU:0 now
where the time goes in v2:
time: 58.7 us; the launch traced here: 58.5 us
  Pallas kernels  32.3 us (55%)
  starting transfers between devices  18.6 us (32%)
  waiting for transfers between devices  4.06 us (7%)
  local copies, waits for them, and re-layouts  2.46 us (4%)
  between operations  0.76 us (1%)
    ppermute x4, starting transfers between devices, from_partner(): lax.ppermute(x, axis, [(i, i ^ 1 << distance) for i in range(lax.axis_siz...  15.3 us
    pallas_call x2, Pallas kernels, add_stage(): pl.pallas_call(functools.partial(next_kernel, stage), out_shape=whole, in...  12 us
    pallas_call x1, Pallas kernels, body(): pl.pallas_call(functools.partial(last_kernel, stage), out_shape=(whole, s...  6.14 us
    pallas_call x1, Pallas kernels, body(): pl.pallas_call(group_kernel, out_shape=whole, scratch_shapes=[single_scra...  4.09 us
    pallas_call x1, Pallas kernels, body(): pl.pallas_call(functools.partial(first_kernel, stage), out_shape=whole, i...  3.77 us
    pallas_call x1, Pallas kernels, body(): pl.pallas_call(leaf_kernel, out_shape=(whole, like((rank, count * rank),...  3.52 us
    pallas_call x1, Pallas kernels, body(): pl.pallas_call(leaf_factors, out_shape=like((rank * count, 2 * rank), jnp...  2.71 us
    ppermute x4, waiting for transfers between devices, from_partner(): lax.ppermute(x, axis, [(i, i ^ 1 << distance) for i in range(lax.axis_siz...  2.33 us
  transfers between devices with their start and end apart: 8, of which 5 were waited for; matrix products, arithmetic and copies ran while one was open for 1% of the time, Pallas kernels for 38%

profile of v2, /device:TPU:0, one launch (start us, length us, event | category | flops | bytes accessed | tf_op | source)
XLA Modules:
  0.0 58.5 jit_solution(14325006494345300771)
XLA Ops:
  0.6 0.7 %copy.7 = bf16[2,2,2,3,128]{4,3,2,1,0:T(4,128)(2,1)S(1)} copy(bf16[2,2,2,3,128]{4,2,3,1,0:T(2,128)(2,1)} %param.6) | data formatting | bytes 12288 | tf_op args[2]
  1.3 0.0 copy-start.1
  1.3 1.0 %copy-done.1 = bf16[2,2,2,64,384]{4,3,2,1,0:T(8,128)(2,1)S(1)} copy-done((bf16[2,2,2,64,384]{4,3,2,1,0:T(8,128)(2,1)S(1)}, bf16[2,2,2,64,384]{4,3,2,1,0:T(8,128)(2,1)}, u32[]{:S(2)}) %copy-start.1) | copy-done | bytes 393240
  2.3 0.1 pack.1
  2.4 3.0 %collective-permute-start = (bf16[4,208,128]{2,1,0:T(8,128)(2,1)S(1)}, bf16[4,208,128]{2,1,0:T(8,128)(2,1)S(1)}, u32[]{:S(2)}, u32[]{:S(2)}) collective-permute-start(bf16[4,208,128]{2,1,0:T(8,128)(2,1)S(1)} %get-tuple-element.24), channel_id=1, source_target_pairs={{0,1},{1,0},{2,3},{3,2},{4,5},{5,4},{6,7},{7,6},{8,9},{9,8},{10,11... | collective-permute-start | bytes 638984 | tf_op jit(solution)/shard_map/ppermute | solution.py:18
  5.5 0.8 %reshape.50.near = s32[216]{0:T(256)S(1)} reshape(s32[2,2,2,27]{3,2,1,0:T(2,128)} %param.7) | data formatting | bytes 1728 | tf_op jit(solution)/shard_map/reshape | solution.py:563
  6.2 3.8 %near_inner.1.before = f32[8,64,384]{2,1,0:T(8,128)S(1)} custom-call(s32[216]{0:T(256)S(1)} %reshape.50.near, f32[8,8,128]{2,1,0:T(8,128)S(1)} %get-tuple-element.22.own, bf16[8,208,128]{2,1,0:T(8,128)(2,1)S(1)} %get-tuple-element.23.own_blocks.rest_0_), custom_call_target="tpu_custom_call" | custom-call | flops 4000000000 | bytes 4194304 | tf_op jit(solution)/shard_map/near_inner/pallas_call | solution.py:596
  10.0 0.7 %collective-permute-done.rest_1_ = bf16[4,208,128]{2,1,0:T(8,128)(2,1)S(1)} collective-permute-done((bf16[4,208,128]{2,1,0:T(8,128)(2,1)S(1)}, bf16[4,208,128]{2,1,0:T(8,128)(2,1)S(1)}, u32[]{:S(2)}, u32[]{:S(2)}) %collective-permute-start) | collective-permute-done | bytes 213024 | tf_op jit(solution)/shard_map/ppermute | solution.py:18
  10.8 1.9 %collective-permute-start.1 = (bf16[2,3,208,128]{3,2,1,0:T(8,128)(2,1)S(1)}, bf16[2,3,208,128]{3,2,1,0:T(8,128)(2,1)S(1)}, u32[]{:S(2)}, u32[]{:S(2)}) collective-permute-start(bf16[2,3,208,128]{3,2,1,0:T(8,128)(2,1)S(1)} %get-tuple-element.43), channel_id=1, source_target_pairs={{0,2},{2,0},{4,6},{6,4},{1,3},{3,1},{5,7},{7,5},{8,10},{10,8},{12,... | collective-permute-start | bytes 958472 | tf_op jit(solution)/shard_map/ppermute | solution.py:197
  12.7 0.7 %collective-permute-start.2 = (bf16[2,3,208,128]{3,2,1,0:T(8,128)(2,1)S(1)}, bf16[2,3,208,128]{3,2,1,0:T(8,128)(2,1)S(1)}, u32[]{:S(2)}, u32[]{:S(2)}) collective-permute-start(bf16[2,3,208,128]{3,2,1,0:T(8,128)(2,1)S(1)} %get-tuple-element.44), channel_id=1, source_target_pairs={{2,4},{4,2},{3,5},{5,3},{10,12},{12,10},{11,13},{13,11},{18,20},{2... | collective-permute-start | bytes 958472 | tf_op jit(solution)/shard_map/ppermute | solution.py:201
  13.3 5.9 %near_inner_and_z.1.before = f32[8,64,384]{2,1,0:T(8,128)S(1)} custom-call(s32[216]{0:T(256)S(1)} %reshape.50.near, f32[8,8,128]{2,1,0:T(8,128)S(1)} %get-tuple-element.22.own, f32[8,64,384]{2,1,0:T(8,128)S(1)} %near_inner.1.before, bf16[8,208,128]{2,1,0:T(8,128)(2,1)S(1)} %get-tuple-element.23.own_blocks.rest_0_, ...), custom_call_target="tpu_custom_call" | custom-call | flops 5000000000 | bytes 4194304 | tf_op jit(solution)/shard_map/near_inner_and_z/pallas_call | solution.py:610
  19.2 0.4 collective-permute-done.1
  19.6 0.0 collective-permute-done.2
  19.6 0.1 pad_maximum_fusion
  19.7 0.1 select_bitcast_fusion
  19.8 0.1 collective-permute-start.3
  19.9 0.7 %collective-permute-start.4 = (bf16[4,3,208,128]{3,2,1,0:T(8,128)(2,1)S(1)}, bf16[4,3,208,128]{3,2,1,0:T(8,128)(2,1)S(1)}, u32[]{:S(2)}, u32[]{:S(2)}) collective-permute-start(bf16[4,3,208,128]{3,2,1,0:T(8,128)(2,1)S(1)} %get-tuple-element.41), channel_id=1, source_target_pairs={{8,16},{16,8},{9,17},{17,9},{10,18},{18,10},{11,19},{19,11},{12,20... | collective-permute-start | bytes 1916936 | tf_op jit(solution)/shard_map/ppermute | solution.py:201
  20.6 1.4 %collective-permute-done.3 = bf16[4,3,208,128]{3,2,1,0:T(8,128)(2,1)S(1)} collective-permute-done((bf16[4,3,208,128]{3,2,1,0:T(8,128)(2,1)S(1)}, bf16[4,3,208,128]{3,2,1,0:T(8,128)(2,1)S(1)}, u32[]{:S(2)}, u32[]{:S(2)}) %collective-permute-start.3) | collective-permute-done | bytes 639008 | tf_op jit(solution)/shard_map/ppermute | solution.py:197
  21.9 0.0 copy-start
  21.9 6.1 %near_y_and_x.1.before = f32[8,64,384]{2,1,0:T(8,128)S(1)} custom-call(s32[216]{0:T(256)S(1)} %reshape.50.near, f32[8,8,128]{2,1,0:T(8,128)S(1)} %get-tuple-element.22.own, f32[8,64,384]{2,1,0:T(8,128)S(1)} %near_inner_and_z.1.before, bf16[6,208,128]{2,1,0:T(8,128)(2,1)S(1)} %bitcast.30, bf16[6,208,128]{2,1,0:T(8,128)(2,1)S(1)} %bitcast.32, ...), custom_call_target="tpu_custom_call" | custom-call | flops 7000000000 | bytes 4194304 | tf_op jit(solution)/shard_map/near_y_and_x/pallas_call | solution.py:610
  28.1 0.0 collective-permute-done.4
  28.1 0.0 copy-done
  28.1 6.1 %near_x_and_box_level.1 = (f32[8,64,384]{2,1,0:T(8,128)S(1)}, f32[8,64,64]{2,1,0:T(8,128)S(1)}, f32[64,64]{1,0:T(8,128)S(1)}, f32[8,64,384]{2,1,0:T(8,128)S(1)}, f32[64,64]{1,0:T(8,128)S(1)}) custom-call(s32[216]{0:T(256)S(1)} %reshape.50.near, f32[8,8,128]{2,1,0:T(8,128)S(1)} %get-tuple-element.22.own, f32[8,64,384]{2,1,0:T(8,128)S(1)} %near_y_and_x.1.before, ...), custom_call_target="tpu_custom_call" | custom-call | tf_op jit(solution)/shard_map/near_x_and_box_level/pallas_call | solution.py:629
  34.2 0.6 %collective-permute-start.5 = (f32[1,64,64]{2,1,0:T(8,128)S(1)}, f32[1,64,64]{2,1,0:T(8,128)S(1)}, u32[]{:S(2)}, u32[]{:S(2)}) collective-permute-start(f32[1,64,64]{2,1,0:T(8,128)S(1)} %bitcast.35), channel_id=1, source_target_pairs={{0,1},{1,0},{2,3},{3,2},{4,5},{5,4},{6,7},{7,6},{8,9},{9,8},{10,11... | collective-permute-start | bytes 49160 | tf_op jit(solution)/shard_map/ppermute | solution.py:18
  34.9 2.7 %leaf_factors.1.factors = f32[512,128]{1,0:T(8,128)S(1)} custom-call(f32[8,64,64]{2,1,0:T(8,128)S(1)} %get-tuple-element.30.grams), custom_call_target="tpu_custom_call" | custom-call | flops 3000000000 | bytes 4194304 | tf_op jit(solution)/shard_map/leaf_factors/pallas_call | solution.py:639
  37.6 0.6 %collective-permute-done.5 = f32[1,64,64]{2,1,0:T(8,128)S(1)} collective-permute-done((f32[1,64,64]{2,1,0:T(8,128)S(1)}, f32[1,64,64]{2,1,0:T(8,128)S(1)}, u32[]{:S(2)}, u32[]{:S(2)}) %collective-permute-start.5) | collective-permute-done | bytes 16416 | tf_op jit(solution)/shard_map/ppermute | solution.py:18
  38.2 6.5 %collective-permute-start.6 = (f32[2,64,64]{2,1,0:T(8,128)S(1)}, f32[2,64,64]{2,1,0:T(8,128)S(1)}, u32[]{:S(2)}, u32[]{:S(2)}) collective-permute-start(f32[2,64,64]{2,1,0:T(8,128)S(1)} %pad_maximum_fusion.4), channel_id=1, source_target_pairs={{0,2},{2,0},{4,6},{6,4},{1,3},{3,1},{5,7},{7,5},{8,10},{10,8},{12,... | collective-permute-start | bytes 98312 | tf_op jit(solution)/shard_map/ppermute | solution.py:18
  44.7 3.5 %leaf_level.1 = (f32[8,64,384]{2,1,0:T(8,128)}, f32[64,512]{1,0:T(8,128)}) custom-call(f32[8,64,384]{2,1,0:T(8,128)S(1)} %get-tuple-element.32.far, f32[512,128]{1,0:T(8,128)S(1)} %leaf_factors.1.factors, f32[8,64,384]{2,1,0:T(8,128)S(1)} %get-tuple-element.34.samples, f32[64,64]{1,0:T(8,128)S(1)} %get-tuple-element.35.box_z), custom_call_target="tpu_custom_call" | custom-call | flops 4000000000 | bytes 4194304 | tf_op jit(solution)/shard_map/leaf_level/pallas_call | solution.py:648
  48.2 0.0 collective-permute-done.6
  48.3 5.1 %collective-permute-start.7 = (f32[4,64,64]{2,1,0:T(8,128)S(1)}, f32[4,64,64]{2,1,0:T(8,128)S(1)}, u32[]{:S(2)}, u32[]{:S(2)}) collective-permute-start(f32[4,64,64]{2,1,0:T(8,128)S(1)} %pad_maximum_fusion.3), channel_id=1, source_target_pairs={{0,8},{8,0},{16,24},{24,16},{1,9},{9,1},{17,25},{25,17},{2,10},{10... | collective-permute-start | bytes 196616 | tf_op jit(solution)/shard_map/ppermute | solution.py:18
  53.4 1.0 %collective-permute-done.7 = f32[4,64,64]{2,1,0:T(8,128)S(1)} collective-permute-done((f32[4,64,64]{2,1,0:T(8,128)S(1)}, f32[4,64,64]{2,1,0:T(8,128)S(1)}, u32[]{:S(2)}, u32[]{:S(2)}) %collective-permute-start.7) | collective-permute-done | bytes 65568 | tf_op jit(solution)/shard_map/ppermute | solution.py:18
  54.4 4.1 %group_level.1 = f32[8,64,384]{2,1,0:T(8,128)} custom-call(f32[8,64,64]{2,1,0:T(8,128)S(1)} %pad_maximum_fusion.2.factors, f32[8,64,384]{2,1,0:T(8,128)S(1)} %get-tuple-element.34.samples, f32[64,64]{1,0:T(8,128)S(1)} %get-tuple-element.35.box_z), custom_call_target="tpu_custom_call" | custom-call | tf_op jit(solution)/shard_map/group_level/pallas_call | solution.py:659
  (5 shorter events, 0.1 us)
Async XLA Ops:
  1.3 1.0 %copy-start.1 = (bf16[2,2,2,64,384]{4,3,2,1,0:T(8,128)(2,1)S(1)}, bf16[2,2,2,64,384]{4,3,2,1,0:T(8,128)(2,1)}, u32[]{:S(2)}) copy-start(bf16[2,2,2,64,384]{4,3,2,1,0:T(8,128)(2,1)} %param.5) | copy-start | bytes 1179652
  2.4 8.3 %collective-permute-start = (bf16[4,208,128]{2,1,0:T(8,128)(2,1)S(1)}, bf16[4,208,128]{2,1,0:T(8,128)(2,1)S(1)}, u32[]{:S(2)}, u32[]{:S(2)}) collective-permute-start(bf16[4,208,128]{2,1,0:T(8,128)(2,1)S(1)} %get-tuple-element.24), channel_id=1, source_target_pairs={{0,1},{1,0},{2,3},{3,2},{4,5},{5,4},{6,7},{7,6},{8,9},{9,8},{10,11... | collective-permute-start | bytes 638984 | tf_op jit(solution)/shard_map/ppermute | solution.py:18
  10.8 8.8 %collective-permute-start.1 = (bf16[2,3,208,128]{3,2,1,0:T(8,128)(2,1)S(1)}, bf16[2,3,208,128]{3,2,1,0:T(8,128)(2,1)S(1)}, u32[]{:S(2)}, u32[]{:S(2)}) collective-permute-start(bf16[2,3,208,128]{3,2,1,0:T(8,128)(2,1)S(1)} %get-tuple-element.43), channel_id=1, source_target_pairs={{0,2},{2,0},{4,6},{6,4},{1,3},{3,1},{5,7},{7,5},{8,10},{10,8},{12,... | collective-permute-start | bytes 958472 | tf_op jit(solution)/shard_map/ppermute | solution.py:197
  12.7 6.9 %collective-permute-start.2 = (bf16[2,3,208,128]{3,2,1,0:T(8,128)(2,1)S(1)}, bf16[2,3,208,128]{3,2,1,0:T(8,128)(2,1)S(1)}, u32[]{:S(2)}, u32[]{:S(2)}) collective-permute-start(bf16[2,3,208,128]{3,2,1,0:T(8,128)(2,1)S(1)} %get-tuple-element.44), channel_id=1, source_target_pairs={{2,4},{4,2},{3,5},{5,3},{10,12},{12,10},{11,13},{13,11},{18,20},{2... | collective-permute-start | bytes 958472 | tf_op jit(solution)/shard_map/ppermute | solution.py:201
  19.8 2.1 %collective-permute-start.3 = (bf16[4,3,208,128]{3,2,1,0:T(8,128)(2,1)S(1)}, bf16[4,3,208,128]{3,2,1,0:T(8,128)(2,1)S(1)}, u32[]{:S(2)}, u32[]{:S(2)}) collective-permute-start(bf16[4,3,208,128]{3,2,1,0:T(8,128)(2,1)S(1)} %get-tuple-element.42), channel_id=1, source_target_pairs={{0,8},{8,0},{16,24},{24,16},{1,9},{9,1},{17,25},{25,17},{2,10},{10... | collective-permute-start | bytes 1916936 | tf_op jit(solution)/shard_map/ppermute | solution.py:197
  19.9 8.2 %collective-permute-start.4 = (bf16[4,3,208,128]{3,2,1,0:T(8,128)(2,1)S(1)}, bf16[4,3,208,128]{3,2,1,0:T(8,128)(2,1)S(1)}, u32[]{:S(2)}, u32[]{:S(2)}) collective-permute-start(bf16[4,3,208,128]{3,2,1,0:T(8,128)(2,1)S(1)} %get-tuple-element.41), channel_id=1, source_target_pairs={{8,16},{16,8},{9,17},{17,9},{10,18},{18,10},{11,19},{19,11},{12,20... | collective-permute-start | bytes 1916936 | tf_op jit(solution)/shard_map/ppermute | solution.py:201
  21.9 6.2 %copy-start = (f32[2,2,2,64,384]{4,3,2,1,0:T(8,128)S(1)}, f32[2,2,2,64,384]{4,3,2,1,0:T(8,128)}, u32[]{:S(2)}) copy-start(f32[2,2,2,64,384]{4,3,2,1,0:T(8,128)} %param.4) | copy-start | bytes 2359300
  34.2 4.0 %collective-permute-start.5 = (f32[1,64,64]{2,1,0:T(8,128)S(1)}, f32[1,64,64]{2,1,0:T(8,128)S(1)}, u32[]{:S(2)}, u32[]{:S(2)}) collective-permute-start(f32[1,64,64]{2,1,0:T(8,128)S(1)} %bitcast.35), channel_id=1, source_target_pairs={{0,1},{1,0},{2,3},{3,2},{4,5},{5,4},{6,7},{7,6},{8,9},{9,8},{10,11... | collective-permute-start | bytes 49160 | tf_op jit(solution)/shard_map/ppermute | solution.py:18
  38.2 10.0 %collective-permute-start.6 = (f32[2,64,64]{2,1,0:T(8,128)S(1)}, f32[2,64,64]{2,1,0:T(8,128)S(1)}, u32[]{:S(2)}, u32[]{:S(2)}) collective-permute-start(f32[2,64,64]{2,1,0:T(8,128)S(1)} %pad_maximum_fusion.4), channel_id=1, source_target_pairs={{0,2},{2,0},{4,6},{6,4},{1,3},{3,1},{5,7},{7,5},{8,10},{10,8},{12,... | collective-permute-start | bytes 98312 | tf_op jit(solution)/shard_map/ppermute | solution.py:18
  48.3 6.1 %collective-permute-start.7 = (f32[4,64,64]{2,1,0:T(8,128)S(1)}, f32[4,64,64]{2,1,0:T(8,128)S(1)}, u32[]{:S(2)}, u32[]{:S(2)}) collective-permute-start(f32[4,64,64]{2,1,0:T(8,128)S(1)} %pad_maximum_fusion.3), channel_id=1, source_target_pairs={{0,8},{8,0},{16,24},{24,16},{1,9},{9,1},{17,25},{25,17},{2,10},{10... | collective-permute-start | bytes 196616 | tf_op jit(solution)/shard_map/ppermute | solution.py:18

commit v3 on v2

--- a/solution.py
+++ b/solution.py
@@ -211,25 +211,42 @@
 
 
 def pair_tables(halos):
-    depth = SIDE + halos[2]
-    stages = ([], [], [], [])
+    planes = halos[2]
+    tables = {}
     for a in range(SIDE**3):
         place = (a // 4, a // 2 % 2, a % 2)
         for k in range(27):
             at = [p + d for p, d in zip(place, (k // 9 - 1, k // 3 % 3 - 1, k % 3 - 1))]
-            sides = tuple((axis, t) for axis, t in enumerate(at) if t in (-1, 2))
-            x, y, z = (2 if t == -1 else t for t in at)
-            if at[0] == -1:
-                stages[3].append((a, k, y * depth + z, sides[1:], True))
-            elif at[0] == 2:
+            sides = tuple((axis, t) for axis, t in enumerate(at) if t in (-1, 2) and axis > 0)
+            key = tuple(t in (-1, 2) for t in at)
+            if at[0] == 2:
                 continue
-            elif y == 2:
-                stages[2].append((a, k, x * depth + z, sides, False))
-            elif z == 2:
-                stages[1].append((a, k, SIDE**3 + x * SIDE + y, sides, False))
-            else:
-                stages[a * 2 // SIDE**3].append((a, k, leaf_index(x, y, z), sides, False))
-    return stages
+            x, y, z = at
+            source = {
+                (False, False, False): leaf_index(x, y, z),
+                (False, False, True): x * SIDE + y,
+                (False, True, False): x * SIDE + z,
+                (False, True, True): x,
+                (True, False, False): y * SIDE + z,
+                (True, False, True): y,
+                (True, True, False): SIDE * planes + z,
+                (True, True, True): 0,
+            }[key]
+            tables.setdefault(key, []).append((a, k, source, sides))
+    return tables
+
+
+def side_steps(key, planes):
+    return {
+        (False, False, False): {},
+        (False, False, True): {2: SIDE * SIDE},
+        (False, True, False): {1: SIDE * SIDE},
+        (False, True, True): {1: SIDE * planes, 2: SIDE},
+        (True, False, False): {},
+        (True, False, True): {2: SIDE},
+        (True, True, False): {1: SIDE},
+        (True, True, True): {1: planes, 2: 1},
+    }[key]
 
 
 def far_sides(halos):
@@ -243,33 +260,26 @@
     return found
 
 
-def list_pairs(pairs, halos, near, listed, count, x_side):
-    found = far_sides(halos)
-    depth = SIDE + halos[2]
+def list_pairs(pairs, steps, first, found, near, listed, count, x_side):
     joint = {}
-    for a, k, source, sides, across in pairs:
-        key = (sides, across)
-        if key not in joint:
-            inside, moved, entry = jnp.int32(1), jnp.int32(0), jnp.int32(0)
-            if across:
-                steps = {1: depth, 2: 1}
-                inside = x_side[1]
-                entry = x_side[0] * (4 * 27 + 18)
-            elif any(axis == 1 for axis, _ in sides):
-                steps = {1: SIDE * depth, 2: 1}
-            else:
-                steps = {2: SIDE * SIDE}
+    entry = None
+    if x_side is not None:
+        entry = x_side[0] * (4 * 27 + 18)
+    for a, k, source, sides in pairs:
+        if sides not in joint:
+            inside, moved = jnp.int32(1), jnp.int32(0)
+            if x_side is not None:
+                inside, moved = x_side[1], entry
             for side in sides:
                 inside = inside * found[side][0]
-                moved = moved + found[side][1] * steps[side[0]]
-            joint[key] = (inside, moved * (8 * 27) + entry, entry)
-        inside, moved, entry = joint[key]
-        code = jnp.int32((source * 8 + a) * 27 + k)
-        if sides or across:
-            taken = near[a * 27 + k + entry] * inside
+                moved = moved + found[side][1] * (steps[side[0]] * 8 * 27)
+            joint[sides] = (inside, moved)
+        inside, moved = joint[sides]
+        code = jnp.int32(((first + source) * 8 + a) * 27 + k)
+        taken = near[a * 27 + k] if entry is None else near[a * 27 + k + entry]
+        if sides or entry is not None:
             code = code + moved
-        else:
-            taken = near[a * 27 + k]
+            taken = taken * inside
         listed[count] = code
         count = count + taken
     return count
@@ -367,11 +377,11 @@
 def near_stage(stage, near, own, parts, total, listed, blocks, turned, spread, semaphore):
     halos, lists = stage
     copies, count = fetch(parts, blocks, semaphore)
+    found = far_sides(halos)
     odd = lax.axis_index("gx") % 2
     size = lax.axis_size("gx")
     start = jnp.int32(0)
-    for pairs, first, within in lists:
-        pairs = [(a, k, source + first, sides, across) for a, k, source, sides, across in pairs]
+    for pairs, steps, first, within in lists:
         x_side = None
         if within is True:
             x_side = (1 - odd, jnp.int32(1))
@@ -379,7 +389,7 @@
             place = lax.axis_index("gx")
             inside = jnp.logical_and(place > 0, place < size - 1).astype(jnp.int32)
             x_side = (odd, inside)
-        start = list_pairs(pairs, halos, near, listed, start, x_side)
+        start = list_pairs(pairs, steps, first, found, near, listed, start, x_side)
     groups = close_list(listed, start, count)
     blocks[count] = jnp.zeros_like(blocks[count])
     for copy in copies:
@@ -428,13 +438,13 @@
 
 
 def near_scratch(stage, count, block):
-    length = sum(len(pairs) for pairs, _, _ in stage[1])
+    length = sum(len(pairs) for pairs, _, _, _ in stage[1])
     return [
         pltpu.SMEM((length + GROUP + 1,), jnp.int32),
         pltpu.VMEM((count + 1,) + block, jnp.bfloat16),
         pltpu.VMEM((128, 128), jnp.float32),
         pltpu.VMEM((count + 1, 3, 128, 128), jnp.float32),
-        pltpu.SemaphoreType.DMA((4,)),
+        pltpu.SemaphoreType.DMA((8,)),
     ]
 
 
@@ -562,51 +572,50 @@
     params = pltpu.CompilerParams(vmem_limit_bytes=VMEM_LIMIT)
     flat_near = near.reshape(count * 27)
     flat_sketch = sketch.reshape(count, rank, leaf_rows)
-    stages = pair_tables(halos)
-    faces = halos[2]
+    tables = pair_tables(halos)
+    planes = halos[2]
     packed, own, *sent = pl.pallas_call(
         pack_kernel,
         out_shape=(
             like((count,) + block, jnp.bfloat16),
             like((count, 8, 128), jnp.float32),
         )
-        + (like((SIDE * SIDE,) + block, jnp.bfloat16),) * faces,
+        + (like((SIDE * SIDE,) + block, jnp.bfloat16),) * planes,
         compiler_params=params,
         name="pack",
     )(test_matrix.reshape(count, rank, leaf_rows), offsets.reshape(count, 3, 128))
     z_halos = [from_partner(sent[0], "gz", 0)]
-    if faces == 2:
+    if planes == 2:
         size = lax.axis_size("gz")
         across = [(i, i + 1) for i in range(1, size - 1, 2)]
         across = across + [(j, i) for i, j in across]
         z_halos.append(lax.ppermute(sent[1], "gz", across))
     inner = packed.reshape((SIDE, SIDE, SIDE) + block)
-    columns = [h.reshape((SIDE, SIDE, 1) + block) for h in z_halos]
-    extended = join([inner] + columns, 2)
-    depth = extended.shape[2]
-    flat = lambda parts: [x.reshape((-1,) + block) for x in parts]
-    column = (SIDE + halos[1]) * depth
-    y_blocks = SIDE * depth * halos[1]
+    z_planes = join([h.reshape((1, SIDE, SIDE) + block) for h in z_halos], 0)
+    y_halos = to_neighbours(inner[:, 0], inner[:, 1], "gy")
+    x_halos = to_neighbours(inner[0], inner[1], "gx")
     whole = like((count, rank, leaf_rows), jnp.float32)
     squares = like((count, rank, rank), jnp.float32)
     square = like((rank, rank), jnp.float32)
     single_scratch = pltpu.VMEM((rank, 2 * rank), jnp.float32)
 
-    stage = (halos, [(stages[0], 0, None)])
-    total = pl.pallas_call(
-        functools.partial(first_kernel, stage),
-        out_shape=whole,
-        in_specs=[IN_SMEM, IN_VMEM, ANYWHERE],
-        scratch_shapes=near_scratch(stage, count, block),
-        cost_estimate=cost(4),
-        compiler_params=params,
-        name="near_inner",
-    )(flat_near, own, packed)
-
-    extended, total = lax.optimization_barrier((extended, total))
-    y_halos = to_neighbours(extended[:, 0], extended[:, 1], "gy")
-
-    def add_stage(stage, total, parts, name, time):
+    def blocks_of(parts):
+        return join([x.reshape((-1,) + block) for x in parts], 0)
+
+    def make_stage(entries):
+        lists, parts, first = [], [], 0
+        for key, arrays, within in entries:
+            lists.append((tables[key], side_steps(key, halos[2]), first, within))
+            if arrays is not None:
+                parts.extend(x.reshape((-1,) + block) for x in arrays)
+                first = sum(part.shape[0] for part in parts)
+        return (halos, lists), parts
+
+    def across_x(key, arrays):
+        return [(key, [x], i == 0) for i, x in enumerate(arrays)]
+
+    def add_stage(entries, total, name, time):
+        stage, parts = make_stage(entries)
         return pl.pallas_call(
             functools.partial(next_kernel, stage),
             out_shape=whole,
@@ -617,22 +626,39 @@
             name=name,
         )(flat_near, own, total, *parts)
 
-    stage = (halos, [(stages[1], 0, None)])
-    total = add_stage(stage, total, [packed] + flat(z_halos), "near_inner_and_z", 5)
-    wide = join([extended] + [h[:, None] for h in y_halos], 1)
-    wide, total = lax.optimization_barrier((wide, total))
-    x_halos = to_neighbours(wide[0], wide[1], "gx")
-    stage = (halos, [(stages[2], 0, None), (stages[3], y_blocks, True)])
-    total = add_stage(stage, total, flat(y_halos) + flat(x_halos[:1]), "near_y_and_x", 7)
-    stage = (halos, [(stages[3], 0, False)] if halos[0] == 2 else [])
-    parts = flat(x_halos[1:])
+    stage, parts = make_stage([((False, False, False), [packed], None)])
+    total = pl.pallas_call(
+        functools.partial(first_kernel, stage),
+        out_shape=whole,
+        in_specs=[IN_SMEM, IN_VMEM, ANYWHERE],
+        scratch_shapes=near_scratch(stage, count, block),
+        cost_estimate=cost(6),
+        compiler_params=params,
+        name="near_inner",
+    )(flat_near, own, packed)
+    z_planes, y_halos, total = lax.optimization_barrier((z_planes, y_halos, total))
+    zy_halos = to_neighbours(z_planes[:, :, 0], z_planes[:, :, 1], "gy")
+    faces = [blocks_of([z_planes[:, i]] + [h[i] for h in y_halos]) for i in range(SIDE)]
+    x_edges = to_neighbours(faces[0], faces[1], "gx")
+    entries = [((False, False, True), [z_planes], None), ((False, True, False), y_halos, None)]
+    entries += across_x((True, False, False), x_halos)
+    total = add_stage(entries, total, "near_faces", 7)
+    zy_halos, total = lax.optimization_barrier((zy_halos, total))
+    faces = [blocks_of([h[:, i] for h in zy_halos]) for i in range(SIDE)]
+    x_corners = to_neighbours(faces[0], faces[1], "gx")
+    entries = [((False, True, True), zy_halos, None)]
+    for i, x in enumerate(x_edges):
+        entries += [((True, False, True), None, i == 0), ((True, True, False), [x], i == 0)]
+    total = add_stage(entries, total, "near_edges", 4)
+    stage, parts = make_stage(across_x((True, True, True), x_corners))
+    sources = sum(part.shape[0] for part in parts)
     far, grams, factor, samples, box_z = pl.pallas_call(
         functools.partial(last_kernel, stage),
         out_shape=(whole, squares, square, whole, square),
         in_specs=[IN_SMEM, IN_VMEM, IN_VMEM, IN_VMEM] + [ANYWHERE] * len(parts),
-        scratch_shapes=near_scratch(stage, column * len(parts), block) + [single_scratch],
+        scratch_shapes=near_scratch(stage, sources, block) + [single_scratch],
         compiler_params=params,
-        name="near_x_and_box_level",
+        name="near_corners_and_box_level",
     )(flat_near, own, total, flat_sketch, *parts)
     grouped = factor[None]
     grouped = join([grouped, from_partner(grouped, "gz", 0)], 0)

time: 58.7 us -> 63.4 us (1.080); the launches traced: 58.5 us -> 62.5 us
  starting transfers between devices: 18.6 us -> 25.5 us
  waiting for transfers between devices: 4.06 us -> 1.51 us
    ppermute x2 -> x5, starting transfers between devices: 1.93 us -> 15.7 us  [to_neighbours(): received = [lax.ppermute(jnp.where(even, high, low), axis, pairs)]]
    ppermute x4, starting transfers between devices: 15.3 us -> 6.49 us  [from_partner(): lax.ppermute(x, axis, [(i, i ^ 1 << distance) for i in range(lax.axis_siz...]
    pallas_call x2, Pallas kernels: 12 us -> 9.76 us  [add_stage(): pl.pallas_call(functools.partial(next_kernel, stage), out_shape=whole, in...]
    ppermute x2 -> x5, starting transfers between devices: 1.37 us -> 3.36 us  [to_neighbours(): received.insert(0, lax.ppermute(jnp.where(even, low, high), axis, across))]
    pallas_call x1, Pallas kernels: 3.77 us -> 5.54 us  [body(): pl.pallas_call(functools.partial(first_kernel, stage), out_shape=whole, i...]
    ppermute x2 -> x5, waiting for transfers between devices: 1.72 us -> 0.01 us  [to_neighbours(): received = [lax.ppermute(jnp.where(even, high, low), axis, pairs)]]
    ppermute x4, waiting for transfers between devices: 2.33 us -> 1.49 us  [from_partner(): lax.ppermute(x, axis, [(i, i ^ 1 << distance) for i in range(lax.axis_siz...]
    reshape x1, local copies, waits for them, and re-layouts: 0.77 us -> 0.08 us  [body(): flat_near = near.reshape(count * 27)]
  transfers between devices with their start and end apart: 8 -> 14, of which waited for: 5 -> 2; matrix products, arithmetic and copies ran while one was open for 1% -> 1% of each run, Pallas kernels for 38% -> 34%
where the time goes in v3:
time: 63.4 us; the launch traced here: 62.5 us
  Pallas kernels  32.5 us (51%)
  starting transfers between devices  25.5 us (40%)
  local copies, waits for them, and re-layouts  1.85 us (3%)
  waiting for transfers between devices  1.51 us (2%)
  between operations  0.88 us (1%)
    ppermute x5, starting transfers between devices, to_neighbours(): received = [lax.ppermute(jnp.where(even, high, low), axis, pairs)]  15.7 us
    pallas_call x2, Pallas kernels, add_stage(): pl.pallas_call(functools.partial(next_kernel, stage), out_shape=whole, in...  9.76 us
    pallas_call x1, Pallas kernels, body(): pl.pallas_call(functools.partial(last_kernel, stage), out_shape=(whole, s...  6.79 us
    ppermute x4, starting transfers between devices, from_partner(): lax.ppermute(x, axis, [(i, i ^ 1 << distance) for i in range(lax.axis_siz...  6.49 us
    pallas_call x1, Pallas kernels, body(): pl.pallas_call(functools.partial(first_kernel, stage), out_shape=whole, i...  5.54 us
    pallas_call x1, Pallas kernels, body(): pl.pallas_call(group_kernel, out_shape=whole, scratch_shapes=[single_scra...  4.09 us
    pallas_call x1, Pallas kernels, body(): pl.pallas_call(leaf_kernel, out_shape=(whole, like((rank, count * rank),...  3.52 us
    ppermute x5, starting transfers between devices, to_neighbours(): received.insert(0, lax.ppermute(jnp.where(even, low, high), axis, across))  3.36 us
  transfers between devices with their start and end apart: 14, of which 2 were waited for; matrix products, arithmetic and copies ran while one was open for 1% of the time, Pallas kernels for 34%

profile of v3, /device:TPU:0, one launch (start us, length us, event | category | flops | bytes accessed | tf_op | source)
XLA Modules:
  0.0 62.5 jit_solution(13269364596764979599)
XLA Ops:
  0.6 0.7 %copy.9 = bf16[2,2,2,3,128]{4,3,2,1,0:T(4,128)(2,1)S(1)} copy(bf16[2,2,2,3,128]{4,2,3,1,0:T(2,128)(2,1)} %param.6) | data formatting | bytes 12288 | tf_op args[2]
  1.3 0.0 copy-start.1
  1.3 1.0 %copy-done.1 = bf16[2,2,2,64,384]{4,3,2,1,0:T(8,128)(2,1)S(1)} copy-done((bf16[2,2,2,64,384]{4,3,2,1,0:T(8,128)(2,1)S(1)}, bf16[2,2,2,64,384]{4,3,2,1,0:T(8,128)(2,1)}, u32[]{:S(2)}) %copy-start.1) | copy-done | bytes 393240
  2.3 0.1 pack.1
  2.4 3.0 %collective-permute-start = (bf16[4,208,128]{2,1,0:T(8,128)(2,1)S(1)}, bf16[4,208,128]{2,1,0:T(8,128)(2,1)S(1)}, u32[]{:S(2)}, u32[]{:S(2)}) collective-permute-start(bf16[4,208,128]{2,1,0:T(8,128)(2,1)S(1)} %get-tuple-element.26), channel_id=1, source_target_pairs={{0,1},{1,0},{2,3},{3,2},{4,5},{5,4},{6,7},{7,6},{8,9},{9,8},{10,11... | collective-permute-start | bytes 638984 | tf_op jit(solution)/shard_map/ppermute | solution.py:18
  5.5 0.7 %collective-permute-start.2 = (bf16[2,2,208,128]{3,2,1,0:T(8,128)(2,1)S(1)}, bf16[2,2,208,128]{3,2,1,0:T(8,128)(2,1)S(1)}, u32[]{:S(2)}, u32[]{:S(2)}) collective-permute-start(bf16[2,2,208,128]{3,2,1,0:T(8,128)(2,1)S(1)} %get-tuple-element.51), channel_id=1, source_target_pairs={{2,4},{4,2},{3,5},{5,3},{10,12},{12,10},{11,13},{13,11},{18,20},{2... | collective-permute-start | bytes 638984 | tf_op jit(solution)/shard_map/ppermute | solution.py:201
  6.2 4.5 %collective-permute-start.1 = (bf16[2,2,208,128]{3,2,1,0:T(8,128)(2,1)S(1)}, bf16[2,2,208,128]{3,2,1,0:T(8,128)(2,1)S(1)}, u32[]{:S(2)}, u32[]{:S(2)}) collective-permute-start(bf16[2,2,208,128]{3,2,1,0:T(8,128)(2,1)S(1)} %get-tuple-element.52), channel_id=1, source_target_pairs={{0,2},{2,0},{4,6},{6,4},{1,3},{3,1},{5,7},{7,5},{8,10},{10,8},{12,... | collective-permute-start | bytes 638984 | tf_op jit(solution)/shard_map/ppermute | solution.py:197
  10.7 0.0 copy-start.2
  10.7 0.1 collective-permute-start.5
  10.8 0.7 %collective-permute-start.6 = (bf16[2,2,208,128]{3,2,1,0:T(8,128)(2,1)S(1)}, bf16[2,2,208,128]{3,2,1,0:T(8,128)(2,1)S(1)}, u32[]{:S(2)}, u32[]{:S(2)}) collective-permute-start(bf16[2,2,208,128]{3,2,1,0:T(8,128)(2,1)S(1)} %bitcast.73), channel_id=1, source_target_pairs={{8,16},{16,8},{9,17},{17,9},{10,18},{18,10},{11,19},{19,11},{12,20... | collective-permute-start | bytes 638984 | tf_op jit(solution)/shard_map/ppermute | solution.py:201
  11.4 0.0 copy-done.2
  11.4 0.1 reshape.107.near
  11.5 5.5 %near_inner.1.before = f32[8,64,384]{2,1,0:T(8,128)S(1)} custom-call(s32[216]{0:T(256)S(1)} %reshape.107.near, f32[8,8,128]{2,1,0:T(8,128)S(1)} %get-tuple-element.25.own, bf16[8,208,128]{2,1,0:T(8,128)(2,1)S(1)} %get-tuple-element.27.own_blocks), custom_call_target="tpu_custom_call" | custom-call | flops 6000000000 | bytes 4194304 | tf_op jit(solution)/shard_map/near_inner/pallas_call | solution.py:630
  17.1 0.0 collective-permute-done
  17.1 0.0 collective-permute-done.2
  17.1 0.0 collective-permute-done.1
  17.2 0.7 %collective-permute-start.4 = (bf16[1,2,208,128]{3,2,1,0:T(8,128)(2,1)S(1)}, bf16[1,2,208,128]{3,2,1,0:T(8,128)(2,1)S(1)}, u32[]{:S(2)}, u32[]{:S(2)}) collective-permute-start(bf16[1,2,208,128]{3,2,1,0:T(8,128)(2,1)S(1)} %get-tuple-element.61), channel_id=1, source_target_pairs={{2,4},{4,2},{3,5},{5,3},{10,12},{12,10},{11,13},{13,11},{18,20},{2... | collective-permute-start | bytes 319496 | tf_op jit(solution)/shard_map/ppermute | solution.py:201
  17.8 3.0 %collective-permute-start.3 = (bf16[1,2,208,128]{3,2,1,0:T(8,128)(2,1)S(1)}, bf16[1,2,208,128]{3,2,1,0:T(8,128)(2,1)S(1)}, u32[]{:S(2)}, u32[]{:S(2)}) collective-permute-start(bf16[1,2,208,128]{3,2,1,0:T(8,128)(2,1)S(1)} %get-tuple-element.62), channel_id=1, source_target_pairs={{0,2},{2,0},{4,6},{6,4},{1,3},{3,1},{5,7},{7,5},{8,10},{10,8},{12,... | collective-permute-start | bytes 319496 | tf_op jit(solution)/shard_map/ppermute | solution.py:197
  20.9 0.1 broadcast_select_fusion
  20.9 0.7 %collective-permute-start.8 = (bf16[6,208,128]{2,1,0:T(8,128)(2,1)S(1)}, bf16[6,208,128]{2,1,0:T(8,128)(2,1)S(1)}, u32[]{:S(2)}, u32[]{:S(2)}) collective-permute-start(bf16[6,208,128]{2,1,0:T(8,128)(2,1)S(1)} %get-tuple-element.47), channel_id=1, source_target_pairs={{8,16},{16,8},{9,17},{17,9},{10,18},{18,10},{11,19},{19,11},{12,20... | collective-permute-start | bytes 958472 | tf_op jit(solution)/shard_map/ppermute | solution.py:201
  21.6 0.0 collective-permute-done.5
  21.6 5.2 %collective-permute-start.7 = (bf16[6,208,128]{2,1,0:T(8,128)(2,1)S(1)}, bf16[6,208,128]{2,1,0:T(8,128)(2,1)S(1)}, u32[]{:S(2)}, u32[]{:S(2)}) collective-permute-start(bf16[6,208,128]{2,1,0:T(8,128)(2,1)S(1)} %get-tuple-element.48), channel_id=1, source_target_pairs={{0,8},{8,0},{16,24},{24,16},{1,9},{9,1},{17,25},{25,17},{2,10},{10... | collective-permute-start | bytes 958472 | tf_op jit(solution)/shard_map/ppermute | solution.py:197
  26.8 0.0 collective-permute-done.6
  26.9 7.1 %near_faces.1.before = f32[8,64,384]{2,1,0:T(8,128)S(1)} custom-call(s32[216]{0:T(256)S(1)} %reshape.107.near, f32[8,8,128]{2,1,0:T(8,128)S(1)} %get-tuple-element.25.own, f32[8,64,384]{2,1,0:T(8,128)S(1)} %near_inner.1.before, bf16[4,208,128]{2,1,0:T(8,128)(2,1)S(1)} %collective-permute-done, bf16[4,208,128]{2,1,0:T(8,128)(2,1)S(1)} %bitcast.64, ...), custom_call_target="tpu_custom_call" | custom-call | flops 7000000000 | bytes 4194304 | tf_op jit(solution)/shard_map/near_faces/pallas_call | solution.py:619
  33.9 0.0 collective-permute-done.4
  33.9 0.0 collective-permute-done.3
  34.0 0.7 %collective-permute-start.10 = (bf16[2,208,128]{2,1,0:T(8,128)(2,1)S(1)}, bf16[2,208,128]{2,1,0:T(8,128)(2,1)S(1)}, u32[]{:S(2)}, u32[]{:S(2)}) collective-permute-start(bf16[2,208,128]{2,1,0:T(8,128)(2,1)S(1)} %get-tuple-element.53), channel_id=1, source_target_pairs={{8,16},{16,8},{9,17},{17,9},{10,18},{18,10},{11,19},{19,11},{12,20... | collective-permute-start | bytes 319496 | tf_op jit(solution)/shard_map/ppermute | solution.py:201
  34.7 3.0 %collective-permute-start.9 = (bf16[2,208,128]{2,1,0:T(8,128)(2,1)S(1)}, bf16[2,208,128]{2,1,0:T(8,128)(2,1)S(1)}, u32[]{:S(2)}, u32[]{:S(2)}) collective-permute-start(bf16[2,208,128]{2,1,0:T(8,128)(2,1)S(1)} %get-tuple-element.54), channel_id=1, source_target_pairs={{0,8},{8,0},{16,24},{24,16},{1,9},{9,1},{17,25},{25,17},{2,10},{10... | collective-permute-start | bytes 319496 | tf_op jit(solution)/shard_map/ppermute | solution.py:197
  37.6 0.0 collective-permute-done.8.rest_3_
  37.6 0.0 collective-permute-done.7.rest_2_
  37.7 0.0 copy-start
  37.7 2.7 %near_edges.1.before = f32[8,64,384]{2,1,0:T(8,128)S(1)} custom-call(s32[216]{0:T(256)S(1)} %reshape.107.near, f32[8,8,128]{2,1,0:T(8,128)S(1)} %get-tuple-element.25.own, f32[8,64,384]{2,1,0:T(8,128)S(1)} %near_faces.1.before, bf16[2,208,128]{2,1,0:T(8,128)(2,1)S(1)} %bitcast.66, bf16[2,208,128]{2,1,0:T(8,128)(2,1)S(1)} %bitcast.65, ...), custom_call_target="tpu_custom_call" | custom-call | flops 4000000000 | bytes 4194304 | tf_op jit(solution)/shard_map/near_edges/pallas_call | solution.py:619
  40.4 0.0 collective-permute-done.10.rest_1_
  40.4 0.0 collective-permute-done.9.rest_0_
  40.4 0.0 copy-done
  40.4 6.8 %near_corners_and_box_level.1 = (f32[8,64,384]{2,1,0:T(8,128)S(1)}, f32[8,64,64]{2,1,0:T(8,128)S(1)}, f32[64,64]{1,0:T(8,128)S(1)}, f32[8,64,384]{2,1,0:T(8,128)S(1)}, f32[64,64]{1,0:T(8,128)S(1)}) custom-call(s32[216]{0:T(256)S(1)} %reshape.107.near, f32[8,8,128]{2,1,0:T(8,128)S(1)} %get-tuple-element.25.own, f32[8,64,384]{2,1,0:T(8,128)S(1)} %near_edges.1.before, ...), custom_call_target="tpu_custom_call" | custom-call | tf_op jit(solution)/shard_map/near_corners_and_box_level/pallas_call | solution.py:655
  47.2 1.2 %collective-permute-start.11 = (f32[1,64,64]{2,1,0:T(8,128)S(1)}, f32[1,64,64]{2,1,0:T(8,128)S(1)}, u32[]{:S(2)}, u32[]{:S(2)}) collective-permute-start(f32[1,64,64]{2,1,0:T(8,128)S(1)} %bitcast.68), channel_id=1, source_target_pairs={{0,1},{1,0},{2,3},{3,2},{4,5},{5,4},{6,7},{7,6},{8,9},{9,8},{10,11... | collective-permute-start | bytes 49160 | tf_op jit(solution)/shard_map/ppermute | solution.py:18
  48.4 2.7 %leaf_factors.1.factors = f32[512,128]{1,0:T(8,128)S(1)} custom-call(f32[8,64,64]{2,1,0:T(8,128)S(1)} %get-tuple-element.36.grams), custom_call_target="tpu_custom_call" | custom-call | flops 3000000000 | bytes 4194304 | tf_op jit(solution)/shard_map/leaf_factors/pallas_call | solution.py:665
  51.1 0.1 collective-permute-done.11
  51.2 2.2 %collective-permute-start.12 = (f32[2,64,64]{2,1,0:T(8,128)S(1)}, f32[2,64,64]{2,1,0:T(8,128)S(1)}, u32[]{:S(2)}, u32[]{:S(2)}) collective-permute-start(f32[2,64,64]{2,1,0:T(8,128)S(1)} %pad_maximum_fusion.6), channel_id=1, source_target_pairs={{0,2},{2,0},{4,6},{6,4},{1,3},{3,1},{5,7},{7,5},{8,10},{10,8},{12,... | collective-permute-start | bytes 98312 | tf_op jit(solution)/shard_map/ppermute | solution.py:18
  53.5 3.5 %leaf_level.1 = (f32[8,64,384]{2,1,0:T(8,128)}, f32[64,512]{1,0:T(8,128)}) custom-call(f32[8,64,384]{2,1,0:T(8,128)S(1)} %get-tuple-element.38.far, f32[512,128]{1,0:T(8,128)S(1)} %leaf_factors.1.factors, f32[8,64,384]{2,1,0:T(8,128)S(1)} %get-tuple-element.40.samples, f32[64,64]{1,0:T(8,128)S(1)} %get-tuple-element.41.box_z), custom_call_target="tpu_custom_call" | custom-call | flops 4000000000 | bytes 4194304 | tf_op jit(solution)/shard_map/leaf_level/pallas_call | solution.py:674
  57.0 0.0 collective-permute-done.12
  57.0 0.1 collective-permute-start.13
  57.1 1.3 %collective-permute-done.13 = f32[4,64,64]{2,1,0:T(8,128)S(1)} collective-permute-done((f32[4,64,64]{2,1,0:T(8,128)S(1)}, f32[4,64,64]{2,1,0:T(8,128)S(1)}, u32[]{:S(2)}, u32[]{:S(2)}) %collective-permute-start.13) | collective-permute-done | bytes 65568 | tf_op jit(solution)/shard_map/ppermute | solution.py:18
  58.4 4.1 %group_level.1 = f32[8,64,384]{2,1,0:T(8,128)} custom-call(f32[8,64,64]{2,1,0:T(8,128)S(1)} %pad_maximum_fusion.2.factors, f32[8,64,384]{2,1,0:T(8,128)S(1)} %get-tuple-element.40.samples, f32[64,64]{1,0:T(8,128)S(1)} %get-tuple-element.41.box_z), custom_call_target="tpu_custom_call" | custom-call | tf_op jit(solution)/shard_map/group_level/pallas_call | solution.py:685
  (10 shorter events, 0.2 us)
Async XLA Ops:
  1.3 1.0 %copy-start.1 = (bf16[2,2,2,64,384]{4,3,2,1,0:T(8,128)(2,1)S(1)}, bf16[2,2,2,64,384]{4,3,2,1,0:T(8,128)(2,1)}, u32[]{:S(2)}) copy-start(bf16[2,2,2,64,384]{4,3,2,1,0:T(8,128)(2,1)} %param.5) | copy-start | bytes 1179652
  2.4 14.7 %collective-permute-start = (bf16[4,208,128]{2,1,0:T(8,128)(2,1)S(1)}, bf16[4,208,128]{2,1,0:T(8,128)(2,1)S(1)}, u32[]{:S(2)}, u32[]{:S(2)}) collective-permute-start(bf16[4,208,128]{2,1,0:T(8,128)(2,1)S(1)} %get-tuple-element.26), channel_id=1, source_target_pairs={{0,1},{1,0},{2,3},{3,2},{4,5},{5,4},{6,7},{7,6},{8,9},{9,8},{10,11... | collective-permute-start | bytes 638984 | tf_op jit(solution)/shard_map/ppermute | solution.py:18
  5.5 11.6 %collective-permute-start.2 = (bf16[2,2,208,128]{3,2,1,0:T(8,128)(2,1)S(1)}, bf16[2,2,208,128]{3,2,1,0:T(8,128)(2,1)S(1)}, u32[]{:S(2)}, u32[]{:S(2)}) collective-permute-start(bf16[2,2,208,128]{3,2,1,0:T(8,128)(2,1)S(1)} %get-tuple-element.51), channel_id=1, source_target_pairs={{2,4},{4,2},{3,5},{5,3},{10,12},{12,10},{11,13},{13,11},{18,20},{2... | collective-permute-start | bytes 638984 | tf_op jit(solution)/shard_map/ppermute | solution.py:201
  6.2 10.9 %collective-permute-start.1 = (bf16[2,2,208,128]{3,2,1,0:T(8,128)(2,1)S(1)}, bf16[2,2,208,128]{3,2,1,0:T(8,128)(2,1)S(1)}, u32[]{:S(2)}, u32[]{:S(2)}) collective-permute-start(bf16[2,2,208,128]{3,2,1,0:T(8,128)(2,1)S(1)} %get-tuple-element.52), channel_id=1, source_target_pairs={{0,2},{2,0},{4,6},{6,4},{1,3},{3,1},{5,7},{7,5},{8,10},{10,8},{12,... | collective-permute-start | bytes 638984 | tf_op jit(solution)/shard_map/ppermute | solution.py:197
  10.7 0.8 %copy-start.2 = (s32[2,2,2,27]{3,2,1,0:T(2,128)S(1)}, s32[2,2,2,27]{3,2,1,0:T(2,128)}, u32[]{:S(2)}) copy-start(s32[2,2,2,27]{3,2,1,0:T(2,128)} %param.7) | copy-start | bytes 2596
  10.7 11.0 %collective-permute-start.5 = (bf16[2,2,208,128]{3,2,1,0:T(8,128)(2,1)S(1)}, bf16[2,2,208,128]{3,2,1,0:T(8,128)(2,1)S(1)}, u32[]{:S(2)}, u32[]{:S(2)}) collective-permute-start(bf16[2,2,208,128]{3,2,1,0:T(8,128)(2,1)S(1)} %bitcast.74), channel_id=1, source_target_pairs={{0,8},{8,0},{16,24},{24,16},{1,9},{9,1},{17,25},{25,17},{2,10},{10... | collective-permute-start | bytes 638984 | tf_op jit(solution)/shard_map/ppermute | solution.py:197
  10.8 16.1 %collective-permute-start.6 = (bf16[2,2,208,128]{3,2,1,0:T(8,128)(2,1)S(1)}, bf16[2,2,208,128]{3,2,1,0:T(8,128)(2,1)S(1)}, u32[]{:S(2)}, u32[]{:S(2)}) collective-permute-start(bf16[2,2,208,128]{3,2,1,0:T(8,128)(2,1)S(1)} %bitcast.73), channel_id=1, source_target_pairs={{8,16},{16,8},{9,17},{17,9},{10,18},{18,10},{11,19},{19,11},{12,20... | collective-permute-start | bytes 638984 | tf_op jit(solution)/shard_map/ppermute | solution.py:201
  17.2 16.8 %collective-permute-start.4 = (bf16[1,2,208,128]{3,2,1,0:T(8,128)(2,1)S(1)}, bf16[1,2,208,128]{3,2,1,0:T(8,128)(2,1)S(1)}, u32[]{:S(2)}, u32[]{:S(2)}) collective-permute-start(bf16[1,2,208,128]{3,2,1,0:T(8,128)(2,1)S(1)} %get-tuple-element.61), channel_id=1, source_target_pairs={{2,4},{4,2},{3,5},{5,3},{10,12},{12,10},{11,13},{13,11},{18,20},{2... | collective-permute-start | bytes 319496 | tf_op jit(solution)/shard_map/ppermute | solution.py:201
  17.8 16.1 %collective-permute-start.3 = (bf16[1,2,208,128]{3,2,1,0:T(8,128)(2,1)S(1)}, bf16[1,2,208,128]{3,2,1,0:T(8,128)(2,1)S(1)}, u32[]{:S(2)}, u32[]{:S(2)}) collective-permute-start(bf16[1,2,208,128]{3,2,1,0:T(8,128)(2,1)S(1)} %get-tuple-element.62), channel_id=1, source_target_pairs={{0,2},{2,0},{4,6},{6,4},{1,3},{3,1},{5,7},{7,5},{8,10},{10,8},{12,... | collective-permute-start | bytes 319496 | tf_op jit(solution)/shard_map/ppermute | solution.py:197
  20.9 16.7 %collective-permute-start.8 = (bf16[6,208,128]{2,1,0:T(8,128)(2,1)S(1)}, bf16[6,208,128]{2,1,0:T(8,128)(2,1)S(1)}, u32[]{:S(2)}, u32[]{:S(2)}) collective-permute-start(bf16[6,208,128]{2,1,0:T(8,128)(2,1)S(1)} %get-tuple-element.47), channel_id=1, source_target_pairs={{8,16},{16,8},{9,17},{17,9},{10,18},{18,10},{11,19},{19,11},{12,20... | collective-permute-start | bytes 958472 | tf_op jit(solution)/shard_map/ppermute | solution.py:201
  21.6 16.0 %collective-permute-start.7 = (bf16[6,208,128]{2,1,0:T(8,128)(2,1)S(1)}, bf16[6,208,128]{2,1,0:T(8,128)(2,1)S(1)}, u32[]{:S(2)}, u32[]{:S(2)}) collective-permute-start(bf16[6,208,128]{2,1,0:T(8,128)(2,1)S(1)} %get-tuple-element.48), channel_id=1, source_target_pairs={{0,8},{8,0},{16,24},{24,16},{1,9},{9,1},{17,25},{25,17},{2,10},{10... | collective-permute-start | bytes 958472 | tf_op jit(solution)/shard_map/ppermute | solution.py:197
  34.0 6.4 %collective-permute-start.10 = (bf16[2,208,128]{2,1,0:T(8,128)(2,1)S(1)}, bf16[2,208,128]{2,1,0:T(8,128)(2,1)S(1)}, u32[]{:S(2)}, u32[]{:S(2)}) collective-permute-start(bf16[2,208,128]{2,1,0:T(8,128)(2,1)S(1)} %get-tuple-element.53), channel_id=1, source_target_pairs={{8,16},{16,8},{9,17},{17,9},{10,18},{18,10},{11,19},{19,11},{12,20... | collective-permute-start | bytes 319496 | tf_op jit(solution)/shard_map/ppermute | solution.py:201
  34.7 5.7 %collective-permute-start.9 = (bf16[2,208,128]{2,1,0:T(8,128)(2,1)S(1)}, bf16[2,208,128]{2,1,0:T(8,128)(2,1)S(1)}, u32[]{:S(2)}, u32[]{:S(2)}) collective-permute-start(bf16[2,208,128]{2,1,0:T(8,128)(2,1)S(1)} %get-tuple-element.54), channel_id=1, source_target_pairs={{0,8},{8,0},{16,24},{24,16},{1,9},{9,1},{17,25},{25,17},{2,10},{10... | collective-permute-start | bytes 319496 | tf_op jit(solution)/shard_map/ppermute | solution.py:197
  37.7 2.7 %copy-start = (f32[2,2,2,64,384]{4,3,2,1,0:T(8,128)S(1)}, f32[2,2,2,64,384]{4,3,2,1,0:T(8,128)}, u32[]{:S(2)}) copy-start(f32[2,2,2,64,384]{4,3,2,1,0:T(8,128)} %param.4) | copy-start | bytes 2359300
  47.2 4.0 %collective-permute-start.11 = (f32[1,64,64]{2,1,0:T(8,128)S(1)}, f32[1,64,64]{2,1,0:T(8,128)S(1)}, u32[]{:S(2)}, u32[]{:S(2)}) collective-permute-start(f32[1,64,64]{2,1,0:T(8,128)S(1)} %bitcast.68), channel_id=1, source_target_pairs={{0,1},{1,0},{2,3},{3,2},{4,5},{5,4},{6,7},{7,6},{8,9},{9,8},{10,11... | collective-permute-start | bytes 49160 | tf_op jit(solution)/shard_map/ppermute | solution.py:18
  51.2 5.8 %collective-permute-start.12 = (f32[2,64,64]{2,1,0:T(8,128)S(1)}, f32[2,64,64]{2,1,0:T(8,128)S(1)}, u32[]{:S(2)}, u32[]{:S(2)}) collective-permute-start(f32[2,64,64]{2,1,0:T(8,128)S(1)} %pad_maximum_fusion.6), channel_id=1, source_target_pairs={{0,2},{2,0},{4,6},{6,4},{1,3},{3,1},{5,7},{7,5},{8,10},{10,8},{12,... | collective-permute-start | bytes 98312 | tf_op jit(solution)/shard_map/ppermute | solution.py:18
  57.0 1.4 %collective-permute-start.13 = (f32[4,64,64]{2,1,0:T(8,128)S(1)}, f32[4,64,64]{2,1,0:T(8,128)S(1)}, u32[]{:S(2)}, u32[]{:S(2)}) collective-permute-start(f32[4,64,64]{2,1,0:T(8,128)S(1)} %pad_maximum_fusion.3), channel_id=1, source_target_pairs={{0,8},{8,0},{16,24},{24,16},{1,9},{9,1},{17,25},{25,17},{2,10},{10... | collective-permute-start | bytes 196616 | tf_op jit(solution)/shard_map/ppermute | solution.py:18

commit v4 on v2

--- a/solution.py
+++ b/solution.py
@@ -97,6 +97,12 @@
     square = matmul(x, x, None)
     x = half_lower(excess - matmul_t(x, x, None))
     return x, x - square
+
+
+def sum_of(parts):
+    while len(parts) > 1:
+        parts = [sum(parts[i : i + 2]) for i in range(0, len(parts), 2)]
+    return parts[0]
 
 
 def not_small(norm):
@@ -193,12 +199,13 @@
 def to_neighbours(low, high, axis):
     size = lax.axis_size(axis)
     even = parity(axis) == 0
-    pairs = [(i, i ^ 1) for i in range(size)]
-    received = [lax.ppermute(jnp.where(even, high, low), axis, pairs)]
+    received = []
     if size > 2:
         across = [(i, i + 1) for i in range(1, size - 1, 2)]
         across = across + [(j, i) for i, j in across]
-        received.insert(0, lax.ppermute(jnp.where(even, low, high), axis, across))
+        received.append(lax.ppermute(jnp.where(even, low, high), axis, across))
+    pairs = [(i, i ^ 1) for i in range(size)]
+    received.append(lax.ppermute(jnp.where(even, high, low), axis, pairs))
     return received[::-1]
 
 
@@ -262,9 +269,9 @@
             for side in sides:
                 inside = inside * found[side][0]
                 moved = moved + found[side][1] * steps[side[0]]
-            joint[key] = (inside, moved * (8 * 27) + entry, entry)
+            joint[key] = (inside, moved * (16 * 27) + entry, entry)
         inside, moved, entry = joint[key]
-        code = jnp.int32((source * 8 + a) * 27 + k)
+        code = jnp.int32((source * 16 + a) * 27 + k)
         if sides or across:
             taken = near[a * 27 + k + entry] * inside
             code = code + moved
@@ -277,7 +284,7 @@
 
 def close_list(listed, count, blank):
     for i in range(GROUP):
-        listed[count + i] = jnp.int32(blank * 8 * 27 + 13)
+        listed[count + i] = jnp.int32(blank)
     return lax.div(count + (GROUP - 1), jnp.int32(GROUP))
 
 
@@ -317,8 +324,8 @@
             code = listed[group * GROUP + u]
             pair = lax.div(code, jnp.int32(27))
             k = code - pair * 27
-            source = lax.shift_right_logical(pair, jnp.int32(3))
-            a = lax.bitwise_and(pair, jnp.int32(7))
+            source = lax.shift_right_logical(pair, jnp.int32(4))
+            a = lax.bitwise_and(pair, jnp.int32(15))
             dx = lax.div(k, jnp.int32(9))
             dy = lax.div(k, jnp.int32(3)) - dx * 3
             dz = k - dx * 9 - dy * 3
@@ -364,9 +371,8 @@
     return copies, first
 
 
-def near_stage(stage, near, own, parts, total, listed, blocks, turned, spread, semaphore):
+def list_stage(stage, near, listed, blank):
     halos, lists = stage
-    copies, count = fetch(parts, blocks, semaphore)
     odd = lax.axis_index("gx") % 2
     size = lax.axis_size("gx")
     start = jnp.int32(0)
@@ -380,7 +386,12 @@
             inside = jnp.logical_and(place > 0, place < size - 1).astype(jnp.int32)
             x_side = (odd, inside)
         start = list_pairs(pairs, halos, near, listed, start, x_side)
-    groups = close_list(listed, start, count)
+    return close_list(listed, start, blank)
+
+
+def near_stage(stage, near, own, parts, total, listed, blocks, turned, spread, semaphore):
+    copies, count = fetch(parts, blocks, semaphore)
+    groups = list_stage(stage, near, listed, count * 16 * 27 + 13)
     blocks[count] = jnp.zeros_like(blocks[count])
     for copy in copies:
         copy.wait()
@@ -401,11 +412,15 @@
 
 
 def last_kernel(stage, near, own, before, sketch, *rest):
-    *parts, far, grams, factor, samples, z_out = rest[:-6]
-    listed, blocks, turned, spread, semaphore, single = rest[-6:]
-    far[...] = before[...]
-    near_stage(stage, near, own, parts, far, listed, blocks, turned, spread, semaphore)
-    far[...] = sketch[...] - far[...]
+    *parts, far, grams, factor, samples, z_out = rest[:-5]
+    listed, turned, spread, total, single = rest[-5:]
+    count = far.shape[0]
+    total[:count] = before[...]
+    for blocks in parts:
+        groups = list_stage(stage, near, listed, count * 27 + 13)
+        spread_offsets(blocks, blocks.shape[0], turned, spread)
+        add_pairs(groups, listed, blocks, own, spread, total)
+    far[...] = sketch[...] - total[:count]
     box_level(far, grams, factor, samples, z_out, single)
 
 
@@ -418,6 +433,7 @@
         rows = jnp.concatenate([offsets[a].astype(jnp.float32), filler], axis=0)
         packed[a, 3 * rank :, :] = rows.astype(jnp.bfloat16)
         own[a] = rows[:8]
+    own[count] = jnp.zeros_like(own[count])
     planes = [1 - parity("gz"), parity("gz")]
     for face, plane in zip(faces, planes):
         for column in range(SIDE * SIDE):
@@ -452,22 +468,21 @@
 def box_level(far, grams_out, factor_out, samples_out, z_out, single):
     count, rank, _ = far.shape
     eye = unit(rank)
-    total = jnp.zeros_like(eye)
+    grams = [gram_of(thirds(far[a])) for a in range(count)]
     for a in range(count):
-        gram = gram_of(thirds(far[a]))
-        grams_out[a] = gram
-        total = total + gram
+        grams_out[a] = grams[a]
+    total = sum_of(grams)
     single[...] = join([eye, 0.5 * (total + total.T)], 1)
     eliminate_single(single, rank)
     left = left_side(single[:, :rank])
     lower = upper(single[:, rank:]).T
-    excess = -eye
+    samples = [matmul(left, right_side(thirds(far[a])), None) for a in range(count)]
+    grams = [near_gram(rows, rows) for rows in samples]
     for a in range(count):
-        samples = matmul(left, right_side(thirds(far[a])), None)
-        samples_out[a] = samples
-        excess = excess + near_gram(samples, samples)
+        samples_out[a] = samples[a]
+    excess = sum_of(grams) - eye
     x, z_out[...] = near_unit_factor(excess)
-    factor_out[...] = lower + matmul(lower, x)
+    factor_out[...] = lower + matmul(left_side(lower), right_side(thirds(x)), None)
 
     @pl.when(not_small(jnp.sum(excess * excess, keepdims=True)))
     def _():
@@ -490,18 +505,21 @@
 def leaf_kernel(far, factors, samples, box_z, leaf_out, level_out, work, blocks, es, zs):
     count, rank, leaf_rows = far.shape
     eye = unit(rank)
-    largest = jnp.zeros((1, 1), jnp.float32)
+    inverses = [factors[pl.ds(a, rank, stride=count), :][:, :rank] for a in range(count)]
+    bases = [
+        matmul(left_side(inverses[a]), right_side(thirds(far[a])), None) for a in range(count)
+    ]
+    products = [near_gram(join([bases[a], samples[a]], 0), bases[a]) for a in range(count)]
+    excesses = [product[:rank] - eye for product in products]
     for a in range(count):
-        inverse = factors[pl.ds(a, rank, stride=count), :][:, :rank]
-        basis = matmul(left_side(inverse), right_side(thirds(far[a])), None)
-        leaf_out[a] = basis
-        products = near_gram(join([basis, samples[a]], 0), basis)
-        blocks[a] = products[rank:]
-        excess = products[:rank] - eye
-        es[a] = excess
-        largest = jnp.maximum(largest, jnp.sum(excess * excess, keepdims=True))
+        leaf_out[a] = bases[a]
+        blocks[a] = products[a][rank:]
+        es[a] = excesses[a]
+    inverse_parts = [near_unit_factor(excess)[1] for excess in excesses]
     for a in range(count):
-        zs[a] = near_unit_factor(es[a])[1]
+        zs[a] = inverse_parts[a]
+    norms = [jnp.sum(excess * excess, keepdims=True) for excess in excesses]
+    largest = functools.reduce(jnp.maximum, norms)
 
     @pl.when(not_small(largest))
     def _():
@@ -514,12 +532,13 @@
             blocks[a] = matmul_t(blocks[a], inverse)
             zs[a] = jnp.zeros_like(eye)
 
+    bases = [leaf_out[a] for a in range(count)]
+    bases = [basis - matmul(zs[a], basis, None) for a, basis in enumerate(bases)]
+    crossed = [blocks[a] for a in range(count)]
+    crossed = [block - matmul_t(block, zs[a], None) for a, block in enumerate(crossed)]
     for a in range(count):
-        basis = leaf_out[a]
-        leaf_out[a] = (basis - matmul(zs[a], basis, None)) * math.sqrt(leaf_rows)
-        block = blocks[a]
-        blocks[a] = (block - matmul_t(block, zs[a], None)) * math.sqrt(count * rank)
-    block = join([blocks[a] for a in range(count)], 1)
+        leaf_out[a] = bases[a] * math.sqrt(leaf_rows)
+    block = join(crossed, 1) * math.sqrt(count * rank)
     level_out[...] = block - matmul(box_z[...], block, None)
 
 
@@ -535,22 +554,24 @@
     block = matmul(left_side(single[:, :rank]), right_side(parts), None)
     excess = near_gram(block, block) - eye
     own = block[:, :rank] * (8.0 * math.sqrt(samples.shape[2]))
-    mixing = own - matmul(near_unit_factor(excess)[1], own, None)
-    mix_samples(mixing, samples, box_z, nested_out)
+    own = own - matmul(own, box_z[...], None)
+    left = join(halves(own) * 2, 1)
+    leaves = range(samples.shape[0])
+    parts = [halves(samples[a]) for a in leaves]
+    mixed = [matmul(left, join([f, f, g, g], 0), None) for f, g in parts]
+    z = near_unit_factor(excess)[1]
+    nested = [rows - matmul(z, rows, None) for rows in mixed]
+    for a in leaves:
+        nested_out[a] = nested[a]
 
     @pl.when(not_small(jnp.sum(excess * excess, keepdims=True)))
     def _():
         single[...] = join([eye, eye + excess], 1)
         eliminate_single(single, rank)
-        mix_samples(matmul(single[:, :rank], own), samples, box_z, nested_out)
-
-
-def mix_samples(mixing, samples, box_z, nested_out):
-    mixing = mixing - matmul(mixing, box_z[...], None)
-    left = join(halves(mixing) * 2, 1)
-    for a in range(samples.shape[0]):
-        f, g = halves(samples[a])
-        nested_out[a] = matmul(left, join([f, f, g, g], 0), None)
+        left = join(halves(matmul(single[:, :rank], own)) * 2, 1)
+        for a in leaves:
+            f, g = halves(samples[a])
+            nested_out[a] = matmul(left, join([f, f, g, g], 0), None)
 
 
 def body(sketch, test_matrix, offsets, near):
@@ -568,7 +589,7 @@
         pack_kernel,
         out_shape=(
             like((count,) + block, jnp.bfloat16),
-            like((count, 8, 128), jnp.float32),
+            like((count + 1, 8, 128), jnp.float32),
         )
         + (like((SIDE * SIDE,) + block, jnp.bfloat16),) * faces,
         compiler_params=params,
@@ -629,8 +650,14 @@
     far, grams, factor, samples, box_z = pl.pallas_call(
         functools.partial(last_kernel, stage),
         out_shape=(whole, squares, square, whole, square),
-        in_specs=[IN_SMEM, IN_VMEM, IN_VMEM, IN_VMEM] + [ANYWHERE] * len(parts),
-        scratch_shapes=near_scratch(stage, column * len(parts), block) + [single_scratch],
+        in_specs=[IN_SMEM, IN_VMEM, IN_VMEM, IN_VMEM] + [IN_VMEM] * len(parts),
+        scratch_shapes=[
+            pltpu.SMEM((len(stages[3]) + GROUP + 1,), jnp.int32),
+            pltpu.VMEM((128, 128), jnp.float32),
+            pltpu.VMEM((column, 3, 128, 128), jnp.float32),
+            pltpu.VMEM((count + 1, rank, leaf_rows), jnp.float32),
+            single_scratch,
+        ],
         compiler_params=params,
         name="near_x_and_box_level",
     )(flat_near, own, total, flat_sketch, *parts)

time: 58.7 us -> 56 us (0.954)
  Pallas kernels: 32.3 us -> 30.6 us
  waiting for transfers between devices: 4.06 us -> 2.6 us
  starting transfers between devices: 18.6 us -> 19.2 us
    pallas_call x1, Pallas kernels: 6.14 us -> 4.79 us  [body(): pl.pallas_call(functools.partial(last_kernel, stage), out_shape=(whole, s...]
    ppermute x4, waiting for transfers between devices: 2.33 us -> 1.24 us  [from_partner(): lax.ppermute(x, axis, [(i, i ^ 1 << distance) for i in range(lax.axis_siz...]
    pallas_call x1, Pallas kernels: 3.52 us -> 2.62 us  [body(): pl.pallas_call(leaf_kernel, out_shape=(whole, like((rank, count * rank),...]
    pallas_call x1, Pallas kernels: 3.77 us -> 4.56 us  [body(): pl.pallas_call(functools.partial(first_kernel, stage), out_shape=whole, i...]
    ppermute x4, starting transfers between devices: 15.3 us -> 16 us  [from_partner(): lax.ppermute(x, axis, [(i, i ^ 1 << distance) for i in range(lax.axis_siz...]
  transfers between devices with their start and end apart: 8 -> 8, of which waited for: 5 -> 3; matrix products, arithmetic and copies ran while one was open for 1% -> 1% of each run, Pallas kernels for 38% -> 39%
where the time goes in v4:
time: 56 us
  Pallas kernels  30.6 us (55%)
  starting transfers between devices  19.2 us (34%)
  waiting for transfers between devices  2.6 us (5%)
  local copies, waits for them, and re-layouts  2.46 us (4%)
  between operations  0.79 us (1%)
    ppermute x4, starting transfers between devices, from_partner(): lax.ppermute(x, axis, [(i, i ^ 1 << distance) for i in range(lax.axis_siz...  16 us
    pallas_call x2, Pallas kernels, add_stage(): pl.pallas_call(functools.partial(next_kernel, stage), out_shape=whole, in...  12 us
    pallas_call x1, Pallas kernels, body(): pl.pallas_call(functools.partial(last_kernel, stage), out_shape=(whole, s...  4.79 us
    pallas_call x1, Pallas kernels, body(): pl.pallas_call(functools.partial(first_kernel, stage), out_shape=whole, i...  4.56 us
    pallas_call x1, Pallas kernels, body(): pl.pallas_call(group_kernel, out_shape=whole, scratch_shapes=[single_scra...  3.85 us
    pallas_call x1, Pallas kernels, body(): pl.pallas_call(leaf_factors, out_shape=like((rank * count, 2 * rank), jnp...  2.71 us
    pallas_call x1, Pallas kernels, body(): pl.pallas_call(leaf_kernel, out_shape=(whole, like((rank, count * rank),...  2.62 us
    ppermute x2, starting transfers between devices, to_neighbours(): received.append(lax.ppermute(jnp.where(even, high, low), axis, pairs))  1.83 us
  transfers between devices with their start and end apart: 8, of which 3 were waited for; matrix products, arithmetic and copies ran while one was open for 1% of the time, Pallas kernels for 39%

profile of v4, /device:TPU:0, one launch (start us, length us, event | category | flops | bytes accessed | tf_op | source)
XLA Modules:
  0.0 56.0 jit_solution(17207516467894882656)
XLA Ops:
  0.6 0.7 %copy.7 = bf16[2,2,2,3,128]{4,3,2,1,0:T(4,128)(2,1)S(1)} copy(bf16[2,2,2,3,128]{4,2,3,1,0:T(2,128)(2,1)} %param.6) | data formatting | bytes 12288 | tf_op args[2]
  1.3 0.0 copy-start.1
  1.3 1.0 %copy-done.1 = bf16[2,2,2,64,384]{4,3,2,1,0:T(8,128)(2,1)S(1)} copy-done((bf16[2,2,2,64,384]{4,3,2,1,0:T(8,128)(2,1)S(1)}, bf16[2,2,2,64,384]{4,3,2,1,0:T(8,128)(2,1)}, u32[]{:S(2)}) %copy-start.1) | copy-done | bytes 393240
  2.3 0.1 pack.1
  2.4 3.0 %collective-permute-start = (bf16[4,208,128]{2,1,0:T(8,128)(2,1)S(1)}, bf16[4,208,128]{2,1,0:T(8,128)(2,1)S(1)}, u32[]{:S(2)}, u32[]{:S(2)}) collective-permute-start(bf16[4,208,128]{2,1,0:T(8,128)(2,1)S(1)} %get-tuple-element.24), channel_id=1, source_target_pairs={{0,1},{1,0},{2,3},{3,2},{4,5},{5,4},{6,7},{7,6},{8,9},{9,8},{10,11... | collective-permute-start | bytes 638984 | tf_op jit(solution)/shard_map/ppermute | solution.py:18
  5.5 0.8 %reshape.50.near = s32[216]{0:T(256)S(1)} reshape(s32[2,2,2,27]{3,2,1,0:T(2,128)} %param.7) | data formatting | bytes 1728 | tf_op jit(solution)/shard_map/reshape | solution.py:584
  6.2 4.6 %near_inner.1.before = f32[8,64,384]{2,1,0:T(8,128)S(1)} custom-call(s32[216]{0:T(256)S(1)} %reshape.50.near, f32[9,8,128]{2,1,0:T(8,128)S(1)} %get-tuple-element.22.own, bf16[8,208,128]{2,1,0:T(8,128)(2,1)S(1)} %get-tuple-element.23.own_blocks.rest_0_), custom_call_target="tpu_custom_call" | custom-call | flops 4000000000 | bytes 4194304 | tf_op jit(solution)/shard_map/near_inner/pallas_call | solution.py:617
  10.8 0.0 collective-permute-done.rest_1_
  10.9 1.8 %collective-permute-start.1 = (bf16[2,3,208,128]{3,2,1,0:T(8,128)(2,1)S(1)}, bf16[2,3,208,128]{3,2,1,0:T(8,128)(2,1)S(1)}, u32[]{:S(2)}, u32[]{:S(2)}) collective-permute-start(bf16[2,3,208,128]{3,2,1,0:T(8,128)(2,1)S(1)} %get-tuple-element.43), channel_id=1, source_target_pairs={{0,2},{2,0},{4,6},{6,4},{1,3},{3,1},{5,7},{7,5},{8,10},{10,8},{12,... | collective-permute-start | bytes 958472 | tf_op jit(solution)/shard_map/ppermute | solution.py:208
  12.7 0.7 %collective-permute-start.2 = (bf16[2,3,208,128]{3,2,1,0:T(8,128)(2,1)S(1)}, bf16[2,3,208,128]{3,2,1,0:T(8,128)(2,1)S(1)}, u32[]{:S(2)}, u32[]{:S(2)}) collective-permute-start(bf16[2,3,208,128]{3,2,1,0:T(8,128)(2,1)S(1)} %get-tuple-element.44), channel_id=1, source_target_pairs={{2,4},{4,2},{3,5},{5,3},{10,12},{12,10},{11,13},{13,11},{18,20},{2... | collective-permute-start | bytes 958472 | tf_op jit(solution)/shard_map/ppermute | solution.py:206
  13.3 6.7 %near_inner_and_z.1.before = f32[8,64,384]{2,1,0:T(8,128)S(1)} custom-call(s32[216]{0:T(256)S(1)} %reshape.50.near, f32[9,8,128]{2,1,0:T(8,128)S(1)} %get-tuple-element.22.own, f32[8,64,384]{2,1,0:T(8,128)S(1)} %near_inner.1.before, bf16[8,208,128]{2,1,0:T(8,128)(2,1)S(1)} %get-tuple-element.23.own_blocks.rest_0_, ...), custom_call_target="tpu_custom_call" | custom-call | flops 5000000000 | bytes 4194304 | tf_op jit(solution)/shard_map/near_inner_and_z/pallas_call | solution.py:631
  20.1 0.0 collective-permute-done.1
  20.1 0.0 collective-permute-done.2
  20.1 0.1 pad_maximum_fusion
  20.2 0.1 select_bitcast_fusion
  20.3 0.1 collective-permute-start.3
  20.3 0.7 %collective-permute-start.4 = (bf16[4,3,208,128]{3,2,1,0:T(8,128)(2,1)S(1)}, bf16[4,3,208,128]{3,2,1,0:T(8,128)(2,1)S(1)}, u32[]{:S(2)}, u32[]{:S(2)}) collective-permute-start(bf16[4,3,208,128]{3,2,1,0:T(8,128)(2,1)S(1)} %get-tuple-element.41), channel_id=1, source_target_pairs={{8,16},{16,8},{9,17},{17,9},{10,18},{18,10},{11,19},{19,11},{12,20... | collective-permute-start | bytes 1916936 | tf_op jit(solution)/shard_map/ppermute | solution.py:206
  21.0 1.4 %collective-permute-done.3 = bf16[4,3,208,128]{3,2,1,0:T(8,128)(2,1)S(1)} collective-permute-done((bf16[4,3,208,128]{3,2,1,0:T(8,128)(2,1)S(1)}, bf16[4,3,208,128]{3,2,1,0:T(8,128)(2,1)S(1)}, u32[]{:S(2)}, u32[]{:S(2)}) %collective-permute-start.3) | collective-permute-done | bytes 639008 | tf_op jit(solution)/shard_map/ppermute | solution.py:208
  22.4 0.0 copy-start
  22.4 5.3 %near_y_and_x.1.before = f32[8,64,384]{2,1,0:T(8,128)S(1)} custom-call(s32[216]{0:T(256)S(1)} %reshape.50.near, f32[9,8,128]{2,1,0:T(8,128)S(1)} %get-tuple-element.22.own, f32[8,64,384]{2,1,0:T(8,128)S(1)} %near_inner_and_z.1.before, bf16[6,208,128]{2,1,0:T(8,128)(2,1)S(1)} %bitcast.30, bf16[6,208,128]{2,1,0:T(8,128)(2,1)S(1)} %bitcast.32, ...), custom_call_target="tpu_custom_call" | custom-call | flops 7000000000 | bytes 4194304 | tf_op jit(solution)/shard_map/near_y_and_x/pallas_call | solution.py:631
  27.7 0.0 collective-permute-done.4
  27.7 0.0 copy-done
  27.7 4.8 %near_x_and_box_level.1 = (f32[8,64,384]{2,1,0:T(8,128)S(1)}, f32[8,64,64]{2,1,0:T(8,128)S(1)}, f32[64,64]{1,0:T(8,128)S(1)}, f32[8,64,384]{2,1,0:T(8,128)S(1)}, f32[64,64]{1,0:T(8,128)S(1)}) custom-call(s32[216]{0:T(256)S(1)} %reshape.50.near, f32[9,8,128]{2,1,0:T(8,128)S(1)} %get-tuple-element.22.own, f32[8,64,384]{2,1,0:T(8,128)S(1)} %near_y_and_x.1.before, ...), custom_call_target="tpu_custom_call" | custom-call | tf_op jit(solution)/shard_map/near_x_and_box_level/pallas_call | solution.py:650
  32.5 1.0 %collective-permute-start.5 = (f32[1,64,64]{2,1,0:T(8,128)S(1)}, f32[1,64,64]{2,1,0:T(8,128)S(1)}, u32[]{:S(2)}, u32[]{:S(2)}) collective-permute-start(f32[1,64,64]{2,1,0:T(8,128)S(1)} %bitcast.35), channel_id=1, source_target_pairs={{0,1},{1,0},{2,3},{3,2},{4,5},{5,4},{6,7},{7,6},{8,9},{9,8},{10,11... | collective-permute-start | bytes 49160 | tf_op jit(solution)/shard_map/ppermute | solution.py:18
  33.5 2.7 %leaf_factors.1.factors = f32[512,128]{1,0:T(8,128)S(1)} custom-call(f32[8,64,64]{2,1,0:T(8,128)S(1)} %get-tuple-element.30.grams), custom_call_target="tpu_custom_call" | custom-call | flops 3000000000 | bytes 4194304 | tf_op jit(solution)/shard_map/leaf_factors/pallas_call | solution.py:666
  36.3 0.3 collective-permute-done.5
  36.5 6.5 %collective-permute-start.6 = (f32[2,64,64]{2,1,0:T(8,128)S(1)}, f32[2,64,64]{2,1,0:T(8,128)S(1)}, u32[]{:S(2)}, u32[]{:S(2)}) collective-permute-start(f32[2,64,64]{2,1,0:T(8,128)S(1)} %pad_maximum_fusion.4), channel_id=1, source_target_pairs={{0,2},{2,0},{4,6},{6,4},{1,3},{3,1},{5,7},{7,5},{8,10},{10,8},{12,... | collective-permute-start | bytes 98312 | tf_op jit(solution)/shard_map/ppermute | solution.py:18
  43.1 2.6 %leaf_level.1 = (f32[8,64,384]{2,1,0:T(8,128)}, f32[64,512]{1,0:T(8,128)}) custom-call(f32[8,64,384]{2,1,0:T(8,128)S(1)} %get-tuple-element.32.far, f32[512,128]{1,0:T(8,128)S(1)} %leaf_factors.1.factors, f32[8,64,384]{2,1,0:T(8,128)S(1)} %get-tuple-element.34.samples, f32[64,64]{1,0:T(8,128)S(1)} %get-tuple-element.35.box_z), custom_call_target="tpu_custom_call" | custom-call | flops 4000000000 | bytes 4194304 | tf_op jit(solution)/shard_map/leaf_level/pallas_call | solution.py:675
  45.7 0.0 collective-permute-done.6
  45.7 5.4 %collective-permute-start.7 = (f32[4,64,64]{2,1,0:T(8,128)S(1)}, f32[4,64,64]{2,1,0:T(8,128)S(1)}, u32[]{:S(2)}, u32[]{:S(2)}) collective-permute-start(f32[4,64,64]{2,1,0:T(8,128)S(1)} %pad_maximum_fusion.3), channel_id=1, source_target_pairs={{0,8},{8,0},{16,24},{24,16},{1,9},{9,1},{17,25},{25,17},{2,10},{10... | collective-permute-start | bytes 196616 | tf_op jit(solution)/shard_map/ppermute | solution.py:18
  51.1 1.0 %collective-permute-done.7 = f32[4,64,64]{2,1,0:T(8,128)S(1)} collective-permute-done((f32[4,64,64]{2,1,0:T(8,128)S(1)}, f32[4,64,64]{2,1,0:T(8,128)S(1)}, u32[]{:S(2)}, u32[]{:S(2)}) %collective-permute-start.7) | collective-permute-done | bytes 65568 | tf_op jit(solution)/shard_map/ppermute | solution.py:18
  52.1 3.8 %group_level.1 = f32[8,64,384]{2,1,0:T(8,128)} custom-call(f32[8,64,64]{2,1,0:T(8,128)S(1)} %pad_maximum_fusion.2.factors, f32[8,64,384]{2,1,0:T(8,128)S(1)} %get-tuple-element.34.samples, f32[64,64]{1,0:T(8,128)S(1)} %get-tuple-element.35.box_z), custom_call_target="tpu_custom_call" | custom-call | tf_op jit(solution)/shard_map/group_level/pallas_call | solution.py:686
  (5 shorter events, 0.1 us)
Async XLA Ops:
  1.3 1.0 %copy-start.1 = (bf16[2,2,2,64,384]{4,3,2,1,0:T(8,128)(2,1)S(1)}, bf16[2,2,2,64,384]{4,3,2,1,0:T(8,128)(2,1)}, u32[]{:S(2)}) copy-start(bf16[2,2,2,64,384]{4,3,2,1,0:T(8,128)(2,1)} %param.5) | copy-start | bytes 1179652
  2.4 8.4 %collective-permute-start = (bf16[4,208,128]{2,1,0:T(8,128)(2,1)S(1)}, bf16[4,208,128]{2,1,0:T(8,128)(2,1)S(1)}, u32[]{:S(2)}, u32[]{:S(2)}) collective-permute-start(bf16[4,208,128]{2,1,0:T(8,128)(2,1)S(1)} %get-tuple-element.24), channel_id=1, source_target_pairs={{0,1},{1,0},{2,3},{3,2},{4,5},{5,4},{6,7},{7,6},{8,9},{9,8},{10,11... | collective-permute-start | bytes 638984 | tf_op jit(solution)/shard_map/ppermute | solution.py:18
  10.9 9.1 %collective-permute-start.1 = (bf16[2,3,208,128]{3,2,1,0:T(8,128)(2,1)S(1)}, bf16[2,3,208,128]{3,2,1,0:T(8,128)(2,1)S(1)}, u32[]{:S(2)}, u32[]{:S(2)}) collective-permute-start(bf16[2,3,208,128]{3,2,1,0:T(8,128)(2,1)S(1)} %get-tuple-element.43), channel_id=1, source_target_pairs={{0,2},{2,0},{4,6},{6,4},{1,3},{3,1},{5,7},{7,5},{8,10},{10,8},{12,... | collective-permute-start | bytes 958472 | tf_op jit(solution)/shard_map/ppermute | solution.py:208
  12.7 7.4 %collective-permute-start.2 = (bf16[2,3,208,128]{3,2,1,0:T(8,128)(2,1)S(1)}, bf16[2,3,208,128]{3,2,1,0:T(8,128)(2,1)S(1)}, u32[]{:S(2)}, u32[]{:S(2)}) collective-permute-start(bf16[2,3,208,128]{3,2,1,0:T(8,128)(2,1)S(1)} %get-tuple-element.44), channel_id=1, source_target_pairs={{2,4},{4,2},{3,5},{5,3},{10,12},{12,10},{11,13},{13,11},{18,20},{2... | collective-permute-start | bytes 958472 | tf_op jit(solution)/shard_map/ppermute | solution.py:206
  20.3 2.1 %collective-permute-start.3 = (bf16[4,3,208,128]{3,2,1,0:T(8,128)(2,1)S(1)}, bf16[4,3,208,128]{3,2,1,0:T(8,128)(2,1)S(1)}, u32[]{:S(2)}, u32[]{:S(2)}) collective-permute-start(bf16[4,3,208,128]{3,2,1,0:T(8,128)(2,1)S(1)} %get-tuple-element.42), channel_id=1, source_target_pairs={{0,8},{8,0},{16,24},{24,16},{1,9},{9,1},{17,25},{25,17},{2,10},{10... | collective-permute-start | bytes 1916936 | tf_op jit(solution)/shard_map/ppermute | solution.py:208
  20.3 7.4 %collective-permute-start.4 = (bf16[4,3,208,128]{3,2,1,0:T(8,128)(2,1)S(1)}, bf16[4,3,208,128]{3,2,1,0:T(8,128)(2,1)S(1)}, u32[]{:S(2)}, u32[]{:S(2)}) collective-permute-start(bf16[4,3,208,128]{3,2,1,0:T(8,128)(2,1)S(1)} %get-tuple-element.41), channel_id=1, source_target_pairs={{8,16},{16,8},{9,17},{17,9},{10,18},{18,10},{11,19},{19,11},{12,20... | collective-permute-start | bytes 1916936 | tf_op jit(solution)/shard_map/ppermute | solution.py:206
  22.4 5.3 %copy-start = (f32[2,2,2,64,384]{4,3,2,1,0:T(8,128)S(1)}, f32[2,2,2,64,384]{4,3,2,1,0:T(8,128)}, u32[]{:S(2)}) copy-start(f32[2,2,2,64,384]{4,3,2,1,0:T(8,128)} %param.4) | copy-start | bytes 2359300
  32.5 4.0 %collective-permute-start.5 = (f32[1,64,64]{2,1,0:T(8,128)S(1)}, f32[1,64,64]{2,1,0:T(8,128)S(1)}, u32[]{:S(2)}, u32[]{:S(2)}) collective-permute-start(f32[1,64,64]{2,1,0:T(8,128)S(1)} %bitcast.35), channel_id=1, source_target_pairs={{0,1},{1,0},{2,3},{3,2},{4,5},{5,4},{6,7},{7,6},{8,9},{9,8},{10,11... | collective-permute-start | bytes 49160 | tf_op jit(solution)/shard_map/ppermute | solution.py:18
  36.5 9.2 %collective-permute-start.6 = (f32[2,64,64]{2,1,0:T(8,128)S(1)}, f32[2,64,64]{2,1,0:T(8,128)S(1)}, u32[]{:S(2)}, u32[]{:S(2)}) collective-permute-start(f32[2,64,64]{2,1,0:T(8,128)S(1)} %pad_maximum_fusion.4), channel_id=1, source_target_pairs={{0,2},{2,0},{4,6},{6,4},{1,3},{3,1},{5,7},{7,5},{8,10},{10,8},{12,... | collective-permute-start | bytes 98312 | tf_op jit(solution)/shard_map/ppermute | solution.py:18
  45.7 6.4 %collective-permute-start.7 = (f32[4,64,64]{2,1,0:T(8,128)S(1)}, f32[4,64,64]{2,1,0:T(8,128)S(1)}, u32[]{:S(2)}, u32[]{:S(2)}) collective-permute-start(f32[4,64,64]{2,1,0:T(8,128)S(1)} %pad_maximum_fusion.3), channel_id=1, source_target_pairs={{0,8},{8,0},{16,24},{24,16},{1,9},{9,1},{17,25},{25,17},{2,10},{10... | collective-permute-start | bytes 196616 | tf_op jit(solution)/shard_map/ppermute | solution.py:18

commit v5 on v4

--- a/solution.py
+++ b/solution.py
@@ -219,21 +219,20 @@
 
 def pair_tables(halos):
     depth = SIDE + halos[2]
+    wide = SIDE + halos[1]
     stages = ([], [], [], [])
     for a in range(SIDE**3):
         place = (a // 4, a // 2 % 2, a % 2)
         for k in range(27):
             at = [p + d for p, d in zip(place, (k // 9 - 1, k // 3 % 3 - 1, k % 3 - 1))]
-            sides = tuple((axis, t) for axis, t in enumerate(at) if t in (-1, 2))
+            sides = tuple((axis, t) for axis, t in enumerate(at) if t in (-1, 2) and axis > 0)
             x, y, z = (2 if t == -1 else t for t in at)
             if at[0] == -1:
-                stages[3].append((a, k, y * depth + z, sides[1:], True))
+                stages[3].append((a, k, y * depth + z, sides, True))
             elif at[0] == 2:
                 continue
-            elif y == 2:
-                stages[2].append((a, k, x * depth + z, sides, False))
-            elif z == 2:
-                stages[1].append((a, k, SIDE**3 + x * SIDE + y, sides, False))
+            elif sides:
+                stages[2].append((a, k, (x * wide + y) * depth + z, sides, False))
             else:
                 stages[a * 2 // SIDE**3].append((a, k, leaf_index(x, y, z), sides, False))
     return stages
@@ -259,13 +258,9 @@
         if key not in joint:
             inside, moved, entry = jnp.int32(1), jnp.int32(0), jnp.int32(0)
             if across:
-                steps = {1: depth, 2: 1}
                 inside = x_side[1]
                 entry = x_side[0] * (4 * 27 + 18)
-            elif any(axis == 1 for axis, _ in sides):
-                steps = {1: SIDE * depth, 2: 1}
-            else:
-                steps = {2: SIDE * SIDE}
+            steps = {1: depth, 2: 1}
             for side in sides:
                 inside = inside * found[side][0]
                 moved = moved + found[side][1] * steps[side[0]]
@@ -288,18 +283,20 @@
     return lax.div(count + (GROUP - 1), jnp.int32(GROUP))
 
 
-def spread_offsets(blocks, count, turned, spread):
+def spread_offsets(blocks, places, turned, spread):
     rank3 = blocks.shape[1] - 16
-    turned[...] = jnp.zeros_like(turned)
-    for s in range(count):
-        turned[4 * s : 4 * s + 4, :] = blocks[s, rank3:, :].astype(jnp.float32)[:4]
-    columns = turned[...].T.astype(jnp.bfloat16)
     row, lane = positions((128, 384))
-    for s in range(count):
-        chosen = jnp.where(row == 4 * s + lane // 128, 1.0, 0.0).astype(jnp.bfloat16)
-        values = matmul(columns, chosen, None)
-        for p in range(3):
-            spread[s, p] = values[:, 128 * p : 128 * (p + 1)]
+    for first in range(0, len(places), 32):
+        chunk = places[first : first + 32]
+        turned[...] = jnp.zeros_like(turned)
+        for i, s in enumerate(chunk):
+            turned[4 * i : 4 * i + 4, :] = blocks[s, rank3:, :].astype(jnp.float32)[:4]
+        columns = turned[...].T.astype(jnp.bfloat16)
+        for i, s in enumerate(chunk):
+            chosen = jnp.where(row == 4 * i + lane // 128, 1.0, 0.0).astype(jnp.bfloat16)
+            values = matmul(columns, chosen, None)
+            for p in range(3):
+                spread[s, p] = values[:, 128 * p : 128 * (p + 1)]
 
 
 def tile_rows(own, spread, rows):
@@ -357,20 +354,6 @@
             total[a] += matmul(sampled, matrix, None)
 
 
-def fetch(parts, blocks, semaphore):
-    copies = []
-    first = 0
-    for i, part in enumerate(parts):
-        copies.append(
-            pltpu.make_async_copy(
-                part, blocks.at[pl.ds(first, part.shape[0])], semaphore.at[i]
-            )
-        )
-        copies[-1].start()
-        first += part.shape[0]
-    return copies, first
-
-
 def list_stage(stage, near, listed, blank):
     halos, lists = stage
     odd = lax.axis_index("gx") % 2
@@ -389,38 +372,44 @@
     return close_list(listed, start, blank)
 
 
-def near_stage(stage, near, own, parts, total, listed, blocks, turned, spread, semaphore):
-    copies, count = fetch(parts, blocks, semaphore)
-    groups = list_stage(stage, near, listed, count * 16 * 27 + 13)
-    blocks[count] = jnp.zeros_like(blocks[count])
-    for copy in copies:
-        copy.wait()
-    spread_offsets(blocks, count, turned, spread)
-    spread[count] = jnp.zeros_like(spread[count])
+def near_stage(stage, near, own, blocks, total, listed, turned, spread):
+    groups = list_stage(stage, near, listed, (total.shape[0] - 1) * 27 + 13)
+    places = sorted({first + pair[2] for pairs, first, _ in stage[1] for pair in pairs})
+    spread_offsets(blocks, with_far_places(places, stage), turned, spread)
     add_pairs(groups, listed, blocks, own, spread, total)
 
 
-def first_kernel(stage, near, own, own_blocks, total, *scratch):
+def with_far_places(places, stage):
+    halos, lists = stage
+    depth = SIDE + halos[2]
+    found = set(places)
+    for pairs, first, _ in lists:
+        for _, _, source, sides, _ in pairs:
+            moves = [0]
+            for axis, _ in sides:
+                step = {1: depth, 2: 1}[axis] * (halos[axis] - 1)
+                moves = moves + [move + step for move in moves]
+            found.update(first + source + move for move in moves)
+    return sorted(found)
+
+
+def first_kernel(stage, near, own, blocks, total, *scratch):
     total[...] = jnp.zeros_like(total)
-    near_stage(stage, near, own, [own_blocks], total, *scratch)
-
-
-def next_kernel(stage, near, own, before, *rest):
-    *parts, total, listed, blocks, turned, spread, semaphore = rest
+    near_stage(stage, near, own, blocks, total, *scratch)
+
+
+def next_kernel(stage, near, own, blocks, before, total, *scratch):
     total[...] = before[...]
-    near_stage(stage, near, own, parts, total, listed, blocks, turned, spread, semaphore)
+    near_stage(stage, near, own, blocks, total, *scratch)
 
 
 def last_kernel(stage, near, own, before, sketch, *rest):
     *parts, far, grams, factor, samples, z_out = rest[:-5]
-    listed, turned, spread, total, single = rest[-5:]
-    count = far.shape[0]
-    total[:count] = before[...]
+    total, single, *scratch = rest[-5:]
+    total[...] = before[...]
     for blocks in parts:
-        groups = list_stage(stage, near, listed, count * 27 + 13)
-        spread_offsets(blocks, blocks.shape[0], turned, spread)
-        add_pairs(groups, listed, blocks, own, spread, total)
-    far[...] = sketch[...] - total[:count]
+        near_stage(stage, near, own, blocks, total, *scratch)
+    far[...] = sketch[...] - total[: far.shape[0]]
     box_level(far, grams, factor, samples, z_out, single)
 
 
@@ -443,14 +432,12 @@
 VMEM_LIMIT = 48 * 1024 * 1024
 
 
-def near_scratch(stage, count, block):
+def near_scratch(stage, count):
     length = sum(len(pairs) for pairs, _, _ in stage[1])
     return [
         pltpu.SMEM((length + GROUP + 1,), jnp.int32),
-        pltpu.VMEM((count + 1,) + block, jnp.bfloat16),
         pltpu.VMEM((128, 128), jnp.float32),
-        pltpu.VMEM((count + 1, 3, 128, 128), jnp.float32),
-        pltpu.SemaphoreType.DMA((4,)),
+        pltpu.VMEM((count, 3, 128, 128), jnp.float32),
     ]
 
 
@@ -462,7 +449,6 @@
 
 IN_SMEM = pl.BlockSpec(memory_space=pltpu.SMEM)
 IN_VMEM = pl.BlockSpec(memory_space=pltpu.VMEM)
-ANYWHERE = pl.BlockSpec(memory_space=pl.ANY)
 
 
 def box_level(far, grams_out, factor_out, samples_out, z_out, single):
@@ -607,57 +593,43 @@
     depth = extended.shape[2]
     flat = lambda parts: [x.reshape((-1,) + block) for x in parts]
     column = (SIDE + halos[1]) * depth
-    y_blocks = SIDE * depth * halos[1]
     whole = like((count, rank, leaf_rows), jnp.float32)
+    sums = like((count + 1, rank, leaf_rows), jnp.float32)
     squares = like((count, rank, rank), jnp.float32)
     square = like((rank, rank), jnp.float32)
     single_scratch = pltpu.VMEM((rank, 2 * rank), jnp.float32)
 
-    stage = (halos, [(stages[0], 0, None)])
-    total = pl.pallas_call(
-        functools.partial(first_kernel, stage),
-        out_shape=whole,
-        in_specs=[IN_SMEM, IN_VMEM, ANYWHERE],
-        scratch_shapes=near_scratch(stage, count, block),
-        cost_estimate=cost(4),
-        compiler_params=params,
-        name="near_inner",
-    )(flat_near, own, packed)
-
-    extended, total = lax.optimization_barrier((extended, total))
-    y_halos = to_neighbours(extended[:, 0], extended[:, 1], "gy")
-
-    def add_stage(stage, total, parts, name, time):
+    def add_stage(stage, blocks, before, name, time):
+        kernel = first_kernel if before is None else next_kernel
+        before = [] if before is None else [before]
         return pl.pallas_call(
-            functools.partial(next_kernel, stage),
-            out_shape=whole,
-            in_specs=[IN_SMEM, IN_VMEM, IN_VMEM] + [ANYWHERE] * len(parts),
-            scratch_shapes=near_scratch(stage, sum(part.shape[0] for part in parts), block),
+            functools.partial(kernel, stage),
+            out_shape=sums,
+            in_specs=[IN_SMEM, IN_VMEM, IN_VMEM] + [IN_VMEM] * len(before),
+            scratch_shapes=near_scratch(stage, blocks.shape[0]),
             cost_estimate=cost(time),
             compiler_params=params,
             name=name,
-        )(flat_near, own, total, *parts)
-
-    stage = (halos, [(stages[1], 0, None)])
-    total = add_stage(stage, total, [packed] + flat(z_halos), "near_inner_and_z", 5)
+        )(flat_near, own, blocks, *before)
+
+    total = add_stage((halos, [(stages[0], 0, None)]), packed, None, "near_inner", 4)
+    extended, total = lax.optimization_barrier((extended, total))
+    y_halos = to_neighbours(extended[:, 0], extended[:, 1], "gy")
+    total = add_stage((halos, [(stages[1], 0, None)]), packed, total, "near_inner_rest", 4)
     wide = join([extended] + [h[:, None] for h in y_halos], 1)
     wide, total = lax.optimization_barrier((wide, total))
     x_halos = to_neighbours(wide[0], wide[1], "gx")
-    stage = (halos, [(stages[2], 0, None), (stages[3], y_blocks, True)])
-    total = add_stage(stage, total, flat(y_halos) + flat(x_halos[:1]), "near_y_and_x", 7)
-    stage = (halos, [(stages[3], 0, False)] if halos[0] == 2 else [])
+    stage = (halos, [(stages[2], 0, None), (stages[3], SIDE * column, True)])
+    blocks = join(flat([wide, x_halos[0]]), 0)
+    total = add_stage(stage, blocks, total, "near_z_y_and_x", 9)
+    stage = (halos, [(stages[3], 0, False)])
     parts = flat(x_halos[1:])
     far, grams, factor, samples, box_z = pl.pallas_call(
         functools.partial(last_kernel, stage),
         out_shape=(whole, squares, square, whole, square),
         in_specs=[IN_SMEM, IN_VMEM, IN_VMEM, IN_VMEM] + [IN_VMEM] * len(parts),
-        scratch_shapes=[
-            pltpu.SMEM((len(stages[3]) + GROUP + 1,), jnp.int32),
-            pltpu.VMEM((128, 128), jnp.float32),
-            pltpu.VMEM((column, 3, 128, 128), jnp.float32),
-            pltpu.VMEM((count + 1, rank, leaf_rows), jnp.float32),
-            single_scratch,
-        ],
+        scratch_shapes=[pltpu.VMEM(sums.shape, jnp.float32), single_scratch]
+        + near_scratch(stage, column),
         compiler_params=params,
         name="near_x_and_box_level",
     )(flat_near, own, total, flat_sketch, *parts)

time: 56 us -> 55.8 us (level)
  waiting for transfers between devices: 2.6 us -> 6.26 us
  Pallas kernels: 30.6 us -> 27.3 us
  starting transfers between devices: 19.2 us -> 18.3 us
    pallas_call x3, Pallas kernels: 16.5 us -> 13.2 us  [add_stage(): pl.pallas_call(functools.partial(kernel, stage), out_shape=sums, in_specs...]
    ppermute x2, waiting for transfers between devices: 1.35 us -> 4.16 us  [to_neighbours(): received.append(lax.ppermute(jnp.where(even, high, low), axis, pairs))]
    ppermute x4, starting transfers between devices: 16 us -> 15 us  [from_partner(): lax.ppermute(x, axis, [(i, i ^ 1 << distance) for i in range(lax.axis_siz...]
    ppermute x4, waiting for transfers between devices: 1.24 us -> 2.09 us  [from_partner(): lax.ppermute(x, axis, [(i, i ^ 1 << distance) for i in range(lax.axis_siz...]
  transfers between devices with their start and end apart: 8 -> 8, of which waited for: 3 -> 4; matrix products, arithmetic and copies ran while one was open for 1% -> 2% of each run, Pallas kernels for 39% -> 33%
where the time goes in v5:
time: 55.8 us; the launch traced here: 55.5 us
  Pallas kernels  27.3 us (49%)
  starting transfers between devices  18.3 us (33%)
  waiting for transfers between devices  6.26 us (11%)
  local copies, waits for them, and re-layouts  2.47 us (4%)
  between operations  0.77 us (1%)
    ppermute x4, starting transfers between devices, from_partner(): lax.ppermute(x, axis, [(i, i ^ 1 << distance) for i in range(lax.axis_siz...  15 us
    pallas_call x3, Pallas kernels, add_stage(): pl.pallas_call(functools.partial(kernel, stage), out_shape=sums, in_specs...  13.2 us
    pallas_call x1, Pallas kernels, body(): pl.pallas_call(functools.partial(last_kernel, stage), out_shape=(whole, s...  4.78 us
    ppermute x2, waiting for transfers between devices, to_neighbours(): received.append(lax.ppermute(jnp.where(even, high, low), axis, pairs))  4.16 us
    pallas_call x1, Pallas kernels, body(): pl.pallas_call(group_kernel, out_shape=whole, scratch_shapes=[single_scra...  3.85 us
    pallas_call x1, Pallas kernels, body(): pl.pallas_call(leaf_factors, out_shape=like((rank * count, 2 * rank), jnp...  2.71 us
    pallas_call x1, Pallas kernels, body(): pl.pallas_call(leaf_kernel, out_shape=(whole, like((rank, count * rank),...  2.61 us
    ppermute x4, waiting for transfers between devices, from_partner(): lax.ppermute(x, axis, [(i, i ^ 1 << distance) for i in range(lax.axis_siz...  2.09 us
  transfers between devices with their start and end apart: 8, of which 4 were waited for; matrix products, arithmetic and copies ran while one was open for 2% of the time, Pallas kernels for 33%

profile of v5, /device:TPU:0, one launch (start us, length us, event | category | flops | bytes accessed | tf_op | source)
XLA Modules:
  0.0 55.5 jit_solution(9616713719921319008)
XLA Ops:
  0.6 0.7 %copy.7 = bf16[2,2,2,3,128]{4,3,2,1,0:T(4,128)(2,1)S(1)} copy(bf16[2,2,2,3,128]{4,2,3,1,0:T(2,128)(2,1)} %param.6) | data formatting | bytes 12288 | tf_op args[2]
  1.3 0.0 copy-start.1
  1.3 1.0 %copy-done.1 = bf16[2,2,2,64,384]{4,3,2,1,0:T(8,128)(2,1)S(1)} copy-done((bf16[2,2,2,64,384]{4,3,2,1,0:T(8,128)(2,1)S(1)}, bf16[2,2,2,64,384]{4,3,2,1,0:T(8,128)(2,1)}, u32[]{:S(2)}) %copy-start.1) | copy-done | bytes 393240
  2.3 0.1 pack.1
  2.4 3.0 %collective-permute-start = (bf16[4,208,128]{2,1,0:T(8,128)(2,1)S(1)}, bf16[4,208,128]{2,1,0:T(8,128)(2,1)S(1)}, u32[]{:S(2)}, u32[]{:S(2)}) collective-permute-start(bf16[4,208,128]{2,1,0:T(8,128)(2,1)S(1)} %get-tuple-element.24), channel_id=1, source_target_pairs={{0,1},{1,0},{2,3},{3,2},{4,5},{5,4},{6,7},{7,6},{8,9},{9,8},{10,11... | collective-permute-start | bytes 638984 | tf_op jit(solution)/shard_map/ppermute | solution.py:18
  5.5 0.8 %reshape.47.near = s32[216]{0:T(256)S(1)} reshape(s32[2,2,2,27]{3,2,1,0:T(2,128)} %param.7) | data formatting | bytes 1728 | tf_op jit(solution)/shard_map/reshape | solution.py:570
  6.2 3.4 %near_inner.1.before = f32[9,64,384]{2,1,0:T(8,128)S(1)} custom-call(s32[216]{0:T(256)S(1)} %reshape.47.near, f32[9,8,128]{2,1,0:T(8,128)S(1)} %get-tuple-element.22.own, bf16[8,208,128]{2,1,0:T(8,128)(2,1)S(1)} %get-tuple-element.23.blocks), custom_call_target="tpu_custom_call" | custom-call | flops 4000000000 | bytes 4194304 | tf_op jit(solution)/shard_map/near_inner/pallas_call | solution.py:605
  9.6 1.1 %collective-permute-done = bf16[4,208,128]{2,1,0:T(8,128)(2,1)S(1)} collective-permute-done((bf16[4,208,128]{2,1,0:T(8,128)(2,1)S(1)}, bf16[4,208,128]{2,1,0:T(8,128)(2,1)S(1)}, u32[]{:S(2)}, u32[]{:S(2)}) %collective-permute-start) | collective-permute-done | bytes 213024 | tf_op jit(solution)/shard_map/ppermute | solution.py:18
  10.8 1.9 %collective-permute-start.1 = (bf16[2,3,208,128]{3,2,1,0:T(8,128)(2,1)S(1)}, bf16[2,3,208,128]{3,2,1,0:T(8,128)(2,1)S(1)}, u32[]{:S(2)}, u32[]{:S(2)}) collective-permute-start(bf16[2,3,208,128]{3,2,1,0:T(8,128)(2,1)S(1)} %get-tuple-element.43), channel_id=1, source_target_pairs={{0,2},{2,0},{4,6},{6,4},{1,3},{3,1},{5,7},{7,5},{8,10},{10,8},{12,... | collective-permute-start | bytes 958472 | tf_op jit(solution)/shard_map/ppermute | solution.py:208
  12.7 0.7 %collective-permute-start.2 = (bf16[2,3,208,128]{3,2,1,0:T(8,128)(2,1)S(1)}, bf16[2,3,208,128]{3,2,1,0:T(8,128)(2,1)S(1)}, u32[]{:S(2)}, u32[]{:S(2)}) collective-permute-start(bf16[2,3,208,128]{3,2,1,0:T(8,128)(2,1)S(1)} %get-tuple-element.44), channel_id=1, source_target_pairs={{2,4},{4,2},{3,5},{5,3},{10,12},{12,10},{11,13},{13,11},{18,20},{2... | collective-permute-start | bytes 958472 | tf_op jit(solution)/shard_map/ppermute | solution.py:206
  13.4 3.4 %near_inner_rest.1.before = f32[9,64,384]{2,1,0:T(8,128)S(1)} custom-call(s32[216]{0:T(256)S(1)} %reshape.47.near, f32[9,8,128]{2,1,0:T(8,128)S(1)} %get-tuple-element.22.own, bf16[8,208,128]{2,1,0:T(8,128)(2,1)S(1)} %get-tuple-element.23.blocks, f32[9,64,384]{2,1,0:T(8,128)S(1)} %near_inner.1.before), custom_call_target="tpu_custom_call" | custom-call | flops 4000000000 | bytes 4194304 | tf_op jit(solution)/shard_map/near_inner_rest/pallas_call | solution.py:605
  16.8 2.8 %collective-permute-done.1 = bf16[2,3,208,128]{3,2,1,0:T(8,128)(2,1)S(1)} collective-permute-done((bf16[2,3,208,128]{3,2,1,0:T(8,128)(2,1)S(1)}, bf16[2,3,208,128]{3,2,1,0:T(8,128)(2,1)S(1)}, u32[]{:S(2)}, u32[]{:S(2)}) %collective-permute-start.1) | collective-permute-done | bytes 319520 | tf_op jit(solution)/shard_map/ppermute | solution.py:208
  19.6 0.0 collective-permute-done.2
  19.6 0.1 pad_maximum_fusion.1
  19.7 0.1 select_bitcast_fusion
  19.8 0.1 collective-permute-start.3
  19.9 0.7 %collective-permute-start.4 = (bf16[4,3,208,128]{3,2,1,0:T(8,128)(2,1)S(1)}, bf16[4,3,208,128]{3,2,1,0:T(8,128)(2,1)S(1)}, u32[]{:S(2)}, u32[]{:S(2)}) collective-permute-start(bf16[4,3,208,128]{3,2,1,0:T(8,128)(2,1)S(1)} %get-tuple-element.41), channel_id=1, source_target_pairs={{8,16},{16,8},{9,17},{17,9},{10,18},{18,10},{11,19},{19,11},{12,20... | collective-permute-start | bytes 1916936 | tf_op jit(solution)/shard_map/ppermute | solution.py:206
  20.6 1.4 %collective-permute-done.3 = bf16[4,3,208,128]{3,2,1,0:T(8,128)(2,1)S(1)} collective-permute-done((bf16[4,3,208,128]{3,2,1,0:T(8,128)(2,1)S(1)}, bf16[4,3,208,128]{3,2,1,0:T(8,128)(2,1)S(1)}, u32[]{:S(2)}, u32[]{:S(2)}) %collective-permute-start.3) | collective-permute-done | bytes 639008 | tf_op jit(solution)/shard_map/ppermute | solution.py:208
  21.9 0.2 pad_maximum_fusion.blocks
  22.1 0.0 copy-start
  22.1 6.4 %near_z_y_and_x.1.before = f32[9,64,384]{2,1,0:T(8,128)S(1)} custom-call(s32[216]{0:T(256)S(1)} %reshape.47.near, f32[9,8,128]{2,1,0:T(8,128)S(1)} %get-tuple-element.22.own, bf16[36,208,128]{2,1,0:T(8,128)(2,1)S(1)} %pad_maximum_fusion.blocks, f32[9,64,384]{2,1,0:T(8,128)S(1)} %near_inner_rest.1.before), custom_call_target="tpu_custom_call" | custom-call | flops 8999999488 | bytes 4194304 | tf_op jit(solution)/shard_map/near_z_y_and_x/pallas_call | solution.py:605
  28.5 0.0 collective-permute-done.4
  28.5 0.0 copy-done
  28.5 4.8 %near_x_and_box_level.1 = (f32[8,64,384]{2,1,0:T(8,128)S(1)}, f32[8,64,64]{2,1,0:T(8,128)S(1)}, f32[64,64]{1,0:T(8,128)S(1)}, f32[8,64,384]{2,1,0:T(8,128)S(1)}, f32[64,64]{1,0:T(8,128)S(1)}) custom-call(s32[216]{0:T(256)S(1)} %reshape.47.near, f32[9,8,128]{2,1,0:T(8,128)S(1)} %get-tuple-element.22.own, f32[9,64,384]{2,1,0:T(8,128)S(1)} %near_z_y_and_x.1.before, ...), custom_call_target="tpu_custom_call" | custom-call | tf_op jit(solution)/shard_map/near_x_and_box_level/pallas_call | solution.py:627
  33.3 1.5 %collective-permute-start.5 = (f32[1,64,64]{2,1,0:T(8,128)S(1)}, f32[1,64,64]{2,1,0:T(8,128)S(1)}, u32[]{:S(2)}, u32[]{:S(2)}) collective-permute-start(f32[1,64,64]{2,1,0:T(8,128)S(1)} %bitcast.29), channel_id=1, source_target_pairs={{0,1},{1,0},{2,3},{3,2},{4,5},{5,4},{6,7},{7,6},{8,9},{9,8},{10,11... | collective-permute-start | bytes 49160 | tf_op jit(solution)/shard_map/ppermute | solution.py:18
  34.8 2.7 %leaf_factors.1.factors = f32[512,128]{1,0:T(8,128)S(1)} custom-call(f32[8,64,64]{2,1,0:T(8,128)S(1)} %get-tuple-element.30.grams), custom_call_target="tpu_custom_call" | custom-call | flops 3000000000 | bytes 4194304 | tf_op jit(solution)/shard_map/leaf_factors/pallas_call | solution.py:638
  37.5 0.0 collective-permute-done.5
  37.6 7.1 %collective-permute-start.6 = (f32[2,64,64]{2,1,0:T(8,128)S(1)}, f32[2,64,64]{2,1,0:T(8,128)S(1)}, u32[]{:S(2)}, u32[]{:S(2)}) collective-permute-start(f32[2,64,64]{2,1,0:T(8,128)S(1)} %pad_maximum_fusion.5), channel_id=1, source_target_pairs={{0,2},{2,0},{4,6},{6,4},{1,3},{3,1},{5,7},{7,5},{8,10},{10,8},{12,... | collective-permute-start | bytes 98312 | tf_op jit(solution)/shard_map/ppermute | solution.py:18
  44.7 2.6 %leaf_level.1 = (f32[8,64,384]{2,1,0:T(8,128)}, f32[64,512]{1,0:T(8,128)}) custom-call(f32[8,64,384]{2,1,0:T(8,128)S(1)} %get-tuple-element.32.far, f32[512,128]{1,0:T(8,128)S(1)} %leaf_factors.1.factors, f32[8,64,384]{2,1,0:T(8,128)S(1)} %get-tuple-element.34.samples, f32[64,64]{1,0:T(8,128)S(1)} %get-tuple-element.35.box_z), custom_call_target="tpu_custom_call" | custom-call | flops 4000000000 | bytes 4194304 | tf_op jit(solution)/shard_map/leaf_level/pallas_call | solution.py:647
  47.3 0.0 collective-permute-done.6
  47.3 3.4 %collective-permute-start.7 = (f32[4,64,64]{2,1,0:T(8,128)S(1)}, f32[4,64,64]{2,1,0:T(8,128)S(1)}, u32[]{:S(2)}, u32[]{:S(2)}) collective-permute-start(f32[4,64,64]{2,1,0:T(8,128)S(1)} %pad_maximum_fusion.4), channel_id=1, source_target_pairs={{0,8},{8,0},{16,24},{24,16},{1,9},{9,1},{17,25},{25,17},{2,10},{10... | collective-permute-start | bytes 196616 | tf_op jit(solution)/shard_map/ppermute | solution.py:18
  50.7 1.0 %collective-permute-done.7 = f32[4,64,64]{2,1,0:T(8,128)S(1)} collective-permute-done((f32[4,64,64]{2,1,0:T(8,128)S(1)}, f32[4,64,64]{2,1,0:T(8,128)S(1)}, u32[]{:S(2)}, u32[]{:S(2)}) %collective-permute-start.7) | collective-permute-done | bytes 65568 | tf_op jit(solution)/shard_map/ppermute | solution.py:18
  51.7 3.8 %group_level.1 = f32[8,64,384]{2,1,0:T(8,128)} custom-call(f32[8,64,64]{2,1,0:T(8,128)S(1)} %pad_maximum_fusion.3.factors, f32[8,64,384]{2,1,0:T(8,128)S(1)} %get-tuple-element.34.samples, f32[64,64]{1,0:T(8,128)S(1)} %get-tuple-element.35.box_z), custom_call_target="tpu_custom_call" | custom-call | tf_op jit(solution)/shard_map/group_level/pallas_call | solution.py:658
  (5 shorter events, 0.1 us)
Async XLA Ops:
  1.3 1.0 %copy-start.1 = (bf16[2,2,2,64,384]{4,3,2,1,0:T(8,128)(2,1)S(1)}, bf16[2,2,2,64,384]{4,3,2,1,0:T(8,128)(2,1)}, u32[]{:S(2)}) copy-start(bf16[2,2,2,64,384]{4,3,2,1,0:T(8,128)(2,1)} %param.5) | copy-start | bytes 1179652
  2.4 8.3 %collective-permute-start = (bf16[4,208,128]{2,1,0:T(8,128)(2,1)S(1)}, bf16[4,208,128]{2,1,0:T(8,128)(2,1)S(1)}, u32[]{:S(2)}, u32[]{:S(2)}) collective-permute-start(bf16[4,208,128]{2,1,0:T(8,128)(2,1)S(1)} %get-tuple-element.24), channel_id=1, source_target_pairs={{0,1},{1,0},{2,3},{3,2},{4,5},{5,4},{6,7},{7,6},{8,9},{9,8},{10,11... | collective-permute-start | bytes 638984 | tf_op jit(solution)/shard_map/ppermute | solution.py:18
  10.8 8.8 %collective-permute-start.1 = (bf16[2,3,208,128]{3,2,1,0:T(8,128)(2,1)S(1)}, bf16[2,3,208,128]{3,2,1,0:T(8,128)(2,1)S(1)}, u32[]{:S(2)}, u32[]{:S(2)}) collective-permute-start(bf16[2,3,208,128]{3,2,1,0:T(8,128)(2,1)S(1)} %get-tuple-element.43), channel_id=1, source_target_pairs={{0,2},{2,0},{4,6},{6,4},{1,3},{3,1},{5,7},{7,5},{8,10},{10,8},{12,... | collective-permute-start | bytes 958472 | tf_op jit(solution)/shard_map/ppermute | solution.py:208
  12.7 6.9 %collective-permute-start.2 = (bf16[2,3,208,128]{3,2,1,0:T(8,128)(2,1)S(1)}, bf16[2,3,208,128]{3,2,1,0:T(8,128)(2,1)S(1)}, u32[]{:S(2)}, u32[]{:S(2)}) collective-permute-start(bf16[2,3,208,128]{3,2,1,0:T(8,128)(2,1)S(1)} %get-tuple-element.44), channel_id=1, source_target_pairs={{2,4},{4,2},{3,5},{5,3},{10,12},{12,10},{11,13},{13,11},{18,20},{2... | collective-permute-start | bytes 958472 | tf_op jit(solution)/shard_map/ppermute | solution.py:206
  19.8 2.1 %collective-permute-start.3 = (bf16[4,3,208,128]{3,2,1,0:T(8,128)(2,1)S(1)}, bf16[4,3,208,128]{3,2,1,0:T(8,128)(2,1)S(1)}, u32[]{:S(2)}, u32[]{:S(2)}) collective-permute-start(bf16[4,3,208,128]{3,2,1,0:T(8,128)(2,1)S(1)} %get-tuple-element.42), channel_id=1, source_target_pairs={{0,8},{8,0},{16,24},{24,16},{1,9},{9,1},{17,25},{25,17},{2,10},{10... | collective-permute-start | bytes 1916936 | tf_op jit(solution)/shard_map/ppermute | solution.py:208
  19.9 8.7 %collective-permute-start.4 = (bf16[4,3,208,128]{3,2,1,0:T(8,128)(2,1)S(1)}, bf16[4,3,208,128]{3,2,1,0:T(8,128)(2,1)S(1)}, u32[]{:S(2)}, u32[]{:S(2)}) collective-permute-start(bf16[4,3,208,128]{3,2,1,0:T(8,128)(2,1)S(1)} %get-tuple-element.41), channel_id=1, source_target_pairs={{8,16},{16,8},{9,17},{17,9},{10,18},{18,10},{11,19},{19,11},{12,20... | collective-permute-start | bytes 1916936 | tf_op jit(solution)/shard_map/ppermute | solution.py:206
  22.1 6.4 %copy-start = (f32[2,2,2,64,384]{4,3,2,1,0:T(8,128)S(1)}, f32[2,2,2,64,384]{4,3,2,1,0:T(8,128)}, u32[]{:S(2)}) copy-start(f32[2,2,2,64,384]{4,3,2,1,0:T(8,128)} %param.4) | copy-start | bytes 2359300
  33.3 4.2 %collective-permute-start.5 = (f32[1,64,64]{2,1,0:T(8,128)S(1)}, f32[1,64,64]{2,1,0:T(8,128)S(1)}, u32[]{:S(2)}, u32[]{:S(2)}) collective-permute-start(f32[1,64,64]{2,1,0:T(8,128)S(1)} %bitcast.29), channel_id=1, source_target_pairs={{0,1},{1,0},{2,3},{3,2},{4,5},{5,4},{6,7},{7,6},{8,9},{9,8},{10,11... | collective-permute-start | bytes 49160 | tf_op jit(solution)/shard_map/ppermute | solution.py:18
  37.6 9.7 %collective-permute-start.6 = (f32[2,64,64]{2,1,0:T(8,128)S(1)}, f32[2,64,64]{2,1,0:T(8,128)S(1)}, u32[]{:S(2)}, u32[]{:S(2)}) collective-permute-start(f32[2,64,64]{2,1,0:T(8,128)S(1)} %pad_maximum_fusion.5), channel_id=1, source_target_pairs={{0,2},{2,0},{4,6},{6,4},{1,3},{3,1},{5,7},{7,5},{8,10},{10,8},{12,... | collective-permute-start | bytes 98312 | tf_op jit(solution)/shard_map/ppermute | solution.py:18
  47.3 4.4 %collective-permute-start.7 = (f32[4,64,64]{2,1,0:T(8,128)S(1)}, f32[4,64,64]{2,1,0:T(8,128)S(1)}, u32[]{:S(2)}, u32[]{:S(2)}) collective-permute-start(f32[4,64,64]{2,1,0:T(8,128)S(1)} %pad_maximum_fusion.4), channel_id=1, source_target_pairs={{0,8},{8,0},{16,24},{24,16},{1,9},{9,1},{17,25},{25,17},{2,10},{10... | collective-permute-start | bytes 196616 | tf_op jit(solution)/shard_map/ppermute | solution.py:18

commit v6 on v5

--- a/solution.py
+++ b/solution.py
@@ -196,17 +196,22 @@
     return lax.axis_index(axis) % 2
 
 
+def swap_within(low, high, axis):
+    pairs = [(i, i ^ 1) for i in range(lax.axis_size(axis))]
+    return lax.ppermute(jnp.where(parity(axis) == 0, high, low), axis, pairs)
+
+
+def swap_across(low, high, axis):
+    size = lax.axis_size(axis)
+    if size == 2:
+        return []
+    across = [(i, i + 1) for i in range(1, size - 1, 2)]
+    across = across + [(j, i) for i, j in across]
+    return [lax.ppermute(jnp.where(parity(axis) == 0, low, high), axis, across)]
+
+
 def to_neighbours(low, high, axis):
-    size = lax.axis_size(axis)
-    even = parity(axis) == 0
-    received = []
-    if size > 2:
-        across = [(i, i + 1) for i in range(1, size - 1, 2)]
-        across = across + [(j, i) for i, j in across]
-        received.append(lax.ppermute(jnp.where(even, low, high), axis, across))
-    pairs = [(i, i ^ 1) for i in range(size)]
-    received.append(lax.ppermute(jnp.where(even, high, low), axis, pairs))
-    return received[::-1]
+    return [swap_within(low, high, axis)] + swap_across(low, high, axis)
 
 
 def halo_count(axis):
@@ -231,10 +236,12 @@
                 stages[3].append((a, k, y * depth + z, sides, True))
             elif at[0] == 2:
                 continue
-            elif sides:
+            elif y == 2:
                 stages[2].append((a, k, (x * wide + y) * depth + z, sides, False))
+            elif sides or a * 2 >= SIDE**3:
+                stages[1].append((a, k, (x * SIDE + y) * depth + z, sides, False))
             else:
-                stages[a * 2 // SIDE**3].append((a, k, leaf_index(x, y, z), sides, False))
+                stages[0].append((a, k, leaf_index(x, y, z), sides, False))
     return stages
 
 
@@ -443,7 +450,7 @@
 
 def cost(microseconds):
     return pl.CostEstimate(
-        flops=microseconds * 1000 * 1000 * 1000, bytes_accessed=4 * 1024 * 1024, transcendentals=0
+        flops=microseconds * 1000 * 1000 * 1000, bytes_accessed=1024, transcendentals=0
     )
 
 
@@ -615,15 +622,20 @@
     total = add_stage((halos, [(stages[0], 0, None)]), packed, None, "near_inner", 4)
     extended, total = lax.optimization_barrier((extended, total))
     y_halos = to_neighbours(extended[:, 0], extended[:, 1], "gy")
-    total = add_stage((halos, [(stages[1], 0, None)]), packed, total, "near_inner_rest", 4)
+    stage = (halos, [(stages[1], 0, None)])
+    blocks = extended.reshape((-1,) + block)
+    total = add_stage(stage, blocks, total, "near_inner_and_z", 6)
     wide = join([extended] + [h[:, None] for h in y_halos], 1)
     wide, total = lax.optimization_barrier((wide, total))
-    x_halos = to_neighbours(wide[0], wide[1], "gx")
-    stage = (halos, [(stages[2], 0, None), (stages[3], SIDE * column, True)])
-    blocks = join(flat([wide, x_halos[0]]), 0)
-    total = add_stage(stage, blocks, total, "near_z_y_and_x", 9)
+    parts = flat(swap_across(wide[0], wide[1], "gx"))
+    stage = (halos, [(stages[2], 0, None)])
+    total = add_stage(stage, wide.reshape((-1,) + block), total, "near_y", 0)
+    half = wide.shape[1] // 2
+    blocks = [swap_within(part[0], part[1], "gx") for part in (wide[:, :half], wide[:, half:])]
+    blocks = join(flat(blocks), 0)
+    stage = (halos, [(stages[3], 0, True)])
+    total = add_stage(stage, blocks, total, "near_x_within", 0)
     stage = (halos, [(stages[3], 0, False)])
-    parts = flat(x_halos[1:])
     far, grams, factor, samples, box_z = pl.pallas_call(
         functools.partial(last_kernel, stage),
         out_shape=(whole, squares, square, whole, square),

time: 55.8 us -> 56.2 us (level)
  waiting for transfers between devices: 6.26 us -> 3.18 us
  starting transfers between devices: 18.3 us -> 20.1 us
  Pallas kernels: 27.3 us -> 28.9 us
    ppermute x4 -> x5, waiting for transfers between devices: 4.17 us -> 1.08 us  [the longest x3 1.07 us: swap_within(): return lax.ppermute(jnp.where(parity(axis) == 0, high, low), axis, pairs)]
    ppermute x4 -> x5, starting transfers between devices: 3.3 us -> 6.09 us  [the longest x3 4.72 us: swap_within(): return lax.ppermute(jnp.where(parity(axis) == 0, high, low), axis, pairs)]
    pallas_call x3 -> x4, Pallas kernels: 13.2 us -> 14.8 us  [add_stage(): pl.pallas_call(functools.partial(kernel, stage), out_shape=sums, in_specs...]
    ppermute x4, starting transfers between devices: 15 us -> 14 us  [from_partner(): lax.ppermute(x, axis, [(i, i ^ 1 << distance) for i in range(lax.axis_siz...]
  transfers between devices with their start and end apart: 8 -> 9, of which waited for: 4 -> 3; matrix products, arithmetic and copies ran while one was open for 2% -> 2% of each run, Pallas kernels for 33% -> 36%
where the time goes in v6:
time: 56.2 us; the launch traced here: 55.9 us
  Pallas kernels  28.9 us (51%)
  starting transfers between devices  20.1 us (36%)
  waiting for transfers between devices  3.18 us (6%)
  local copies, waits for them, and re-layouts  2.51 us (4%)
  between operations  0.81 us (1%)
    pallas_call x4, Pallas kernels, add_stage(): pl.pallas_call(functools.partial(kernel, stage), out_shape=sums, in_specs...  14.8 us
    ppermute x4, starting transfers between devices, from_partner(): lax.ppermute(x, axis, [(i, i ^ 1 << distance) for i in range(lax.axis_siz...  14 us
    pallas_call x1, Pallas kernels, body(): pl.pallas_call(functools.partial(last_kernel, stage), out_shape=(whole, s...  4.8 us
    ppermute x3, starting transfers between devices, swap_within(): return lax.ppermute(jnp.where(parity(axis) == 0, high, low), axis, pairs)  4.72 us
    pallas_call x1, Pallas kernels, body(): pl.pallas_call(group_kernel, out_shape=whole, scratch_shapes=[single_scra...  3.85 us
    pallas_call x1, Pallas kernels, body(): pl.pallas_call(leaf_factors, out_shape=like((rank * count, 2 * rank), jnp...  2.71 us
    pallas_call x1, Pallas kernels, body(): pl.pallas_call(leaf_kernel, out_shape=(whole, like((rank, count * rank),...  2.63 us
    ppermute x4, waiting for transfers between devices, from_partner(): lax.ppermute(x, axis, [(i, i ^ 1 << distance) for i in range(lax.axis_siz...  2.1 us
  transfers between devices with their start and end apart: 9, of which 3 were waited for; matrix products, arithmetic and copies ran while one was open for 2% of the time, Pallas kernels for 36%

profile of v6, /device:TPU:0, one launch (start us, length us, event | category | flops | bytes accessed | tf_op | source)
XLA Modules:
  0.0 55.9 jit_solution(4492873468991070498)
XLA Ops:
  0.6 0.7 %copy.7 = bf16[2,2,2,3,128]{4,3,2,1,0:T(4,128)(2,1)S(1)} copy(bf16[2,2,2,3,128]{4,2,3,1,0:T(2,128)(2,1)} %param.6) | data formatting | bytes 12288 | tf_op args[2]
  1.3 0.0 copy-start.1
  1.3 1.0 %copy-done.1 = bf16[2,2,2,64,384]{4,3,2,1,0:T(8,128)(2,1)S(1)} copy-done((bf16[2,2,2,64,384]{4,3,2,1,0:T(8,128)(2,1)S(1)}, bf16[2,2,2,64,384]{4,3,2,1,0:T(8,128)(2,1)}, u32[]{:S(2)}) %copy-start.1) | copy-done | bytes 393240
  2.3 0.1 pack.1
  2.4 3.0 %collective-permute-start = (bf16[4,208,128]{2,1,0:T(8,128)(2,1)S(1)}, bf16[4,208,128]{2,1,0:T(8,128)(2,1)S(1)}, u32[]{:S(2)}, u32[]{:S(2)}) collective-permute-start(bf16[4,208,128]{2,1,0:T(8,128)(2,1)S(1)} %get-tuple-element.24), channel_id=1, source_target_pairs={{0,1},{1,0},{2,3},{3,2},{4,5},{5,4},{6,7},{7,6},{8,9},{9,8},{10,11... | collective-permute-start | bytes 638984 | tf_op jit(solution)/shard_map/ppermute | solution.py:18
  5.5 0.8 %reshape.55.near = s32[216]{0:T(256)S(1)} reshape(s32[2,2,2,27]{3,2,1,0:T(2,128)} %param.7) | data formatting | bytes 1728 | tf_op jit(solution)/shard_map/reshape | solution.py:577
  6.2 3.4 %near_inner.1.before = f32[9,64,384]{2,1,0:T(8,128)S(1)} custom-call(s32[216]{0:T(256)S(1)} %reshape.55.near, f32[9,8,128]{2,1,0:T(8,128)S(1)} %get-tuple-element.22.own, bf16[8,208,128]{2,1,0:T(8,128)(2,1)S(1)} %get-tuple-element.23.blocks), custom_call_target="tpu_custom_call" | custom-call | flops 4000000000 | bytes 1024 | tf_op jit(solution)/shard_map/near_inner/pallas_call | solution.py:612
  9.6 1.1 %collective-permute-done = bf16[4,208,128]{2,1,0:T(8,128)(2,1)S(1)} collective-permute-done((bf16[4,208,128]{2,1,0:T(8,128)(2,1)S(1)}, bf16[4,208,128]{2,1,0:T(8,128)(2,1)S(1)}, u32[]{:S(2)}, u32[]{:S(2)}) %collective-permute-start) | collective-permute-done | bytes 213024 | tf_op jit(solution)/shard_map/ppermute | solution.py:18
  10.9 1.9 %collective-permute-start.1 = (bf16[2,3,208,128]{3,2,1,0:T(8,128)(2,1)S(1)}, bf16[2,3,208,128]{3,2,1,0:T(8,128)(2,1)S(1)}, u32[]{:S(2)}, u32[]{:S(2)}) collective-permute-start(bf16[2,3,208,128]{3,2,1,0:T(8,128)(2,1)S(1)} %get-tuple-element.43), channel_id=1, source_target_pairs={{0,2},{2,0},{4,6},{6,4},{1,3},{3,1},{5,7},{7,5},{8,10},{10,8},{12,... | collective-permute-start | bytes 958472 | tf_op jit(solution)/shard_map/ppermute | solution.py:201
  12.7 0.7 %collective-permute-start.2 = (bf16[2,3,208,128]{3,2,1,0:T(8,128)(2,1)S(1)}, bf16[2,3,208,128]{3,2,1,0:T(8,128)(2,1)S(1)}, u32[]{:S(2)}, u32[]{:S(2)}) collective-permute-start(bf16[2,3,208,128]{3,2,1,0:T(8,128)(2,1)S(1)} %get-tuple-element.44), channel_id=1, source_target_pairs={{2,4},{4,2},{3,5},{5,3},{10,12},{12,10},{11,13},{13,11},{18,20},{2... | collective-permute-start | bytes 958472 | tf_op jit(solution)/shard_map/ppermute | solution.py:210
  13.4 5.2 %near_inner_and_z.1.before = f32[9,64,384]{2,1,0:T(8,128)S(1)} custom-call(s32[216]{0:T(256)S(1)} %reshape.55.near, f32[9,8,128]{2,1,0:T(8,128)S(1)} %get-tuple-element.22.own, bf16[12,208,128]{2,1,0:T(8,128)(2,1)S(1)} %bitcast.30, f32[9,64,384]{2,1,0:T(8,128)S(1)} %near_inner.1.before), custom_call_target="tpu_custom_call" | custom-call | flops 6000000000 | bytes 1024 | tf_op jit(solution)/shard_map/near_inner_and_z/pallas_call | solution.py:612
  18.6 1.1 %collective-permute-done.1 = bf16[2,3,208,128]{3,2,1,0:T(8,128)(2,1)S(1)} collective-permute-done((bf16[2,3,208,128]{3,2,1,0:T(8,128)(2,1)S(1)}, bf16[2,3,208,128]{3,2,1,0:T(8,128)(2,1)S(1)}, u32[]{:S(2)}, u32[]{:S(2)}) %collective-permute-start.1) | collective-permute-done | bytes 319520 | tf_op jit(solution)/shard_map/ppermute | solution.py:201
  19.7 0.0 collective-permute-done.2
  19.7 0.1 pad_maximum_fusion
  19.7 0.1 select_bitcast_fusion
  19.8 0.7 %collective-permute-start.5 = (bf16[4,3,208,128]{3,2,1,0:T(8,128)(2,1)S(1)}, bf16[4,3,208,128]{3,2,1,0:T(8,128)(2,1)S(1)}, u32[]{:S(2)}, u32[]{:S(2)}) collective-permute-start(bf16[4,3,208,128]{3,2,1,0:T(8,128)(2,1)S(1)} %select_bitcast_fusion), channel_id=1, source_target_pairs={{8,16},{16,8},{9,17},{17,9},{10,18},{18,10},{11,19},{19,11},{12,20... | collective-permute-start | bytes 1916936 | tf_op jit(solution)/shard_map/ppermute | solution.py:210
  20.5 0.1 select_bitcast_fusion.2
  20.6 2.8 %collective-permute-start.3 = (bf16[2,3,208,128]{3,2,1,0:T(8,128)(2,1)S(1)}, bf16[2,3,208,128]{3,2,1,0:T(8,128)(2,1)S(1)}, u32[]{:S(2)}, u32[]{:S(2)}) collective-permute-start(bf16[2,3,208,128]{3,2,1,0:T(8,128)(2,1)S(1)} %get-tuple-element.41), channel_id=1, source_target_pairs={{0,8},{8,0},{16,24},{24,16},{1,9},{9,1},{17,25},{25,17},{2,10},{10... | collective-permute-start | bytes 958472 | tf_op jit(solution)/shard_map/ppermute | solution.py:201
  23.4 0.1 collective-permute-start.4
  23.5 2.7 %near_y.1.before = f32[9,64,384]{2,1,0:T(8,128)S(1)} custom-call(s32[216]{0:T(256)S(1)} %reshape.55.near, f32[9,8,128]{2,1,0:T(8,128)S(1)} %get-tuple-element.22.own, bf16[24,208,128]{2,1,0:T(8,128)(2,1)S(1)} %bitcast.28, f32[9,64,384]{2,1,0:T(8,128)S(1)} %near_inner_and_z.1.before), custom_call_target="tpu_custom_call" | custom-call | bytes 1024 | tf_op jit(solution)/shard_map/near_y/pallas_call | solution.py:612
  26.2 0.0 collective-permute-done.3
  26.2 0.0 collective-permute-done.4
  26.2 0.1 pad_maximum_fusion.2.blocks
  26.3 0.0 copy-start
  26.3 3.5 %near_x_within.1.before = f32[9,64,384]{2,1,0:T(8,128)S(1)} custom-call(s32[216]{0:T(256)S(1)} %reshape.55.near, f32[9,8,128]{2,1,0:T(8,128)S(1)} %get-tuple-element.22.own, bf16[12,208,128]{2,1,0:T(8,128)(2,1)S(1)} %pad_maximum_fusion.2.blocks, f32[9,64,384]{2,1,0:T(8,128)S(1)} %near_y.1.before), custom_call_target="tpu_custom_call" | custom-call | bytes 1024 | tf_op jit(solution)/shard_map/near_x_within/pallas_call | solution.py:612
  29.8 0.0 collective-permute-done.5
  29.8 0.0 copy-done
  29.9 4.8 %near_x_and_box_level.1 = (f32[8,64,384]{2,1,0:T(8,128)S(1)}, f32[8,64,64]{2,1,0:T(8,128)S(1)}, f32[64,64]{1,0:T(8,128)S(1)}, f32[8,64,384]{2,1,0:T(8,128)S(1)}, f32[64,64]{1,0:T(8,128)S(1)}) custom-call(s32[216]{0:T(256)S(1)} %reshape.55.near, f32[9,8,128]{2,1,0:T(8,128)S(1)} %get-tuple-element.22.own, f32[9,64,384]{2,1,0:T(8,128)S(1)} %near_x_within.1.before, ...), custom_call_target="tpu_custom_call" | custom-call | tf_op jit(solution)/shard_map/near_x_and_box_level/pallas_call | solution.py:639
  34.7 2.4 %collective-permute-start.6 = (f32[1,64,64]{2,1,0:T(8,128)S(1)}, f32[1,64,64]{2,1,0:T(8,128)S(1)}, u32[]{:S(2)}, u32[]{:S(2)}) collective-permute-start(f32[1,64,64]{2,1,0:T(8,128)S(1)} %bitcast.35), channel_id=1, source_target_pairs={{0,1},{1,0},{2,3},{3,2},{4,5},{5,4},{6,7},{7,6},{8,9},{9,8},{10,11... | collective-permute-start | bytes 49160 | tf_op jit(solution)/shard_map/ppermute | solution.py:18
  37.1 2.7 %leaf_factors.1.factors = f32[512,128]{1,0:T(8,128)S(1)} custom-call(f32[8,64,64]{2,1,0:T(8,128)S(1)} %get-tuple-element.30.grams), custom_call_target="tpu_custom_call" | custom-call | flops 3000000000 | bytes 1024 | tf_op jit(solution)/shard_map/leaf_factors/pallas_call | solution.py:650
  39.8 0.0 collective-permute-done.6
  39.8 6.3 %collective-permute-start.7 = (f32[2,64,64]{2,1,0:T(8,128)S(1)}, f32[2,64,64]{2,1,0:T(8,128)S(1)}, u32[]{:S(2)}, u32[]{:S(2)}) collective-permute-start(f32[2,64,64]{2,1,0:T(8,128)S(1)} %pad_maximum_fusion.5), channel_id=1, source_target_pairs={{0,2},{2,0},{4,6},{6,4},{1,3},{3,1},{5,7},{7,5},{8,10},{10,8},{12,... | collective-permute-start | bytes 98312 | tf_op jit(solution)/shard_map/ppermute | solution.py:18
  46.1 2.6 %leaf_level.1 = (f32[8,64,384]{2,1,0:T(8,128)}, f32[64,512]{1,0:T(8,128)}) custom-call(f32[8,64,384]{2,1,0:T(8,128)S(1)} %get-tuple-element.32.far, f32[512,128]{1,0:T(8,128)S(1)} %leaf_factors.1.factors, f32[8,64,384]{2,1,0:T(8,128)S(1)} %get-tuple-element.34.samples, f32[64,64]{1,0:T(8,128)S(1)} %get-tuple-element.35.box_z), custom_call_target="tpu_custom_call" | custom-call | flops 4000000000 | bytes 1024 | tf_op jit(solution)/shard_map/leaf_level/pallas_call | solution.py:659
  48.7 0.0 collective-permute-done.7
  48.8 2.3 %collective-permute-start.8 = (f32[4,64,64]{2,1,0:T(8,128)S(1)}, f32[4,64,64]{2,1,0:T(8,128)S(1)}, u32[]{:S(2)}, u32[]{:S(2)}) collective-permute-start(f32[4,64,64]{2,1,0:T(8,128)S(1)} %pad_maximum_fusion.4), channel_id=1, source_target_pairs={{0,8},{8,0},{16,24},{24,16},{1,9},{9,1},{17,25},{25,17},{2,10},{10... | collective-permute-start | bytes 196616 | tf_op jit(solution)/shard_map/ppermute | solution.py:18
  51.1 1.0 %collective-permute-done.8 = f32[4,64,64]{2,1,0:T(8,128)S(1)} collective-permute-done((f32[4,64,64]{2,1,0:T(8,128)S(1)}, f32[4,64,64]{2,1,0:T(8,128)S(1)}, u32[]{:S(2)}, u32[]{:S(2)}) %collective-permute-start.8) | collective-permute-done | bytes 65568 | tf_op jit(solution)/shard_map/ppermute | solution.py:18
  52.1 3.8 %group_level.1 = f32[8,64,384]{2,1,0:T(8,128)} custom-call(f32[8,64,64]{2,1,0:T(8,128)S(1)} %pad_maximum_fusion.3.factors, f32[8,64,384]{2,1,0:T(8,128)S(1)} %get-tuple-element.34.samples, f32[64,64]{1,0:T(8,128)S(1)} %get-tuple-element.35.box_z), custom_call_target="tpu_custom_call" | custom-call | tf_op jit(solution)/shard_map/group_level/pallas_call | solution.py:670
  (6 shorter events, 0.2 us)
Async XLA Ops:
  1.3 1.0 %copy-start.1 = (bf16[2,2,2,64,384]{4,3,2,1,0:T(8,128)(2,1)S(1)}, bf16[2,2,2,64,384]{4,3,2,1,0:T(8,128)(2,1)}, u32[]{:S(2)}) copy-start(bf16[2,2,2,64,384]{4,3,2,1,0:T(8,128)(2,1)} %param.5) | copy-start | bytes 1179652
  2.4 8.3 %collective-permute-start = (bf16[4,208,128]{2,1,0:T(8,128)(2,1)S(1)}, bf16[4,208,128]{2,1,0:T(8,128)(2,1)S(1)}, u32[]{:S(2)}, u32[]{:S(2)}) collective-permute-start(bf16[4,208,128]{2,1,0:T(8,128)(2,1)S(1)} %get-tuple-element.24), channel_id=1, source_target_pairs={{0,1},{1,0},{2,3},{3,2},{4,5},{5,4},{6,7},{7,6},{8,9},{9,8},{10,11... | collective-permute-start | bytes 638984 | tf_op jit(solution)/shard_map/ppermute | solution.py:18
  10.9 8.8 %collective-permute-start.1 = (bf16[2,3,208,128]{3,2,1,0:T(8,128)(2,1)S(1)}, bf16[2,3,208,128]{3,2,1,0:T(8,128)(2,1)S(1)}, u32[]{:S(2)}, u32[]{:S(2)}) collective-permute-start(bf16[2,3,208,128]{3,2,1,0:T(8,128)(2,1)S(1)} %get-tuple-element.43), channel_id=1, source_target_pairs={{0,2},{2,0},{4,6},{6,4},{1,3},{3,1},{5,7},{7,5},{8,10},{10,8},{12,... | collective-permute-start | bytes 958472 | tf_op jit(solution)/shard_map/ppermute | solution.py:201
  12.7 6.9 %collective-permute-start.2 = (bf16[2,3,208,128]{3,2,1,0:T(8,128)(2,1)S(1)}, bf16[2,3,208,128]{3,2,1,0:T(8,128)(2,1)S(1)}, u32[]{:S(2)}, u32[]{:S(2)}) collective-permute-start(bf16[2,3,208,128]{3,2,1,0:T(8,128)(2,1)S(1)} %get-tuple-element.44), channel_id=1, source_target_pairs={{2,4},{4,2},{3,5},{5,3},{10,12},{12,10},{11,13},{13,11},{18,20},{2... | collective-permute-start | bytes 958472 | tf_op jit(solution)/shard_map/ppermute | solution.py:210
  19.8 10.0 %collective-permute-start.5 = (bf16[4,3,208,128]{3,2,1,0:T(8,128)(2,1)S(1)}, bf16[4,3,208,128]{3,2,1,0:T(8,128)(2,1)S(1)}, u32[]{:S(2)}, u32[]{:S(2)}) collective-permute-start(bf16[4,3,208,128]{3,2,1,0:T(8,128)(2,1)S(1)} %select_bitcast_fusion), channel_id=1, source_target_pairs={{8,16},{16,8},{9,17},{17,9},{10,18},{18,10},{11,19},{19,11},{12,20... | collective-permute-start | bytes 1916936 | tf_op jit(solution)/shard_map/ppermute | solution.py:210
  20.6 5.6 %collective-permute-start.3 = (bf16[2,3,208,128]{3,2,1,0:T(8,128)(2,1)S(1)}, bf16[2,3,208,128]{3,2,1,0:T(8,128)(2,1)S(1)}, u32[]{:S(2)}, u32[]{:S(2)}) collective-permute-start(bf16[2,3,208,128]{3,2,1,0:T(8,128)(2,1)S(1)} %get-tuple-element.41), channel_id=1, source_target_pairs={{0,8},{8,0},{16,24},{24,16},{1,9},{9,1},{17,25},{25,17},{2,10},{10... | collective-permute-start | bytes 958472 | tf_op jit(solution)/shard_map/ppermute | solution.py:201
  23.4 2.8 %collective-permute-start.4 = (bf16[2,3,208,128]{3,2,1,0:T(8,128)(2,1)S(1)}, bf16[2,3,208,128]{3,2,1,0:T(8,128)(2,1)S(1)}, u32[]{:S(2)}, u32[]{:S(2)}) collective-permute-start(bf16[2,3,208,128]{3,2,1,0:T(8,128)(2,1)S(1)} %get-tuple-element.42), channel_id=1, source_target_pairs={{0,8},{8,0},{16,24},{24,16},{1,9},{9,1},{17,25},{25,17},{2,10},{10... | collective-permute-start | bytes 958472 | tf_op jit(solution)/shard_map/ppermute | solution.py:201
  26.3 3.6 %copy-start = (f32[2,2,2,64,384]{4,3,2,1,0:T(8,128)S(1)}, f32[2,2,2,64,384]{4,3,2,1,0:T(8,128)}, u32[]{:S(2)}) copy-start(f32[2,2,2,64,384]{4,3,2,1,0:T(8,128)} %param.4) | copy-start | bytes 2359300
  34.7 5.1 %collective-permute-start.6 = (f32[1,64,64]{2,1,0:T(8,128)S(1)}, f32[1,64,64]{2,1,0:T(8,128)S(1)}, u32[]{:S(2)}, u32[]{:S(2)}) collective-permute-start(f32[1,64,64]{2,1,0:T(8,128)S(1)} %bitcast.35), channel_id=1, source_target_pairs={{0,1},{1,0},{2,3},{3,2},{4,5},{5,4},{6,7},{7,6},{8,9},{9,8},{10,11... | collective-permute-start | bytes 49160 | tf_op jit(solution)/shard_map/ppermute | solution.py:18
  39.8 8.9 %collective-permute-start.7 = (f32[2,64,64]{2,1,0:T(8,128)S(1)}, f32[2,64,64]{2,1,0:T(8,128)S(1)}, u32[]{:S(2)}, u32[]{:S(2)}) collective-permute-start(f32[2,64,64]{2,1,0:T(8,128)S(1)} %pad_maximum_fusion.5), channel_id=1, source_target_pairs={{0,2},{2,0},{4,6},{6,4},{1,3},{3,1},{5,7},{7,5},{8,10},{10,8},{12,... | collective-permute-start | bytes 98312 | tf_op jit(solution)/shard_map/ppermute | solution.py:18
  48.8 3.3 %collective-permute-start.8 = (f32[4,64,64]{2,1,0:T(8,128)S(1)}, f32[4,64,64]{2,1,0:T(8,128)S(1)}, u32[]{:S(2)}, u32[]{:S(2)}) collective-permute-start(f32[4,64,64]{2,1,0:T(8,128)S(1)} %pad_maximum_fusion.4), channel_id=1, source_target_pairs={{0,8},{8,0},{16,24},{24,16},{1,9},{9,1},{17,25},{25,17},{2,10},{10... | collective-permute-start | bytes 196616 | tf_op jit(solution)/shard_map/ppermute | solution.py:18

commit v7 on v5

--- a/solution.py
+++ b/solution.py
@@ -284,7 +284,7 @@
 
 
 def spread_offsets(blocks, places, turned, spread):
-    rank3 = blocks.shape[1] - 16
+    rank3 = blocks.shape[1] - 8
     row, lane = positions((128, 384))
     for first in range(0, len(places), 32):
         chunk = places[first : first + 32]
@@ -415,13 +415,13 @@
 
 def pack_kernel(samples, offsets, packed, own, *faces):
     count, rank, leaf_rows = samples.shape
-    filler = jnp.zeros((13, 128), jnp.float32)
+    filler = jnp.zeros((5, 128), jnp.float32)
     for a in range(count):
         for q in range(3):
             packed[a, q * rank : (q + 1) * rank, :] = samples[a, :, q * 128 : (q + 1) * 128]
         rows = jnp.concatenate([offsets[a].astype(jnp.float32), filler], axis=0)
         packed[a, 3 * rank :, :] = rows.astype(jnp.bfloat16)
-        own[a] = rows[:8]
+        own[a] = rows
     own[count] = jnp.zeros_like(own[count])
     planes = [1 - parity("gz"), parity("gz")]
     for face, plane in zip(faces, planes):
@@ -565,7 +565,7 @@
     count = SIDE**3
     halos = [halo_count(axis) for axis in ("gx", "gy", "gz")]
     like = jax.ShapeDtypeStruct
-    block = (3 * rank + 16, 128)
+    block = (3 * rank + 8, 128)
     params = pltpu.CompilerParams(vmem_limit_bytes=VMEM_LIMIT)
     flat_near = near.reshape(count * 27)
     flat_sketch = sketch.reshape(count, rank, leaf_rows)

time: 55.8 us -> 55.1 us (0.987)
  waiting for transfers between devices: 6.26 us -> 4.42 us
  Pallas kernels: 27.3 us -> 28.7 us
    pallas_call x3, Pallas kernels: 13.2 us -> 14.6 us  [add_stage(): pl.pallas_call(functools.partial(kernel, stage), out_shape=sums, in_specs...]
    ppermute x4, waiting for transfers between devices: 2.09 us -> 1.13 us  [from_partner(): lax.ppermute(x, axis, [(i, i ^ 1 << distance) for i in range(lax.axis_siz...]
    ppermute x2, waiting for transfers between devices: 4.16 us -> 3.29 us  [to_neighbours(): received.append(lax.ppermute(jnp.where(even, high, low), axis, pairs))]
  transfers between devices with their start and end apart: 8 -> 8, of which waited for: 4 -> 4; matrix products, arithmetic and copies ran while one was open for 2% -> 2% of each run, Pallas kernels for 33% -> 36%
where the time goes in v7:
time: 55.1 us; the launch traced here: 55 us
  Pallas kernels  28.7 us (52%)
  starting transfers between devices  18.1 us (33%)
  waiting for transfers between devices  4.42 us (8%)
  local copies, waits for them, and re-layouts  2.47 us (4%)
  between operations  0.78 us (1%)
    ppermute x4, starting transfers between devices, from_partner(): lax.ppermute(x, axis, [(i, i ^ 1 << distance) for i in range(lax.axis_siz...  14.8 us
    pallas_call x3, Pallas kernels, add_stage(): pl.pallas_call(functools.partial(kernel, stage), out_shape=sums, in_specs...  14.6 us
    pallas_call x1, Pallas kernels, body(): pl.pallas_call(functools.partial(last_kernel, stage), out_shape=(whole, s...  4.78 us
    pallas_call x1, Pallas kernels, body(): pl.pallas_call(group_kernel, out_shape=whole, scratch_shapes=[single_scra...  3.85 us
    ppermute x2, waiting for transfers between devices, to_neighbours(): received.append(lax.ppermute(jnp.where(even, high, low), axis, pairs))  3.29 us
    pallas_call x1, Pallas kernels, body(): pl.pallas_call(leaf_factors, out_shape=like((rank * count, 2 * rank), jnp...  2.71 us
    pallas_call x1, Pallas kernels, body(): pl.pallas_call(leaf_kernel, out_shape=(whole, like((rank, count * rank),...  2.62 us
    ppermute x2, starting transfers between devices, to_neighbours(): received.append(lax.ppermute(jnp.where(even, high, low), axis, pairs))  1.93 us
  transfers between devices with their start and end apart: 8, of which 4 were waited for; matrix products, arithmetic and copies ran while one was open for 2% of the time, Pallas kernels for 36%

profile of v7, /device:TPU:0, one launch (start us, length us, event | category | flops | bytes accessed | tf_op | source)
XLA Modules:
  0.0 55.0 jit_solution(14755948113620807448)
XLA Ops:
  0.6 0.7 %copy.7 = bf16[2,2,2,3,128]{4,3,2,1,0:T(4,128)(2,1)S(1)} copy(bf16[2,2,2,3,128]{4,2,3,1,0:T(2,128)(2,1)} %param.6) | data formatting | bytes 12288 | tf_op args[2]
  1.3 0.0 copy-start.1
  1.3 1.0 %copy-done.1 = bf16[2,2,2,64,384]{4,3,2,1,0:T(8,128)(2,1)S(1)} copy-done((bf16[2,2,2,64,384]{4,3,2,1,0:T(8,128)(2,1)S(1)}, bf16[2,2,2,64,384]{4,3,2,1,0:T(8,128)(2,1)}, u32[]{:S(2)}) %copy-start.1) | copy-done | bytes 393240
  2.3 0.1 pack.1
  2.4 3.0 %collective-permute-start = (bf16[4,200,128]{2,1,0:T(8,128)(2,1)S(1)}, bf16[4,200,128]{2,1,0:T(8,128)(2,1)S(1)}, u32[]{:S(2)}, u32[]{:S(2)}) collective-permute-start(bf16[4,200,128]{2,1,0:T(8,128)(2,1)S(1)} %get-tuple-element.24), channel_id=1, source_target_pairs={{0,1},{1,0},{2,3},{3,2},{4,5},{5,4},{6,7},{7,6},{8,9},{9,8},{10,11... | collective-permute-start | bytes 614408 | tf_op jit(solution)/shard_map/ppermute | solution.py:18
  5.5 0.8 %reshape.47.near = s32[216]{0:T(256)S(1)} reshape(s32[2,2,2,27]{3,2,1,0:T(2,128)} %param.7) | data formatting | bytes 1728 | tf_op jit(solution)/shard_map/reshape | solution.py:570
  6.2 4.2 %near_inner.1.before = f32[9,64,384]{2,1,0:T(8,128)S(1)} custom-call(s32[216]{0:T(256)S(1)} %reshape.47.near, f32[9,8,128]{2,1,0:T(8,128)S(1)} %get-tuple-element.22.own, bf16[8,200,128]{2,1,0:T(8,128)(2,1)S(1)} %get-tuple-element.23.blocks), custom_call_target="tpu_custom_call" | custom-call | flops 4000000000 | bytes 4194304 | tf_op jit(solution)/shard_map/near_inner/pallas_call | solution.py:605
  10.4 0.1 collective-permute-done
  10.6 1.9 %collective-permute-start.1 = (bf16[2,3,200,128]{3,2,1,0:T(8,128)(2,1)S(1)}, bf16[2,3,200,128]{3,2,1,0:T(8,128)(2,1)S(1)}, u32[]{:S(2)}, u32[]{:S(2)}) collective-permute-start(bf16[2,3,200,128]{3,2,1,0:T(8,128)(2,1)S(1)} %get-tuple-element.43), channel_id=1, source_target_pairs={{0,2},{2,0},{4,6},{6,4},{1,3},{3,1},{5,7},{7,5},{8,10},{10,8},{12,... | collective-permute-start | bytes 921608 | tf_op jit(solution)/shard_map/ppermute | solution.py:208
  12.5 0.7 %collective-permute-start.2 = (bf16[2,3,200,128]{3,2,1,0:T(8,128)(2,1)S(1)}, bf16[2,3,200,128]{3,2,1,0:T(8,128)(2,1)S(1)}, u32[]{:S(2)}, u32[]{:S(2)}) collective-permute-start(bf16[2,3,200,128]{3,2,1,0:T(8,128)(2,1)S(1)} %get-tuple-element.44), channel_id=1, source_target_pairs={{2,4},{4,2},{3,5},{5,3},{10,12},{12,10},{11,13},{13,11},{18,20},{2... | collective-permute-start | bytes 921608 | tf_op jit(solution)/shard_map/ppermute | solution.py:206
  13.2 4.2 %near_inner_rest.1.before = f32[9,64,384]{2,1,0:T(8,128)S(1)} custom-call(s32[216]{0:T(256)S(1)} %reshape.47.near, f32[9,8,128]{2,1,0:T(8,128)S(1)} %get-tuple-element.22.own, bf16[8,200,128]{2,1,0:T(8,128)(2,1)S(1)} %get-tuple-element.23.blocks, f32[9,64,384]{2,1,0:T(8,128)S(1)} %near_inner.1.before), custom_call_target="tpu_custom_call" | custom-call | flops 4000000000 | bytes 4194304 | tf_op jit(solution)/shard_map/near_inner_rest/pallas_call | solution.py:605
  17.3 2.0 %collective-permute-done.1 = bf16[2,3,200,128]{3,2,1,0:T(8,128)(2,1)S(1)} collective-permute-done((bf16[2,3,200,128]{3,2,1,0:T(8,128)(2,1)S(1)}, bf16[2,3,200,128]{3,2,1,0:T(8,128)(2,1)S(1)}, u32[]{:S(2)}, u32[]{:S(2)}) %collective-permute-start.1) | collective-permute-done | bytes 307232 | tf_op jit(solution)/shard_map/ppermute | solution.py:208
  19.3 0.0 collective-permute-done.2
  19.3 0.1 pad_maximum_fusion.1
  19.5 0.1 select_bitcast_fusion
  19.5 0.1 collective-permute-start.3
  19.6 0.7 %collective-permute-start.4 = (bf16[4,3,200,128]{3,2,1,0:T(8,128)(2,1)S(1)}, bf16[4,3,200,128]{3,2,1,0:T(8,128)(2,1)S(1)}, u32[]{:S(2)}, u32[]{:S(2)}) collective-permute-start(bf16[4,3,200,128]{3,2,1,0:T(8,128)(2,1)S(1)} %get-tuple-element.41), channel_id=1, source_target_pairs={{8,16},{16,8},{9,17},{17,9},{10,18},{18,10},{11,19},{19,11},{12,20... | collective-permute-start | bytes 1843208 | tf_op jit(solution)/shard_map/ppermute | solution.py:206
  20.3 1.3 %collective-permute-done.3 = bf16[4,3,200,128]{3,2,1,0:T(8,128)(2,1)S(1)} collective-permute-done((bf16[4,3,200,128]{3,2,1,0:T(8,128)(2,1)S(1)}, bf16[4,3,200,128]{3,2,1,0:T(8,128)(2,1)S(1)}, u32[]{:S(2)}, u32[]{:S(2)}) %collective-permute-start.3) | collective-permute-done | bytes 614432 | tf_op jit(solution)/shard_map/ppermute | solution.py:208
  21.7 0.2 pad_maximum_fusion.blocks
  21.8 0.0 copy-start
  21.8 6.3 %near_z_y_and_x.1.before = f32[9,64,384]{2,1,0:T(8,128)S(1)} custom-call(s32[216]{0:T(256)S(1)} %reshape.47.near, f32[9,8,128]{2,1,0:T(8,128)S(1)} %get-tuple-element.22.own, bf16[36,200,128]{2,1,0:T(8,128)(2,1)S(1)} %pad_maximum_fusion.blocks, f32[9,64,384]{2,1,0:T(8,128)S(1)} %near_inner_rest.1.before), custom_call_target="tpu_custom_call" | custom-call | flops 8999999488 | bytes 4194304 | tf_op jit(solution)/shard_map/near_z_y_and_x/pallas_call | solution.py:605
  28.1 0.0 collective-permute-done.4
  28.1 0.0 copy-done
  28.1 4.8 %near_x_and_box_level.1 = (f32[8,64,384]{2,1,0:T(8,128)S(1)}, f32[8,64,64]{2,1,0:T(8,128)S(1)}, f32[64,64]{1,0:T(8,128)S(1)}, f32[8,64,384]{2,1,0:T(8,128)S(1)}, f32[64,64]{1,0:T(8,128)S(1)}) custom-call(s32[216]{0:T(256)S(1)} %reshape.47.near, f32[9,8,128]{2,1,0:T(8,128)S(1)} %get-tuple-element.22.own, f32[9,64,384]{2,1,0:T(8,128)S(1)} %near_z_y_and_x.1.before, ...), custom_call_target="tpu_custom_call" | custom-call | tf_op jit(solution)/shard_map/near_x_and_box_level/pallas_call | solution.py:627
  32.9 1.3 %collective-permute-start.5 = (f32[1,64,64]{2,1,0:T(8,128)S(1)}, f32[1,64,64]{2,1,0:T(8,128)S(1)}, u32[]{:S(2)}, u32[]{:S(2)}) collective-permute-start(f32[1,64,64]{2,1,0:T(8,128)S(1)} %bitcast.29), channel_id=1, source_target_pairs={{0,1},{1,0},{2,3},{3,2},{4,5},{5,4},{6,7},{7,6},{8,9},{9,8},{10,11... | collective-permute-start | bytes 49160 | tf_op jit(solution)/shard_map/ppermute | solution.py:18
  34.3 2.7 %leaf_factors.1.factors = f32[512,128]{1,0:T(8,128)S(1)} custom-call(f32[8,64,64]{2,1,0:T(8,128)S(1)} %get-tuple-element.30.grams), custom_call_target="tpu_custom_call" | custom-call | flops 3000000000 | bytes 4194304 | tf_op jit(solution)/shard_map/leaf_factors/pallas_call | solution.py:638
  37.0 0.0 collective-permute-done.5
  37.0 7.0 %collective-permute-start.6 = (f32[2,64,64]{2,1,0:T(8,128)S(1)}, f32[2,64,64]{2,1,0:T(8,128)S(1)}, u32[]{:S(2)}, u32[]{:S(2)}) collective-permute-start(f32[2,64,64]{2,1,0:T(8,128)S(1)} %pad_maximum_fusion.5), channel_id=1, source_target_pairs={{0,2},{2,0},{4,6},{6,4},{1,3},{3,1},{5,7},{7,5},{8,10},{10,8},{12,... | collective-permute-start | bytes 98312 | tf_op jit(solution)/shard_map/ppermute | solution.py:18
  44.0 2.6 %leaf_level.1 = (f32[8,64,384]{2,1,0:T(8,128)}, f32[64,512]{1,0:T(8,128)}) custom-call(f32[8,64,384]{2,1,0:T(8,128)S(1)} %get-tuple-element.32.far, f32[512,128]{1,0:T(8,128)S(1)} %leaf_factors.1.factors, f32[8,64,384]{2,1,0:T(8,128)S(1)} %get-tuple-element.34.samples, f32[64,64]{1,0:T(8,128)S(1)} %get-tuple-element.35.box_z), custom_call_target="tpu_custom_call" | custom-call | flops 4000000000 | bytes 4194304 | tf_op jit(solution)/shard_map/leaf_level/pallas_call | solution.py:647
  46.7 0.0 collective-permute-done.6
  46.7 3.4 %collective-permute-start.7 = (f32[4,64,64]{2,1,0:T(8,128)S(1)}, f32[4,64,64]{2,1,0:T(8,128)S(1)}, u32[]{:S(2)}, u32[]{:S(2)}) collective-permute-start(f32[4,64,64]{2,1,0:T(8,128)S(1)} %pad_maximum_fusion.4), channel_id=1, source_target_pairs={{0,8},{8,0},{16,24},{24,16},{1,9},{9,1},{17,25},{25,17},{2,10},{10... | collective-permute-start | bytes 196616 | tf_op jit(solution)/shard_map/ppermute | solution.py:18
  50.1 1.0 %collective-permute-done.7 = f32[4,64,64]{2,1,0:T(8,128)S(1)} collective-permute-done((f32[4,64,64]{2,1,0:T(8,128)S(1)}, f32[4,64,64]{2,1,0:T(8,128)S(1)}, u32[]{:S(2)}, u32[]{:S(2)}) %collective-permute-start.7) | collective-permute-done | bytes 65568 | tf_op jit(solution)/shard_map/ppermute | solution.py:18
  51.1 3.8 %group_level.1 = f32[8,64,384]{2,1,0:T(8,128)} custom-call(f32[8,64,64]{2,1,0:T(8,128)S(1)} %pad_maximum_fusion.3.factors, f32[8,64,384]{2,1,0:T(8,128)S(1)} %get-tuple-element.34.samples, f32[64,64]{1,0:T(8,128)S(1)} %get-tuple-element.35.box_z), custom_call_target="tpu_custom_call" | custom-call | tf_op jit(solution)/shard_map/group_level/pallas_call | solution.py:658
  (5 shorter events, 0.1 us)
Async XLA Ops:
  1.3 1.0 %copy-start.1 = (bf16[2,2,2,64,384]{4,3,2,1,0:T(8,128)(2,1)S(1)}, bf16[2,2,2,64,384]{4,3,2,1,0:T(8,128)(2,1)}, u32[]{:S(2)}) copy-start(bf16[2,2,2,64,384]{4,3,2,1,0:T(8,128)(2,1)} %param.5) | copy-start | bytes 1179652
  2.4 8.1 %collective-permute-start = (bf16[4,200,128]{2,1,0:T(8,128)(2,1)S(1)}, bf16[4,200,128]{2,1,0:T(8,128)(2,1)S(1)}, u32[]{:S(2)}, u32[]{:S(2)}) collective-permute-start(bf16[4,200,128]{2,1,0:T(8,128)(2,1)S(1)} %get-tuple-element.24), channel_id=1, source_target_pairs={{0,1},{1,0},{2,3},{3,2},{4,5},{5,4},{6,7},{7,6},{8,9},{9,8},{10,11... | collective-permute-start | bytes 614408 | tf_op jit(solution)/shard_map/ppermute | solution.py:18
  10.6 8.7 %collective-permute-start.1 = (bf16[2,3,200,128]{3,2,1,0:T(8,128)(2,1)S(1)}, bf16[2,3,200,128]{3,2,1,0:T(8,128)(2,1)S(1)}, u32[]{:S(2)}, u32[]{:S(2)}) collective-permute-start(bf16[2,3,200,128]{3,2,1,0:T(8,128)(2,1)S(1)} %get-tuple-element.43), channel_id=1, source_target_pairs={{0,2},{2,0},{4,6},{6,4},{1,3},{3,1},{5,7},{7,5},{8,10},{10,8},{12,... | collective-permute-start | bytes 921608 | tf_op jit(solution)/shard_map/ppermute | solution.py:208
  12.5 6.8 %collective-permute-start.2 = (bf16[2,3,200,128]{3,2,1,0:T(8,128)(2,1)S(1)}, bf16[2,3,200,128]{3,2,1,0:T(8,128)(2,1)S(1)}, u32[]{:S(2)}, u32[]{:S(2)}) collective-permute-start(bf16[2,3,200,128]{3,2,1,0:T(8,128)(2,1)S(1)} %get-tuple-element.44), channel_id=1, source_target_pairs={{2,4},{4,2},{3,5},{5,3},{10,12},{12,10},{11,13},{13,11},{18,20},{2... | collective-permute-start | bytes 921608 | tf_op jit(solution)/shard_map/ppermute | solution.py:206
  19.5 2.1 %collective-permute-start.3 = (bf16[4,3,200,128]{3,2,1,0:T(8,128)(2,1)S(1)}, bf16[4,3,200,128]{3,2,1,0:T(8,128)(2,1)S(1)}, u32[]{:S(2)}, u32[]{:S(2)}) collective-permute-start(bf16[4,3,200,128]{3,2,1,0:T(8,128)(2,1)S(1)} %get-tuple-element.42), channel_id=1, source_target_pairs={{0,8},{8,0},{16,24},{24,16},{1,9},{9,1},{17,25},{25,17},{2,10},{10... | collective-permute-start | bytes 1843208 | tf_op jit(solution)/shard_map/ppermute | solution.py:208
  19.6 8.5 %collective-permute-start.4 = (bf16[4,3,200,128]{3,2,1,0:T(8,128)(2,1)S(1)}, bf16[4,3,200,128]{3,2,1,0:T(8,128)(2,1)S(1)}, u32[]{:S(2)}, u32[]{:S(2)}) collective-permute-start(bf16[4,3,200,128]{3,2,1,0:T(8,128)(2,1)S(1)} %get-tuple-element.41), channel_id=1, source_target_pairs={{8,16},{16,8},{9,17},{17,9},{10,18},{18,10},{11,19},{19,11},{12,20... | collective-permute-start | bytes 1843208 | tf_op jit(solution)/shard_map/ppermute | solution.py:206
  21.8 6.3 %copy-start = (f32[2,2,2,64,384]{4,3,2,1,0:T(8,128)S(1)}, f32[2,2,2,64,384]{4,3,2,1,0:T(8,128)}, u32[]{:S(2)}) copy-start(f32[2,2,2,64,384]{4,3,2,1,0:T(8,128)} %param.4) | copy-start | bytes 2359300
  32.9 4.0 %collective-permute-start.5 = (f32[1,64,64]{2,1,0:T(8,128)S(1)}, f32[1,64,64]{2,1,0:T(8,128)S(1)}, u32[]{:S(2)}, u32[]{:S(2)}) collective-permute-start(f32[1,64,64]{2,1,0:T(8,128)S(1)} %bitcast.29), channel_id=1, source_target_pairs={{0,1},{1,0},{2,3},{3,2},{4,5},{5,4},{6,7},{7,6},{8,9},{9,8},{10,11... | collective-permute-start | bytes 49160 | tf_op jit(solution)/shard_map/ppermute | solution.py:18
  37.0 9.7 %collective-permute-start.6 = (f32[2,64,64]{2,1,0:T(8,128)S(1)}, f32[2,64,64]{2,1,0:T(8,128)S(1)}, u32[]{:S(2)}, u32[]{:S(2)}) collective-permute-start(f32[2,64,64]{2,1,0:T(8,128)S(1)} %pad_maximum_fusion.5), channel_id=1, source_target_pairs={{0,2},{2,0},{4,6},{6,4},{1,3},{3,1},{5,7},{7,5},{8,10},{10,8},{12,... | collective-permute-start | bytes 98312 | tf_op jit(solution)/shard_map/ppermute | solution.py:18
  46.7 4.4 %collective-permute-start.7 = (f32[4,64,64]{2,1,0:T(8,128)S(1)}, f32[4,64,64]{2,1,0:T(8,128)S(1)}, u32[]{:S(2)}, u32[]{:S(2)}) collective-permute-start(f32[4,64,64]{2,1,0:T(8,128)S(1)} %pad_maximum_fusion.4), channel_id=1, source_target_pairs={{0,8},{8,0},{16,24},{24,16},{1,9},{9,1},{17,25},{25,17},{2,10},{10... | collective-permute-start | bytes 196616 | tf_op jit(solution)/shard_map/ppermute | solution.py:18

commit v8 on v7

--- a/solution.py
+++ b/solution.py
@@ -10,6 +10,7 @@
 
 EPSILON = 0.1
 GROUP = 8
+FIRST_LEAVES = 3
 SIDE = 2
 HIGHEST = lax.Precision.HIGHEST
 
@@ -234,7 +235,7 @@
             elif sides:
                 stages[2].append((a, k, (x * wide + y) * depth + z, sides, False))
             else:
-                stages[a * 2 // SIDE**3].append((a, k, leaf_index(x, y, z), sides, False))
+                stages[0 if a < FIRST_LEAVES else 1].append((a, k, leaf_index(x, y, z), sides, False))
     return stages
 
 
@@ -256,22 +257,25 @@
     for a, k, source, sides, across in pairs:
         key = (sides, across)
         if key not in joint:
-            inside, moved, entry = jnp.int32(1), jnp.int32(0), jnp.int32(0)
+            inside, moved, high = jnp.int32(1), jnp.int32(0), jnp.int32(0)
             if across:
                 inside = x_side[1]
-                entry = x_side[0] * (4 * 27 + 18)
+                high = x_side[0]
             steps = {1: depth, 2: 1}
             for side in sides:
                 inside = inside * found[side][0]
                 moved = moved + found[side][1] * steps[side[0]]
-            joint[key] = (inside, moved * (16 * 27) + entry, entry)
-        inside, moved, entry = joint[key]
+            joint[key] = (inside, moved * (16 * 27) + high * (4 * 27 + 18), high)
+        inside, moved, high = joint[key]
+        x, y, z = a // 4, a // 2 % 2, a % 2
         code = jnp.int32((source * 16 + a) * 27 + k)
         if sides or across:
-            taken = near[a * 27 + k + entry] * inside
+            if across:
+                x, k = x + high, k + high * 18
+            taken = near[x, y, z, k] * inside
             code = code + moved
         else:
-            taken = near[a * 27 + k]
+            taken = near[x, y, z, k]
         listed[count] = code
         count = count + taken
     return count
@@ -567,7 +571,6 @@
     like = jax.ShapeDtypeStruct
     block = (3 * rank + 8, 128)
     params = pltpu.CompilerParams(vmem_limit_bytes=VMEM_LIMIT)
-    flat_near = near.reshape(count * 27)
     flat_sketch = sketch.reshape(count, rank, leaf_rows)
     stages = pair_tables(halos)
     faces = halos[2]
@@ -610,7 +613,7 @@
             cost_estimate=cost(time),
             compiler_params=params,
             name=name,
-        )(flat_near, own, blocks, *before)
+        )(near, own, blocks, *before)
 
     total = add_stage((halos, [(stages[0], 0, None)]), packed, None, "near_inner", 4)
     extended, total = lax.optimization_barrier((extended, total))
@@ -632,7 +635,7 @@
         + near_scratch(stage, column),
         compiler_params=params,
         name="near_x_and_box_level",
-    )(flat_near, own, total, flat_sketch, *parts)
+    )(near, own, total, flat_sketch, *parts)
     grouped = factor[None]
     grouped = join([grouped, from_partner(grouped, "gz", 0)], 0)
     factors = pl.pallas_call(

time: 55.1 us -> 55.1 us (level)
    reshape x1 -> x0, local copies, waits for them, and re-layouts: 0.77 us -> none  [body(): flat_near = near.reshape(count * 27)]
    ppermute x4, waiting for transfers between devices: 1.13 us -> 1.88 us  [from_partner(): lax.ppermute(x, axis, [(i, i ^ 1 << distance) for i in range(lax.axis_siz...]
    unnamed x5 -> x7, local copies, waits for them, and re-layouts: 1.7 us -> 2.39 us
    pallas_call x3, Pallas kernels: 14.6 us -> 14.1 us  [add_stage(): pl.pallas_call(functools.partial(kernel, stage), out_shape=sums, in_specs...]
  transfers between devices with their start and end apart: 8 -> 8, of which waited for: 4 -> 4; matrix products, arithmetic and copies ran while one was open for 2% -> 0% of each run, Pallas kernels for 36% -> 36%
where the time goes in v8:
time: 55.1 us; the launch traced here: 54.5 us
  Pallas kernels  28.2 us (51%)
  starting transfers between devices  17.8 us (32%)
  waiting for transfers between devices  4.96 us (9%)
  local copies, waits for them, and re-layouts  2.39 us (4%)
  between operations  0.78 us (1%)
    ppermute x4, starting transfers between devices, from_partner(): lax.ppermute(x, axis, [(i, i ^ 1 << distance) for i in range(lax.axis_siz...  14.5 us
    pallas_call x3, Pallas kernels, add_stage(): pl.pallas_call(functools.partial(kernel, stage), out_shape=sums, in_specs...  14.1 us
    pallas_call x1, Pallas kernels, body(): pl.pallas_call(functools.partial(last_kernel, stage), out_shape=(whole, s...  4.83 us
    pallas_call x1, Pallas kernels, body(): pl.pallas_call(group_kernel, out_shape=whole, scratch_shapes=[single_scra...  3.85 us
    ppermute x2, waiting for transfers between devices, to_neighbours(): received.append(lax.ppermute(jnp.where(even, high, low), axis, pairs))  3.07 us
    pallas_call x1, Pallas kernels, body(): pl.pallas_call(leaf_factors, out_shape=like((rank * count, 2 * rank), jnp...  2.71 us
    pallas_call x1, Pallas kernels, body(): pl.pallas_call(leaf_kernel, out_shape=(whole, like((rank, count * rank),...  2.62 us
    unnamed x7, local copies, waits for them, and re-layouts  2.39 us
  transfers between devices with their start and end apart: 8, of which 4 were waited for; matrix products, arithmetic and copies ran while one was open for 0% of the time, Pallas kernels for 36%

profile of v8, /device:TPU:0, one launch (start us, length us, event | category | flops | bytes accessed | tf_op | source)
XLA Modules:
  0.0 54.5 jit_solution(5095499229980810276)
XLA Ops:
  0.6 0.7 %copy.7 = bf16[2,2,2,3,128]{4,3,2,1,0:T(4,128)(2,1)S(1)} copy(bf16[2,2,2,3,128]{4,2,3,1,0:T(2,128)(2,1)} %param.6) | data formatting | bytes 12288 | tf_op args[2]
  1.3 0.0 copy-start.1
  1.3 1.0 %copy-done.1 = bf16[2,2,2,64,384]{4,3,2,1,0:T(8,128)(2,1)S(1)} copy-done((bf16[2,2,2,64,384]{4,3,2,1,0:T(8,128)(2,1)S(1)}, bf16[2,2,2,64,384]{4,3,2,1,0:T(8,128)(2,1)}, u32[]{:S(2)}) %copy-start.1) | copy-done | bytes 393240
  2.3 0.1 pack.1
  2.4 3.0 %collective-permute-start = (bf16[4,200,128]{2,1,0:T(8,128)(2,1)S(1)}, bf16[4,200,128]{2,1,0:T(8,128)(2,1)S(1)}, u32[]{:S(2)}, u32[]{:S(2)}) collective-permute-start(bf16[4,200,128]{2,1,0:T(8,128)(2,1)S(1)} %get-tuple-element.24), channel_id=1, source_target_pairs={{0,1},{1,0},{2,3},{3,2},{4,5},{5,4},{6,7},{7,6},{8,9},{9,8},{10,11... | collective-permute-start | bytes 614408 | tf_op jit(solution)/shard_map/ppermute | solution.py:19
  5.5 0.0 copy-start.2
  5.5 0.7 %copy-done.2 = s32[2,2,2,27]{3,2,1,0:T(2,128)S(1)} copy-done((s32[2,2,2,27]{3,2,1,0:T(2,128)S(1)}, s32[2,2,2,27]{3,2,1,0:T(2,128)}, u32[]{:S(2)}) %copy-start.2) | copy-done | bytes 888
  6.1 3.5 %near_inner.1.before = f32[9,64,384]{2,1,0:T(8,128)S(1)} custom-call(s32[2,2,2,27]{3,2,1,0:T(2,128)S(1)} %copy-done.2, f32[9,8,128]{2,1,0:T(8,128)S(1)} %get-tuple-element.22.own, bf16[8,200,128]{2,1,0:T(8,128)(2,1)S(1)} %get-tuple-element.23.blocks), custom_call_target="tpu_custom_call" | custom-call | flops 4000000000 | bytes 4194304 | tf_op jit(solution)/shard_map/near_inner/pallas_call | solution.py:608
  9.6 0.9 %collective-permute-done = bf16[4,200,128]{2,1,0:T(8,128)(2,1)S(1)} collective-permute-done((bf16[4,200,128]{2,1,0:T(8,128)(2,1)S(1)}, bf16[4,200,128]{2,1,0:T(8,128)(2,1)S(1)}, u32[]{:S(2)}, u32[]{:S(2)}) %collective-permute-start) | collective-permute-done | bytes 204832 | tf_op jit(solution)/shard_map/ppermute | solution.py:19
  10.5 0.1 pad_maximum_fusion.2
  10.6 1.9 %collective-permute-start.1 = (bf16[2,3,200,128]{3,2,1,0:T(8,128)(2,1)S(1)}, bf16[2,3,200,128]{3,2,1,0:T(8,128)(2,1)S(1)}, u32[]{:S(2)}, u32[]{:S(2)}) collective-permute-start(bf16[2,3,200,128]{3,2,1,0:T(8,128)(2,1)S(1)} %get-tuple-element.43), channel_id=1, source_target_pairs={{0,2},{2,0},{4,6},{6,4},{1,3},{3,1},{5,7},{7,5},{8,10},{10,8},{12,... | collective-permute-start | bytes 921608 | tf_op jit(solution)/shard_map/ppermute | solution.py:209
  12.5 0.7 %collective-permute-start.2 = (bf16[2,3,200,128]{3,2,1,0:T(8,128)(2,1)S(1)}, bf16[2,3,200,128]{3,2,1,0:T(8,128)(2,1)S(1)}, u32[]{:S(2)}, u32[]{:S(2)}) collective-permute-start(bf16[2,3,200,128]{3,2,1,0:T(8,128)(2,1)S(1)} %get-tuple-element.44), channel_id=1, source_target_pairs={{2,4},{4,2},{3,5},{5,3},{10,12},{12,10},{11,13},{13,11},{18,20},{2... | collective-permute-start | bytes 921608 | tf_op jit(solution)/shard_map/ppermute | solution.py:207
  13.2 4.2 %near_inner_rest.1.before = f32[9,64,384]{2,1,0:T(8,128)S(1)} custom-call(s32[2,2,2,27]{3,2,1,0:T(2,128)S(1)} %copy-done.2, f32[9,8,128]{2,1,0:T(8,128)S(1)} %get-tuple-element.22.own, bf16[8,200,128]{2,1,0:T(8,128)(2,1)S(1)} %get-tuple-element.23.blocks, f32[9,64,384]{2,1,0:T(8,128)S(1)} %near_inner.1.before), custom_call_target="tpu_custom_call" | custom-call | flops 4000000000 | bytes 4194304 | tf_op jit(solution)/shard_map/near_inner_rest/pallas_call | solution.py:608
  17.4 1.8 %collective-permute-done.1 = bf16[2,3,200,128]{3,2,1,0:T(8,128)(2,1)S(1)} collective-permute-done((bf16[2,3,200,128]{3,2,1,0:T(8,128)(2,1)S(1)}, bf16[2,3,200,128]{3,2,1,0:T(8,128)(2,1)S(1)}, u32[]{:S(2)}, u32[]{:S(2)}) %collective-permute-start.1) | collective-permute-done | bytes 307232 | tf_op jit(solution)/shard_map/ppermute | solution.py:209
  19.2 0.0 collective-permute-done.2
  19.2 0.1 pad_maximum_fusion.1
  19.3 0.1 select_bitcast_fusion
  19.4 0.1 collective-permute-start.3
  19.5 0.7 %collective-permute-start.4 = (bf16[4,3,200,128]{3,2,1,0:T(8,128)(2,1)S(1)}, bf16[4,3,200,128]{3,2,1,0:T(8,128)(2,1)S(1)}, u32[]{:S(2)}, u32[]{:S(2)}) collective-permute-start(bf16[4,3,200,128]{3,2,1,0:T(8,128)(2,1)S(1)} %get-tuple-element.41), channel_id=1, source_target_pairs={{8,16},{16,8},{9,17},{17,9},{10,18},{18,10},{11,19},{19,11},{12,20... | collective-permute-start | bytes 1843208 | tf_op jit(solution)/shard_map/ppermute | solution.py:207
  20.2 1.3 %collective-permute-done.3 = bf16[4,3,200,128]{3,2,1,0:T(8,128)(2,1)S(1)} collective-permute-done((bf16[4,3,200,128]{3,2,1,0:T(8,128)(2,1)S(1)}, bf16[4,3,200,128]{3,2,1,0:T(8,128)(2,1)S(1)}, u32[]{:S(2)}, u32[]{:S(2)}) %collective-permute-start.3) | collective-permute-done | bytes 614432 | tf_op jit(solution)/shard_map/ppermute | solution.py:209
  21.5 0.2 pad_maximum_fusion.blocks
  21.7 0.0 copy-start
  21.7 6.4 %near_z_y_and_x.1.before = f32[9,64,384]{2,1,0:T(8,128)S(1)} custom-call(s32[2,2,2,27]{3,2,1,0:T(2,128)S(1)} %copy-done.2, f32[9,8,128]{2,1,0:T(8,128)S(1)} %get-tuple-element.22.own, bf16[36,200,128]{2,1,0:T(8,128)(2,1)S(1)} %pad_maximum_fusion.blocks, f32[9,64,384]{2,1,0:T(8,128)S(1)} %near_inner_rest.1.before), custom_call_target="tpu_custom_call" | custom-call | flops 8999999488 | bytes 4194304 | tf_op jit(solution)/shard_map/near_z_y_and_x/pallas_call | solution.py:608
  28.0 0.0 collective-permute-done.4
  28.0 0.0 copy-done
  28.0 4.8 %near_x_and_box_level.1 = (f32[8,64,384]{2,1,0:T(8,128)S(1)}, f32[8,64,64]{2,1,0:T(8,128)S(1)}, f32[64,64]{1,0:T(8,128)S(1)}, f32[8,64,384]{2,1,0:T(8,128)S(1)}, f32[64,64]{1,0:T(8,128)S(1)}) custom-call(s32[2,2,2,27]{3,2,1,0:T(2,128)S(1)} %copy-done.2, f32[9,8,128]{2,1,0:T(8,128)S(1)} %get-tuple-element.22.own, f32[9,64,384]{2,1,0:T(8,128)S(1)} %near_z_y_and_x.1.before, ...), custom_call_target="tpu_custom_call" | custom-call | tf_op jit(solution)/shard_map/near_x_and_box_level/pallas_call | solution.py:630
  32.9 1.5 %collective-permute-start.5 = (f32[1,64,64]{2,1,0:T(8,128)S(1)}, f32[1,64,64]{2,1,0:T(8,128)S(1)}, u32[]{:S(2)}, u32[]{:S(2)}) collective-permute-start(f32[1,64,64]{2,1,0:T(8,128)S(1)} %bitcast.29), channel_id=1, source_target_pairs={{0,1},{1,0},{2,3},{3,2},{4,5},{5,4},{6,7},{7,6},{8,9},{9,8},{10,11... | collective-permute-start | bytes 49160 | tf_op jit(solution)/shard_map/ppermute | solution.py:19
  34.4 2.7 %leaf_factors.1.factors = f32[512,128]{1,0:T(8,128)S(1)} custom-call(f32[8,64,64]{2,1,0:T(8,128)S(1)} %get-tuple-element.30.grams), custom_call_target="tpu_custom_call" | custom-call | flops 3000000000 | bytes 4194304 | tf_op jit(solution)/shard_map/leaf_factors/pallas_call | solution.py:641
  37.1 0.0 collective-permute-done.5
  37.1 7.1 %collective-permute-start.6 = (f32[2,64,64]{2,1,0:T(8,128)S(1)}, f32[2,64,64]{2,1,0:T(8,128)S(1)}, u32[]{:S(2)}, u32[]{:S(2)}) collective-permute-start(f32[2,64,64]{2,1,0:T(8,128)S(1)} %pad_maximum_fusion.5), channel_id=1, source_target_pairs={{0,2},{2,0},{4,6},{6,4},{1,3},{3,1},{5,7},{7,5},{8,10},{10,8},{12,... | collective-permute-start | bytes 98312 | tf_op jit(solution)/shard_map/ppermute | solution.py:19
  44.2 2.6 %leaf_level.1 = (f32[8,64,384]{2,1,0:T(8,128)}, f32[64,512]{1,0:T(8,128)}) custom-call(f32[8,64,384]{2,1,0:T(8,128)S(1)} %get-tuple-element.32.far, f32[512,128]{1,0:T(8,128)S(1)} %leaf_factors.1.factors, f32[8,64,384]{2,1,0:T(8,128)S(1)} %get-tuple-element.34.samples, f32[64,64]{1,0:T(8,128)S(1)} %get-tuple-element.35.box_z), custom_call_target="tpu_custom_call" | custom-call | flops 4000000000 | bytes 4194304 | tf_op jit(solution)/shard_map/leaf_level/pallas_call | solution.py:650
  46.8 0.0 collective-permute-done.6
  46.8 2.9 %collective-permute-start.7 = (f32[4,64,64]{2,1,0:T(8,128)S(1)}, f32[4,64,64]{2,1,0:T(8,128)S(1)}, u32[]{:S(2)}, u32[]{:S(2)}) collective-permute-start(f32[4,64,64]{2,1,0:T(8,128)S(1)} %pad_maximum_fusion.4), channel_id=1, source_target_pairs={{0,8},{8,0},{16,24},{24,16},{1,9},{9,1},{17,25},{25,17},{2,10},{10... | collective-permute-start | bytes 196616 | tf_op jit(solution)/shard_map/ppermute | solution.py:19
  49.7 1.0 %collective-permute-done.7 = f32[4,64,64]{2,1,0:T(8,128)S(1)} collective-permute-done((f32[4,64,64]{2,1,0:T(8,128)S(1)}, f32[4,64,64]{2,1,0:T(8,128)S(1)}, u32[]{:S(2)}, u32[]{:S(2)}) %collective-permute-start.7) | collective-permute-done | bytes 65568 | tf_op jit(solution)/shard_map/ppermute | solution.py:19
  50.7 3.8 %group_level.1 = f32[8,64,384]{2,1,0:T(8,128)} custom-call(f32[8,64,64]{2,1,0:T(8,128)S(1)} %pad_maximum_fusion.3.factors, f32[8,64,384]{2,1,0:T(8,128)S(1)} %get-tuple-element.34.samples, f32[64,64]{1,0:T(8,128)S(1)} %get-tuple-element.35.box_z), custom_call_target="tpu_custom_call" | custom-call | tf_op jit(solution)/shard_map/group_level/pallas_call | solution.py:661
  (4 shorter events, 0.1 us)
Async XLA Ops:
  1.3 1.0 %copy-start.1 = (bf16[2,2,2,64,384]{4,3,2,1,0:T(8,128)(2,1)S(1)}, bf16[2,2,2,64,384]{4,3,2,1,0:T(8,128)(2,1)}, u32[]{:S(2)}) copy-start(bf16[2,2,2,64,384]{4,3,2,1,0:T(8,128)(2,1)} %param.5) | copy-start | bytes 1179652
  2.4 8.1 %collective-permute-start = (bf16[4,200,128]{2,1,0:T(8,128)(2,1)S(1)}, bf16[4,200,128]{2,1,0:T(8,128)(2,1)S(1)}, u32[]{:S(2)}, u32[]{:S(2)}) collective-permute-start(bf16[4,200,128]{2,1,0:T(8,128)(2,1)S(1)} %get-tuple-element.24), channel_id=1, source_target_pairs={{0,1},{1,0},{2,3},{3,2},{4,5},{5,4},{6,7},{7,6},{8,9},{9,8},{10,11... | collective-permute-start | bytes 614408 | tf_op jit(solution)/shard_map/ppermute | solution.py:19
  5.5 0.7 %copy-start.2 = (s32[2,2,2,27]{3,2,1,0:T(2,128)S(1)}, s32[2,2,2,27]{3,2,1,0:T(2,128)}, u32[]{:S(2)}) copy-start(s32[2,2,2,27]{3,2,1,0:T(2,128)} %near.7) | copy-start | bytes 2596
  10.6 8.5 %collective-permute-start.1 = (bf16[2,3,200,128]{3,2,1,0:T(8,128)(2,1)S(1)}, bf16[2,3,200,128]{3,2,1,0:T(8,128)(2,1)S(1)}, u32[]{:S(2)}, u32[]{:S(2)}) collective-permute-start(bf16[2,3,200,128]{3,2,1,0:T(8,128)(2,1)S(1)} %get-tuple-element.43), channel_id=1, source_target_pairs={{0,2},{2,0},{4,6},{6,4},{1,3},{3,1},{5,7},{7,5},{8,10},{10,8},{12,... | collective-permute-start | bytes 921608 | tf_op jit(solution)/shard_map/ppermute | solution.py:209
  12.5 6.7 %collective-permute-start.2 = (bf16[2,3,200,128]{3,2,1,0:T(8,128)(2,1)S(1)}, bf16[2,3,200,128]{3,2,1,0:T(8,128)(2,1)S(1)}, u32[]{:S(2)}, u32[]{:S(2)}) collective-permute-start(bf16[2,3,200,128]{3,2,1,0:T(8,128)(2,1)S(1)} %get-tuple-element.44), channel_id=1, source_target_pairs={{2,4},{4,2},{3,5},{5,3},{10,12},{12,10},{11,13},{13,11},{18,20},{2... | collective-permute-start | bytes 921608 | tf_op jit(solution)/shard_map/ppermute | solution.py:207
  19.4 2.1 %collective-permute-start.3 = (bf16[4,3,200,128]{3,2,1,0:T(8,128)(2,1)S(1)}, bf16[4,3,200,128]{3,2,1,0:T(8,128)(2,1)S(1)}, u32[]{:S(2)}, u32[]{:S(2)}) collective-permute-start(bf16[4,3,200,128]{3,2,1,0:T(8,128)(2,1)S(1)} %get-tuple-element.42), channel_id=1, source_target_pairs={{0,8},{8,0},{16,24},{24,16},{1,9},{9,1},{17,25},{25,17},{2,10},{10... | collective-permute-start | bytes 1843208 | tf_op jit(solution)/shard_map/ppermute | solution.py:209
  19.5 8.6 %collective-permute-start.4 = (bf16[4,3,200,128]{3,2,1,0:T(8,128)(2,1)S(1)}, bf16[4,3,200,128]{3,2,1,0:T(8,128)(2,1)S(1)}, u32[]{:S(2)}, u32[]{:S(2)}) collective-permute-start(bf16[4,3,200,128]{3,2,1,0:T(8,128)(2,1)S(1)} %get-tuple-element.41), channel_id=1, source_target_pairs={{8,16},{16,8},{9,17},{17,9},{10,18},{18,10},{11,19},{19,11},{12,20... | collective-permute-start | bytes 1843208 | tf_op jit(solution)/shard_map/ppermute | solution.py:207
  21.7 6.4 %copy-start = (f32[2,2,2,64,384]{4,3,2,1,0:T(8,128)S(1)}, f32[2,2,2,64,384]{4,3,2,1,0:T(8,128)}, u32[]{:S(2)}) copy-start(f32[2,2,2,64,384]{4,3,2,1,0:T(8,128)} %param.4) | copy-start | bytes 2359300
  32.9 4.2 %collective-permute-start.5 = (f32[1,64,64]{2,1,0:T(8,128)S(1)}, f32[1,64,64]{2,1,0:T(8,128)S(1)}, u32[]{:S(2)}, u32[]{:S(2)}) collective-permute-start(f32[1,64,64]{2,1,0:T(8,128)S(1)} %bitcast.29), channel_id=1, source_target_pairs={{0,1},{1,0},{2,3},{3,2},{4,5},{5,4},{6,7},{7,6},{8,9},{9,8},{10,11... | collective-permute-start | bytes 49160 | tf_op jit(solution)/shard_map/ppermute | solution.py:19
  37.1 9.7 %collective-permute-start.6 = (f32[2,64,64]{2,1,0:T(8,128)S(1)}, f32[2,64,64]{2,1,0:T(8,128)S(1)}, u32[]{:S(2)}, u32[]{:S(2)}) collective-permute-start(f32[2,64,64]{2,1,0:T(8,128)S(1)} %pad_maximum_fusion.5), channel_id=1, source_target_pairs={{0,2},{2,0},{4,6},{6,4},{1,3},{3,1},{5,7},{7,5},{8,10},{10,8},{12,... | collective-permute-start | bytes 98312 | tf_op jit(solution)/shard_map/ppermute | solution.py:19
  46.8 3.9 %collective-permute-start.7 = (f32[4,64,64]{2,1,0:T(8,128)S(1)}, f32[4,64,64]{2,1,0:T(8,128)S(1)}, u32[]{:S(2)}, u32[]{:S(2)}) collective-permute-start(f32[4,64,64]{2,1,0:T(8,128)S(1)} %pad_maximum_fusion.4), channel_id=1, source_target_pairs={{0,8},{8,0},{16,24},{24,16},{1,9},{9,1},{17,25},{25,17},{2,10},{10... | collective-permute-start | bytes 196616 | tf_op jit(solution)/shard_map/ppermute | solution.py:19

commit v9 on v8

--- a/solution.py
+++ b/solution.py
@@ -284,7 +284,7 @@
 def close_list(listed, count, blank):
     for i in range(GROUP):
         listed[count + i] = jnp.int32(blank)
-    return lax.div(count + (GROUP - 1), jnp.int32(GROUP))
+    return count
 
 
 def spread_offsets(blocks, places, turned, spread):
@@ -316,13 +316,12 @@
     return {pq: tile.astype(jnp.bfloat16) for pq, tile in tiles.items()}
 
 
-def add_pairs(groups, listed, blocks, own, spread, total):
+def add_pairs(count, listed, blocks, own, spread, total):
     chunk = 16
 
-    @pl.loop(0, groups)
-    def _(group):
-        for u in range(GROUP):
-            code = listed[group * GROUP + u]
+    def add_group(first, size):
+        for u in range(size):
+            code = listed[first + u]
             pair = lax.div(code, jnp.int32(27))
             k = code - pair * 27
             source = lax.shift_right_logical(pair, jnp.int32(4))
@@ -357,6 +356,21 @@
             )
             total[a] += matmul(sampled, matrix, None)
 
+    groups = lax.div(count, jnp.int32(GROUP))
+    rest = count - groups * GROUP
+
+    @pl.loop(0, groups)
+    def _(group):
+        add_group(group * GROUP, GROUP)
+
+    @pl.when(rest > GROUP // 2)
+    def _():
+        add_group(groups * GROUP, GROUP)
+
+    @pl.when(jnp.logical_and(rest > 0, rest <= GROUP // 2))
+    def _():
+        add_group(groups * GROUP, GROUP // 2)
+
 
 def list_stage(stage, near, listed, blank):
     halos, lists = stage
@@ -377,10 +391,10 @@
 
 
 def near_stage(stage, near, own, blocks, total, listed, turned, spread):
-    groups = list_stage(stage, near, listed, (total.shape[0] - 1) * 27 + 13)
+    count = list_stage(stage, near, listed, (total.shape[0] - 1) * 27 + 13)
     places = sorted({first + pair[2] for pairs, first, _ in stage[1] for pair in pairs})
     spread_offsets(blocks, with_far_places(places, stage), turned, spread)
-    add_pairs(groups, listed, blocks, own, spread, total)
+    add_pairs(count, listed, blocks, own, spread, total)
 
 
 def with_far_places(places, stage):

time: 55.1 us -> 55.5 us (level)
    ppermute x4, waiting for transfers between devices: 1.88 us -> 2.77 us  [from_partner(): lax.ppermute(x, axis, [(i, i ^ 1 << distance) for i in range(lax.axis_siz...]
  transfers between devices with their start and end apart: 8 -> 8, of which waited for: 4 -> 5; matrix products, arithmetic and copies ran while one was open for 0% -> 0% of each run, Pallas kernels for 36% -> 36%
where the time goes in v9:
time: 55.5 us; the launch traced here: 55.2 us
  Pallas kernels  28.5 us (51%)
  starting transfers between devices  17.7 us (32%)
  waiting for transfers between devices  5.36 us (10%)
  local copies, waits for them, and re-layouts  2.39 us (4%)
  between operations  0.76 us (1%)
    ppermute x4, starting transfers between devices, from_partner(): lax.ppermute(x, axis, [(i, i ^ 1 << distance) for i in range(lax.axis_siz...  14.4 us
    pallas_call x3, Pallas kernels, add_stage(): pl.pallas_call(functools.partial(kernel, stage), out_shape=sums, in_specs...  14.2 us
    pallas_call x1, Pallas kernels, body(): pl.pallas_call(functools.partial(last_kernel, stage), out_shape=(whole, s...  4.84 us
    pallas_call x1, Pallas kernels, body(): pl.pallas_call(group_kernel, out_shape=whole, scratch_shapes=[single_scra...  3.85 us
    pallas_call x1, Pallas kernels, body(): pl.pallas_call(leaf_kernel, out_shape=(whole, like((rank, count * rank),...  2.83 us
    ppermute x4, waiting for transfers between devices, from_partner(): lax.ppermute(x, axis, [(i, i ^ 1 << distance) for i in range(lax.axis_siz...  2.77 us
    pallas_call x1, Pallas kernels, body(): pl.pallas_call(leaf_factors, out_shape=like((rank * count, 2 * rank), jnp...  2.71 us
    ppermute x2, waiting for transfers between devices, to_neighbours(): received.append(lax.ppermute(jnp.where(even, high, low), axis, pairs))  2.59 us
  transfers between devices with their start and end apart: 8, of which 5 were waited for; matrix products, arithmetic and copies ran while one was open for 0% of the time, Pallas kernels for 36%

profile of v9, /device:TPU:0, one launch (start us, length us, event | category | flops | bytes accessed | tf_op | source)
XLA Modules:
  0.0 55.2 jit_solution(4587391562125585261)
XLA Ops:
  0.6 0.7 %copy.7 = bf16[2,2,2,3,128]{4,3,2,1,0:T(4,128)(2,1)S(1)} copy(bf16[2,2,2,3,128]{4,2,3,1,0:T(2,128)(2,1)} %param.6) | data formatting | bytes 12288 | tf_op args[2]
  1.3 0.0 copy-start.1
  1.3 1.0 %copy-done.1 = bf16[2,2,2,64,384]{4,3,2,1,0:T(8,128)(2,1)S(1)} copy-done((bf16[2,2,2,64,384]{4,3,2,1,0:T(8,128)(2,1)S(1)}, bf16[2,2,2,64,384]{4,3,2,1,0:T(8,128)(2,1)}, u32[]{:S(2)}) %copy-start.1) | copy-done | bytes 393240
  2.3 0.1 pack.1
  2.4 3.0 %collective-permute-start = (bf16[4,200,128]{2,1,0:T(8,128)(2,1)S(1)}, bf16[4,200,128]{2,1,0:T(8,128)(2,1)S(1)}, u32[]{:S(2)}, u32[]{:S(2)}) collective-permute-start(bf16[4,200,128]{2,1,0:T(8,128)(2,1)S(1)} %get-tuple-element.24), channel_id=1, source_target_pairs={{0,1},{1,0},{2,3},{3,2},{4,5},{5,4},{6,7},{7,6},{8,9},{9,8},{10,11... | collective-permute-start | bytes 614408 | tf_op jit(solution)/shard_map/ppermute | solution.py:19
  5.5 0.0 copy-start.2
  5.5 0.7 %copy-done.2 = s32[2,2,2,27]{3,2,1,0:T(2,128)S(1)} copy-done((s32[2,2,2,27]{3,2,1,0:T(2,128)S(1)}, s32[2,2,2,27]{3,2,1,0:T(2,128)}, u32[]{:S(2)}) %copy-start.2) | copy-done | bytes 888
  6.1 3.2 %near_inner.1.before = f32[9,64,384]{2,1,0:T(8,128)S(1)} custom-call(s32[2,2,2,27]{3,2,1,0:T(2,128)S(1)} %copy-done.2, f32[9,8,128]{2,1,0:T(8,128)S(1)} %get-tuple-element.22.own, bf16[8,200,128]{2,1,0:T(8,128)(2,1)S(1)} %get-tuple-element.23.blocks), custom_call_target="tpu_custom_call" | custom-call | flops 4000000000 | bytes 4194304 | tf_op jit(solution)/shard_map/near_inner/pallas_call | solution.py:622
  9.3 1.2 %collective-permute-done = bf16[4,200,128]{2,1,0:T(8,128)(2,1)S(1)} collective-permute-done((bf16[4,200,128]{2,1,0:T(8,128)(2,1)S(1)}, bf16[4,200,128]{2,1,0:T(8,128)(2,1)S(1)}, u32[]{:S(2)}, u32[]{:S(2)}) %collective-permute-start) | collective-permute-done | bytes 204832 | tf_op jit(solution)/shard_map/ppermute | solution.py:19
  10.5 0.1 pad_maximum_fusion.2
  10.6 1.9 %collective-permute-start.1 = (bf16[2,3,200,128]{3,2,1,0:T(8,128)(2,1)S(1)}, bf16[2,3,200,128]{3,2,1,0:T(8,128)(2,1)S(1)}, u32[]{:S(2)}, u32[]{:S(2)}) collective-permute-start(bf16[2,3,200,128]{3,2,1,0:T(8,128)(2,1)S(1)} %get-tuple-element.43), channel_id=1, source_target_pairs={{0,2},{2,0},{4,6},{6,4},{1,3},{3,1},{5,7},{7,5},{8,10},{10,8},{12,... | collective-permute-start | bytes 921608 | tf_op jit(solution)/shard_map/ppermute | solution.py:209
  12.5 0.7 %collective-permute-start.2 = (bf16[2,3,200,128]{3,2,1,0:T(8,128)(2,1)S(1)}, bf16[2,3,200,128]{3,2,1,0:T(8,128)(2,1)S(1)}, u32[]{:S(2)}, u32[]{:S(2)}) collective-permute-start(bf16[2,3,200,128]{3,2,1,0:T(8,128)(2,1)S(1)} %get-tuple-element.44), channel_id=1, source_target_pairs={{2,4},{4,2},{3,5},{5,3},{10,12},{12,10},{11,13},{13,11},{18,20},{2... | collective-permute-start | bytes 921608 | tf_op jit(solution)/shard_map/ppermute | solution.py:207
  13.2 4.7 %near_inner_rest.1.before = f32[9,64,384]{2,1,0:T(8,128)S(1)} custom-call(s32[2,2,2,27]{3,2,1,0:T(2,128)S(1)} %copy-done.2, f32[9,8,128]{2,1,0:T(8,128)S(1)} %get-tuple-element.22.own, bf16[8,200,128]{2,1,0:T(8,128)(2,1)S(1)} %get-tuple-element.23.blocks, f32[9,64,384]{2,1,0:T(8,128)S(1)} %near_inner.1.before), custom_call_target="tpu_custom_call" | custom-call | flops 4000000000 | bytes 4194304 | tf_op jit(solution)/shard_map/near_inner_rest/pallas_call | solution.py:622
  17.9 1.3 %collective-permute-done.1 = bf16[2,3,200,128]{3,2,1,0:T(8,128)(2,1)S(1)} collective-permute-done((bf16[2,3,200,128]{3,2,1,0:T(8,128)(2,1)S(1)}, bf16[2,3,200,128]{3,2,1,0:T(8,128)(2,1)S(1)}, u32[]{:S(2)}, u32[]{:S(2)}) %collective-permute-start.1) | collective-permute-done | bytes 307232 | tf_op jit(solution)/shard_map/ppermute | solution.py:209
  19.2 0.0 collective-permute-done.2
  19.2 0.1 pad_maximum_fusion.1
  19.3 0.1 select_bitcast_fusion
  19.4 0.1 collective-permute-start.3
  19.5 0.7 %collective-permute-start.4 = (bf16[4,3,200,128]{3,2,1,0:T(8,128)(2,1)S(1)}, bf16[4,3,200,128]{3,2,1,0:T(8,128)(2,1)S(1)}, u32[]{:S(2)}, u32[]{:S(2)}) collective-permute-start(bf16[4,3,200,128]{3,2,1,0:T(8,128)(2,1)S(1)} %get-tuple-element.41), channel_id=1, source_target_pairs={{8,16},{16,8},{9,17},{17,9},{10,18},{18,10},{11,19},{19,11},{12,20... | collective-permute-start | bytes 1843208 | tf_op jit(solution)/shard_map/ppermute | solution.py:207
  20.2 1.3 %collective-permute-done.3 = bf16[4,3,200,128]{3,2,1,0:T(8,128)(2,1)S(1)} collective-permute-done((bf16[4,3,200,128]{3,2,1,0:T(8,128)(2,1)S(1)}, bf16[4,3,200,128]{3,2,1,0:T(8,128)(2,1)S(1)}, u32[]{:S(2)}, u32[]{:S(2)}) %collective-permute-start.3) | collective-permute-done | bytes 614432 | tf_op jit(solution)/shard_map/ppermute | solution.py:209
  21.5 0.2 pad_maximum_fusion.blocks
  21.7 0.0 copy-start
  21.7 6.3 %near_z_y_and_x.1.before = f32[9,64,384]{2,1,0:T(8,128)S(1)} custom-call(s32[2,2,2,27]{3,2,1,0:T(2,128)S(1)} %copy-done.2, f32[9,8,128]{2,1,0:T(8,128)S(1)} %get-tuple-element.22.own, bf16[36,200,128]{2,1,0:T(8,128)(2,1)S(1)} %pad_maximum_fusion.blocks, f32[9,64,384]{2,1,0:T(8,128)S(1)} %near_inner_rest.1.before), custom_call_target="tpu_custom_call" | custom-call | flops 8999999488 | bytes 4194304 | tf_op jit(solution)/shard_map/near_z_y_and_x/pallas_call | solution.py:622
  28.0 0.0 collective-permute-done.4
  28.0 0.0 copy-done
  28.0 4.8 %near_x_and_box_level.1 = (f32[8,64,384]{2,1,0:T(8,128)S(1)}, f32[8,64,64]{2,1,0:T(8,128)S(1)}, f32[64,64]{1,0:T(8,128)S(1)}, f32[8,64,384]{2,1,0:T(8,128)S(1)}, f32[64,64]{1,0:T(8,128)S(1)}) custom-call(s32[2,2,2,27]{3,2,1,0:T(2,128)S(1)} %copy-done.2, f32[9,8,128]{2,1,0:T(8,128)S(1)} %get-tuple-element.22.own, f32[9,64,384]{2,1,0:T(8,128)S(1)} %near_z_y_and_x.1.before, ...), custom_call_target="tpu_custom_call" | custom-call | tf_op jit(solution)/shard_map/near_x_and_box_level/pallas_call | solution.py:644
  32.9 0.7 %collective-permute-start.5 = (f32[1,64,64]{2,1,0:T(8,128)S(1)}, f32[1,64,64]{2,1,0:T(8,128)S(1)}, u32[]{:S(2)}, u32[]{:S(2)}) collective-permute-start(f32[1,64,64]{2,1,0:T(8,128)S(1)} %bitcast.29), channel_id=1, source_target_pairs={{0,1},{1,0},{2,3},{3,2},{4,5},{5,4},{6,7},{7,6},{8,9},{9,8},{10,11... | collective-permute-start | bytes 49160 | tf_op jit(solution)/shard_map/ppermute | solution.py:19
  33.6 2.7 %leaf_factors.1.factors = f32[512,128]{1,0:T(8,128)S(1)} custom-call(f32[8,64,64]{2,1,0:T(8,128)S(1)} %get-tuple-element.30.grams), custom_call_target="tpu_custom_call" | custom-call | flops 3000000000 | bytes 4194304 | tf_op jit(solution)/shard_map/leaf_factors/pallas_call | solution.py:655
  36.3 0.6 %collective-permute-done.5 = f32[1,64,64]{2,1,0:T(8,128)S(1)} collective-permute-done((f32[1,64,64]{2,1,0:T(8,128)S(1)}, f32[1,64,64]{2,1,0:T(8,128)S(1)}, u32[]{:S(2)}, u32[]{:S(2)}) %collective-permute-start.5) | collective-permute-done | bytes 16416 | tf_op jit(solution)/shard_map/ppermute | solution.py:19
  36.9 7.0 %collective-permute-start.6 = (f32[2,64,64]{2,1,0:T(8,128)S(1)}, f32[2,64,64]{2,1,0:T(8,128)S(1)}, u32[]{:S(2)}, u32[]{:S(2)}) collective-permute-start(f32[2,64,64]{2,1,0:T(8,128)S(1)} %pad_maximum_fusion.5), channel_id=1, source_target_pairs={{0,2},{2,0},{4,6},{6,4},{1,3},{3,1},{5,7},{7,5},{8,10},{10,8},{12,... | collective-permute-start | bytes 98312 | tf_op jit(solution)/shard_map/ppermute | solution.py:19
  43.8 2.8 %leaf_level.1 = (f32[8,64,384]{2,1,0:T(8,128)}, f32[64,512]{1,0:T(8,128)}) custom-call(f32[8,64,384]{2,1,0:T(8,128)S(1)} %get-tuple-element.32.far, f32[512,128]{1,0:T(8,128)S(1)} %leaf_factors.1.factors, f32[8,64,384]{2,1,0:T(8,128)S(1)} %get-tuple-element.34.samples, f32[64,64]{1,0:T(8,128)S(1)} %get-tuple-element.35.box_z), custom_call_target="tpu_custom_call" | custom-call | flops 4000000000 | bytes 4194304 | tf_op jit(solution)/shard_map/leaf_level/pallas_call | solution.py:664
  46.7 0.0 collective-permute-done.6
  46.7 3.7 %collective-permute-start.7 = (f32[4,64,64]{2,1,0:T(8,128)S(1)}, f32[4,64,64]{2,1,0:T(8,128)S(1)}, u32[]{:S(2)}, u32[]{:S(2)}) collective-permute-start(f32[4,64,64]{2,1,0:T(8,128)S(1)} %pad_maximum_fusion.4), channel_id=1, source_target_pairs={{0,8},{8,0},{16,24},{24,16},{1,9},{9,1},{17,25},{25,17},{2,10},{10... | collective-permute-start | bytes 196616 | tf_op jit(solution)/shard_map/ppermute | solution.py:19
  50.4 1.0 %collective-permute-done.7 = f32[4,64,64]{2,1,0:T(8,128)S(1)} collective-permute-done((f32[4,64,64]{2,1,0:T(8,128)S(1)}, f32[4,64,64]{2,1,0:T(8,128)S(1)}, u32[]{:S(2)}, u32[]{:S(2)}) %collective-permute-start.7) | collective-permute-done | bytes 65568 | tf_op jit(solution)/shard_map/ppermute | solution.py:19
  51.4 3.8 %group_level.1 = f32[8,64,384]{2,1,0:T(8,128)} custom-call(f32[8,64,64]{2,1,0:T(8,128)S(1)} %pad_maximum_fusion.3.factors, f32[8,64,384]{2,1,0:T(8,128)S(1)} %get-tuple-element.34.samples, f32[64,64]{1,0:T(8,128)S(1)} %get-tuple-element.35.box_z), custom_call_target="tpu_custom_call" | custom-call | tf_op jit(solution)/shard_map/group_level/pallas_call | solution.py:675
  (4 shorter events, 0.1 us)
Async XLA Ops:
  1.3 1.0 %copy-start.1 = (bf16[2,2,2,64,384]{4,3,2,1,0:T(8,128)(2,1)S(1)}, bf16[2,2,2,64,384]{4,3,2,1,0:T(8,128)(2,1)}, u32[]{:S(2)}) copy-start(bf16[2,2,2,64,384]{4,3,2,1,0:T(8,128)(2,1)} %param.5) | copy-start | bytes 1179652
  2.4 8.1 %collective-permute-start = (bf16[4,200,128]{2,1,0:T(8,128)(2,1)S(1)}, bf16[4,200,128]{2,1,0:T(8,128)(2,1)S(1)}, u32[]{:S(2)}, u32[]{:S(2)}) collective-permute-start(bf16[4,200,128]{2,1,0:T(8,128)(2,1)S(1)} %get-tuple-element.24), channel_id=1, source_target_pairs={{0,1},{1,0},{2,3},{3,2},{4,5},{5,4},{6,7},{7,6},{8,9},{9,8},{10,11... | collective-permute-start | bytes 614408 | tf_op jit(solution)/shard_map/ppermute | solution.py:19
  5.5 0.7 %copy-start.2 = (s32[2,2,2,27]{3,2,1,0:T(2,128)S(1)}, s32[2,2,2,27]{3,2,1,0:T(2,128)}, u32[]{:S(2)}) copy-start(s32[2,2,2,27]{3,2,1,0:T(2,128)} %near.7) | copy-start | bytes 2596
  10.6 8.5 %collective-permute-start.1 = (bf16[2,3,200,128]{3,2,1,0:T(8,128)(2,1)S(1)}, bf16[2,3,200,128]{3,2,1,0:T(8,128)(2,1)S(1)}, u32[]{:S(2)}, u32[]{:S(2)}) collective-permute-start(bf16[2,3,200,128]{3,2,1,0:T(8,128)(2,1)S(1)} %get-tuple-element.43), channel_id=1, source_target_pairs={{0,2},{2,0},{4,6},{6,4},{1,3},{3,1},{5,7},{7,5},{8,10},{10,8},{12,... | collective-permute-start | bytes 921608 | tf_op jit(solution)/shard_map/ppermute | solution.py:209
  12.5 6.7 %collective-permute-start.2 = (bf16[2,3,200,128]{3,2,1,0:T(8,128)(2,1)S(1)}, bf16[2,3,200,128]{3,2,1,0:T(8,128)(2,1)S(1)}, u32[]{:S(2)}, u32[]{:S(2)}) collective-permute-start(bf16[2,3,200,128]{3,2,1,0:T(8,128)(2,1)S(1)} %get-tuple-element.44), channel_id=1, source_target_pairs={{2,4},{4,2},{3,5},{5,3},{10,12},{12,10},{11,13},{13,11},{18,20},{2... | collective-permute-start | bytes 921608 | tf_op jit(solution)/shard_map/ppermute | solution.py:207
  19.4 2.1 %collective-permute-start.3 = (bf16[4,3,200,128]{3,2,1,0:T(8,128)(2,1)S(1)}, bf16[4,3,200,128]{3,2,1,0:T(8,128)(2,1)S(1)}, u32[]{:S(2)}, u32[]{:S(2)}) collective-permute-start(bf16[4,3,200,128]{3,2,1,0:T(8,128)(2,1)S(1)} %get-tuple-element.42), channel_id=1, source_target_pairs={{0,8},{8,0},{16,24},{24,16},{1,9},{9,1},{17,25},{25,17},{2,10},{10... | collective-permute-start | bytes 1843208 | tf_op jit(solution)/shard_map/ppermute | solution.py:209
  19.5 8.6 %collective-permute-start.4 = (bf16[4,3,200,128]{3,2,1,0:T(8,128)(2,1)S(1)}, bf16[4,3,200,128]{3,2,1,0:T(8,128)(2,1)S(1)}, u32[]{:S(2)}, u32[]{:S(2)}) collective-permute-start(bf16[4,3,200,128]{3,2,1,0:T(8,128)(2,1)S(1)} %get-tuple-element.41), channel_id=1, source_target_pairs={{8,16},{16,8},{9,17},{17,9},{10,18},{18,10},{11,19},{19,11},{12,20... | collective-permute-start | bytes 1843208 | tf_op jit(solution)/shard_map/ppermute | solution.py:207
  21.7 6.4 %copy-start = (f32[2,2,2,64,384]{4,3,2,1,0:T(8,128)S(1)}, f32[2,2,2,64,384]{4,3,2,1,0:T(8,128)}, u32[]{:S(2)}) copy-start(f32[2,2,2,64,384]{4,3,2,1,0:T(8,128)} %param.4) | copy-start | bytes 2359300
  32.9 4.0 %collective-permute-start.5 = (f32[1,64,64]{2,1,0:T(8,128)S(1)}, f32[1,64,64]{2,1,0:T(8,128)S(1)}, u32[]{:S(2)}, u32[]{:S(2)}) collective-permute-start(f32[1,64,64]{2,1,0:T(8,128)S(1)} %bitcast.29), channel_id=1, source_target_pairs={{0,1},{1,0},{2,3},{3,2},{4,5},{5,4},{6,7},{7,6},{8,9},{9,8},{10,11... | collective-permute-start | bytes 49160 | tf_op jit(solution)/shard_map/ppermute | solution.py:19
  36.9 9.8 %collective-permute-start.6 = (f32[2,64,64]{2,1,0:T(8,128)S(1)}, f32[2,64,64]{2,1,0:T(8,128)S(1)}, u32[]{:S(2)}, u32[]{:S(2)}) collective-permute-start(f32[2,64,64]{2,1,0:T(8,128)S(1)} %pad_maximum_fusion.5), channel_id=1, source_target_pairs={{0,2},{2,0},{4,6},{6,4},{1,3},{3,1},{5,7},{7,5},{8,10},{10,8},{12,... | collective-permute-start | bytes 98312 | tf_op jit(solution)/shard_map/ppermute | solution.py:19
  46.7 4.7 %collective-permute-start.7 = (f32[4,64,64]{2,1,0:T(8,128)S(1)}, f32[4,64,64]{2,1,0:T(8,128)S(1)}, u32[]{:S(2)}, u32[]{:S(2)}) collective-permute-start(f32[4,64,64]{2,1,0:T(8,128)S(1)} %pad_maximum_fusion.4), channel_id=1, source_target_pairs={{0,8},{8,0},{16,24},{24,16},{1,9},{9,1},{17,25},{25,17},{2,10},{10... | collective-permute-start | bytes 196616 | tf_op jit(solution)/shard_map/ppermute | solution.py:19
